TPU v7x, 32 devices: a whole 2x2x4 slice. The times are simulated.
32 devices in a mesh: dp: 8 (over z, x), mp: 4 (over y, core).
Axes of the slice: x: 2, y: 2, z: 4, core: 2. Of those that a mesh axis runs over, the one named last changes fastest.
Arguments:
- tokens: bfloat16 [16384, 1024], P('dp', 'mp'), may hold values from -6 to 6
- cotangent: bfloat16 [2448, 1024], P('dp', 'mp'), may hold values from -8 to 8
- mask_rows: int32 [16, 153], P('dp'), may hold values from 0 to 1023, as said below
- genome: int32 [16], P('dp'), may hold values from 0 to 15
- group_tokens: int32 [16], replicated, may hold values from 1000 to 29999
- owner: int32 [8], replicated, may hold values from 0 to 7, each once
- qkv_master: float32 [3, 1024, 1024], P(None, 'dp', 'mp'), may hold values from -0.1875 to 0.1875
- qkv_first: float32 [3, 1024, 1024], P(None, 'dp', 'mp'), may hold values from -384 to 384
- qkv_second: float32 [3, 1024, 1024], P(None, 'dp', 'mp'), may hold values from 1762.56 to 21150.72
- qkv_average: float32 [3, 1024, 1024], P(None, 'dp', 'mp'), may hold values from -0.1875 to 0.1875
- proj_master: float32 [1024, 1024], P('mp', 'dp'), may hold values from -3.5 to 3.5
- proj_first: float32 [1024, 1024], P('mp', 'dp'), may hold values from -20 to 20
- proj_second: float32 [1024, 1024], P('mp', 'dp'), may hold values from 4.78125 to 57.375
- proj_average: float32 [1024, 1024], P('mp', 'dp'), may hold values from -3.5 to 3.5
- gate_up_master: float32 [2, 1024, 4096], P(None, 'dp', 'mp'), may hold values from -0.1875 to 0.1875
- gate_up_first: float32 [2, 1024, 4096], P(None, 'dp', 'mp'), may hold values from -96 to 96
- gate_up_second: float32 [2, 1024, 4096], P(None, 'dp', 'mp'), may hold values from 110.16 to 1321.92
- gate_up_average: float32 [2, 1024, 4096], P(None, 'dp', 'mp'), may hold values from -0.1875 to 0.1875
- down_master: float32 [4096, 1024], P('mp', 'dp'), may hold values from -0.09375 to 0.09375
- down_first: float32 [4096, 1024], P('mp', 'dp'), may hold values from -192 to 192
- down_second: float32 [4096, 1024], P('mp', 'dp'), may hold values from 440.64 to 5287.68
- down_average: float32 [4096, 1024], P('mp', 'dp'), may hold values from -0.09375 to 0.09375
- gains_master: float32 [2, 1024], P(None, 'dp'), may hold values from 0.5 to 1.5
- gains_first: float32 [2, 1024], P(None, 'dp'), may hold values from -384 to 384
- gains_second: float32 [2, 1024], P(None, 'dp'), may hold values from 2068.56 to 24822.72
- gains_average: float32 [2, 1024], P(None, 'dp'), may hold values from 0.5 to 1.5
Outputs:
- output: bfloat16 [16384, 1024], P('dp', 'mp')
- input_grad: bfloat16 [16384, 1024], P('dp', 'mp')
- qkv_grad: float32 [3, 1024, 1024], P(None, 'dp', 'mp')
- qkv_new: float32 [3, 1024, 1024], P(None, 'dp', 'mp')
- qkv_first_new: float32 [3, 1024, 1024], P(None, 'dp', 'mp')
- qkv_second_new: float32 [3, 1024, 1024], P(None, 'dp', 'mp')
- qkv_average_new: float32 [3, 1024, 1024], P(None, 'dp', 'mp')
- qkv_copy: bfloat16 [3, 1024, 1024], P(None, 'dp', 'mp')
- proj_grad: float32 [1024, 1024], P('mp', 'dp')
- proj_new: float32 [1024, 1024], P('mp', 'dp')
- proj_first_new: float32 [1024, 1024], P('mp', 'dp')
- proj_second_new: float32 [1024, 1024], P('mp', 'dp')
- proj_average_new: float32 [1024, 1024], P('mp', 'dp')
- proj_copy: bfloat16 [1024, 1024], P('mp', 'dp')
- gate_up_grad: float32 [2, 1024, 4096], P(None, 'dp', 'mp')
- gate_up_new: float32 [2, 1024, 4096], P(None, 'dp', 'mp')
- gate_up_first_new: float32 [2, 1024, 4096], P(None, 'dp', 'mp')
- gate_up_second_new: float32 [2, 1024, 4096], P(None, 'dp', 'mp')
- gate_up_average_new: float32 [2, 1024, 4096], P(None, 'dp', 'mp')
- gate_up_copy: bfloat16 [2, 1024, 4096], P(None, 'dp', 'mp')
- down_grad: float32 [4096, 1024], P('mp', 'dp')
- down_new: float32 [4096, 1024], P('mp', 'dp')
- down_first_new: float32 [4096, 1024], P('mp', 'dp')
- down_second_new: float32 [4096, 1024], P('mp', 'dp')
- down_average_new: float32 [4096, 1024], P('mp', 'dp')
- down_copy: bfloat16 [4096, 1024], P('mp', 'dp')
- gains_grad: float32 [2, 1024], P(None, 'dp')
- gains_new: float32 [2, 1024], P(None, 'dp')
- gains_first_new: float32 [2, 1024], P(None, 'dp')
- gains_second_new: float32 [2, 1024], P(None, 'dp')
- gains_average_new: float32 [2, 1024], P(None, 'dp')
- gains_copy: bfloat16 [2, 1024], P(None, 'dp')
Inputs may be any that keep to these rules, and one draw needn't show every extreme that they name: `mask_rows`: each row lists 153 distinct positions of its window. A permutation: index j of dp holds block owner[j] of the model-width dimension of every weight.
All inputs are finite; a program needn't handle non-finite values.
Results may differ from a plain program's by a relative error of at most 0.017.
Values may be sent and summed in bfloat16 or wider, within the bound.
No kernel may reach another device: no remote copies, remote signals or barrier semaphores. Data moves between devices by JAX's collectives and lax.ppermute only.
A program may use at most 192 MiB of HBM per device.

v0:
```python
import jax
import jax.numpy as jnp
from jax import lax
from jax.sharding import PartitionSpec as P

D = 1024
FF = 4096
HEAD_DIM = 64
SEQ = 1024
NGROUP = 16
STEP = 7


EPS = 1e-05
THETA = 10000.0
BETA_ONE = 0.5
BETA_TWO = 0.5
ADAM_EPS = 1e-08
DECAY_RATE = 0.1
EMA_RATE = 0.6
GAIN_RATE = 0.4


def dot_transposed(left, right):
    return lax.dot_general(
        left, right, (((1,), (1,)), ((), ())), preferred_element_type=jnp.float32
    )


def dot_leading(left, right):
    return lax.dot_general(
        left, right, (((0,), (0,)), ((), ())), preferred_element_type=jnp.float32
    )


def rotary_tables():
    half_dim = HEAD_DIM // 2
    frequency = THETA ** (-jnp.arange(half_dim, dtype=jnp.float32) / half_dim)
    angles = jnp.arange(SEQ, dtype=jnp.float32)[:, None] * frequency[None, :]
    return (jnp.cos(angles), jnp.sin(angles))


def rotate(values, cosine_rows, sine_rows):
    half_dim = values.shape[-1] // 2
    first_half = values[..., :half_dim]
    second_half = values[..., half_dim:]
    return jnp.concatenate(
        [
            first_half * cosine_rows - second_half * sine_rows,
            second_half * cosine_rows + first_half * sine_rows,
        ],
        axis=-1,
    )


def rotate_back(values, cosine_rows, sine_rows):
    half_dim = values.shape[-1] // 2
    first_half = values[..., :half_dim]
    second_half = values[..., half_dim:]
    return jnp.concatenate(
        [
            first_half * cosine_rows + second_half * sine_rows,
            second_half * cosine_rows - first_half * sine_rows,
        ],
        axis=-1,
    )


def reorder(values, block_order, pieces):
    moved_axis = jnp.moveaxis(values, 1, 0)
    shaped = moved_axis.reshape((pieces, moved_axis.shape[0] // pieces) + moved_axis.shape[1:])
    taken = jnp.take(shaped, block_order, axis=0).reshape(moved_axis.shape)
    return jnp.moveaxis(taken, 0, 1)


def adam_step(summed, master, first_old, second, average, step_rate, weight_decay):
    new_first = BETA_ONE * first_old + (1.0 - BETA_ONE) * summed
    new_second = BETA_TWO * second + (1.0 - BETA_TWO) * summed * summed
    update = (
        new_first
        / (1.0 - BETA_ONE**STEP)
        / (jnp.sqrt(new_second / (1.0 - BETA_TWO**STEP)) + ADAM_EPS)
    )
    new_master = master - step_rate * (update + weight_decay * master)
    new_average = EMA_RATE * average + (1.0 - EMA_RATE) * new_master
    return (summed, new_master, new_first, new_second, new_average, new_master.astype(jnp.bfloat16))


def local(
    tokens,
    cotangent,
    mask_rows,
    genome,
    group_tokens,
    owner,
    qkv_master,
    qkv_first,
    qkv_second,
    qkv_average,
    proj_master,
    proj_first,
    proj_second,
    proj_average,
    gate_up_master,
    gate_up_first,
    gate_up_second,
    gate_up_average,
    down_master,
    down_first,
    down_second,
    down_average,
    gains_master,
    gains_first,
    gains_second,
    gains_average,
):
    dp_count = lax.axis_size("dp")
    mp_index = lax.axis_index("mp")
    inverse = jnp.argsort(owner)
    gathered = (
        lax.all_gather(qkv_master.astype(jnp.bfloat16), "dp", axis=1, tiled=True),
        lax.all_gather(proj_master.astype(jnp.bfloat16), "dp", axis=1, tiled=True),
        lax.all_gather(gate_up_master.astype(jnp.bfloat16), "dp", axis=1, tiled=True),
        lax.all_gather(down_master.astype(jnp.bfloat16), "dp", axis=1, tiled=True),
        lax.all_gather(gains_master.astype(jnp.bfloat16), "dp", axis=1, tiled=True),
    )
    qkv_w, proj_w, gate_up_w, down_w, gains_w = [
        reorder(piece_w, inverse, dp_count) for piece_w in gathered
    ]
    gains_f = gains_w.astype(jnp.float32)
    full_tokens, full_cot = (
        lax.all_gather(tokens, "mp", axis=1, tiled=True),
        lax.all_gather(cotangent, "mp", axis=1, tiled=True),
    )
    window_count = mask_rows.shape[0]
    masked_count = mask_rows.shape[1]
    width = full_tokens.shape[1]
    share = tokens.shape[1]
    heads_local = qkv_w.shape[2] // HEAD_DIM
    col_start = mp_index * share
    rows_index = (jnp.arange(window_count, dtype=jnp.int32)[:, None] * SEQ + mask_rows).reshape(-1)
    tokens_f = full_tokens.astype(jnp.float32)
    scale_one = lax.rsqrt(jnp.mean(tokens_f * tokens_f, axis=1, keepdims=True) + EPS)
    norm_one = (tokens_f * scale_one * gains_f[0]).astype(jnp.bfloat16)
    projected = jnp.einsum("sd,tdh->tsh", norm_one, qkv_w, preferred_element_type=jnp.float32)
    cosine_table, sine_table = rotary_tables()
    cosine_rows = cosine_table[:, None, :]
    sine_rows = sine_table[:, None, :]
    heads_shape = (window_count, SEQ, heads_local, HEAD_DIM)
    queries = rotate(projected[0].reshape(heads_shape), cosine_rows, sine_rows).astype(jnp.bfloat16)
    keys_rot = rotate(projected[1].reshape(heads_shape), cosine_rows, sine_rows).astype(
        jnp.bfloat16
    )
    values_in = projected[2].reshape(heads_shape).astype(jnp.bfloat16)
    head_scale = HEAD_DIM ** (-0.5)

    def attend(window_items):
        window_q, window_k, window_v = window_items
        scores = (
            jnp.einsum("qhd,khd->hqk", window_q, window_k, preferred_element_type=jnp.float32)
            * head_scale
        )
        probability = jax.nn.softmax(scores, axis=-1).astype(jnp.bfloat16)
        return jnp.einsum(
            "hqk,khd->qhd", probability, window_v, preferred_element_type=jnp.float32
        ).astype(jnp.bfloat16)

    attended = lax.map(attend, (queries, keys_rot, values_in)).reshape(
        window_count * SEQ, heads_local * HEAD_DIM
    )
    attn_part = jnp.dot(attended, proj_w, preferred_element_type=jnp.float32)
    tokens_share = tokens.astype(jnp.float32)
    attn_sum = lax.psum(attn_part, "mp")
    residual = tokens_f + attn_sum
    scale_two = lax.rsqrt(jnp.mean(residual * residual, axis=1, keepdims=True) + EPS)
    norm_two = (residual * scale_two * gains_f[1]).astype(jnp.bfloat16)
    residual_share = lax.dynamic_slice_in_dim(residual, col_start, share, 1)
    kept_residual = residual[rows_index]
    gate_act = jnp.dot(norm_two, gate_up_w[0], preferred_element_type=jnp.float32)
    upward = jnp.dot(norm_two, gate_up_w[1], preferred_element_type=jnp.float32)
    hidden = (jax.nn.silu(gate_act) * upward).astype(jnp.bfloat16)
    ffn_part = jnp.dot(hidden, down_w, preferred_element_type=jnp.float32)
    ffn_share = lax.psum_scatter(
        ffn_part.astype(jnp.bfloat16), "mp", scatter_dimension=1, tiled=True
    ).astype(jnp.float32)
    output = (residual_share + ffn_share).astype(jnp.bfloat16)
    counts = group_tokens.astype(jnp.float32)
    picked = jnp.sum(
        jnp.where(
            genome[:, None] == jnp.arange(NGROUP, dtype=jnp.int32)[None, :], counts[None, :], 0.0
        ),
        axis=1,
    )
    window_scale = NGROUP * picked / jnp.sum(counts)
    row_scale = jnp.repeat(window_scale, masked_count)
    out_grad = row_scale[:, None] * full_cot.astype(jnp.float32)
    out_grad_b = out_grad.astype(jnp.bfloat16)
    gate_rows = gate_act[rows_index]
    up_rows = upward[rows_index]
    hidden_rows = hidden[rows_index]
    norm_two_rows = norm_two[rows_index]
    hidden_grad = dot_transposed(out_grad_b, down_w)
    gate_sigmoid = jax.nn.sigmoid(gate_rows)
    gate_grad = (
        hidden_grad * up_rows * gate_sigmoid * (1.0 + gate_rows * (1.0 - gate_sigmoid))
    ).astype(jnp.bfloat16)
    up_grad = (hidden_grad * (gate_rows * gate_sigmoid)).astype(jnp.bfloat16)
    down_grad = dot_leading(hidden_rows, out_grad_b)
    gate_up_grad = jnp.stack(
        [dot_leading(norm_two_rows, gate_grad), dot_leading(norm_two_rows, up_grad)]
    )
    norm_two_grad = lax.psum(
        dot_transposed(gate_grad, gate_up_w[0]) + dot_transposed(up_grad, gate_up_w[1]), "mp"
    )
    scale_rows = scale_two[rows_index]
    normed_rows = kept_residual * scale_rows
    gain_two_grad = jnp.sum(norm_two_grad * normed_rows, axis=0)
    scaled_grad = norm_two_grad * gains_f[1]
    residual_grad = out_grad + scale_rows * (
        scaled_grad - normed_rows * jnp.mean(scaled_grad * normed_rows, axis=1, keepdims=True)
    )
    attn_grad_b = residual_grad.astype(jnp.bfloat16)
    attended_rows = attended[rows_index]
    proj_grad = dot_leading(attended_rows, attn_grad_b)
    context_grad = dot_transposed(attn_grad_b, proj_w).astype(jnp.bfloat16)
    context_heads = context_grad.reshape(window_count, masked_count, heads_local, HEAD_DIM)
    masked_q = queries.reshape(window_count * SEQ, heads_local * HEAD_DIM)[rows_index].reshape(
        window_count, masked_count, heads_local, HEAD_DIM
    )

    def attend_back(window_items):
        window_q, window_k, window_v, window_do = window_items
        scores = (
            jnp.einsum("qhd,khd->hqk", window_q, window_k, preferred_element_type=jnp.float32)
            * head_scale
        )
        probability = jax.nn.softmax(scores, axis=-1)
        prob_grad = jnp.einsum(
            "qhd,khd->hqk", window_do, window_v, preferred_element_type=jnp.float32
        )
        row_delta = jnp.sum(probability * prob_grad, axis=-1, keepdims=True)
        score_grad = (probability * (prob_grad - row_delta)).astype(jnp.bfloat16)
        value_grad = jnp.einsum(
            "hqk,qhd->khd",
            probability.astype(jnp.bfloat16),
            window_do,
            preferred_element_type=jnp.float32,
        ).astype(jnp.bfloat16)
        query_grad = (
            jnp.einsum("hqk,khd->qhd", score_grad, window_k, preferred_element_type=jnp.float32)
            * head_scale
        )
        key_grad = (
            jnp.einsum("hqk,qhd->khd", score_grad, window_q, preferred_element_type=jnp.float32)
            * head_scale
        )
        return (query_grad, key_grad, value_grad)

    query_grad, key_grad, value_grad = lax.map(
        attend_back, (masked_q, keys_rot, values_in, context_heads)
    )
    mask_cosine = cosine_table[mask_rows][:, :, None, :]
    mask_sine = sine_table[mask_rows][:, :, None, :]
    q_raw_grad = (
        rotate_back(query_grad, mask_cosine, mask_sine)
        .reshape(window_count * masked_count, heads_local * HEAD_DIM)
        .astype(jnp.bfloat16)
    )
    k_raw_grad = (
        rotate_back(key_grad, cosine_rows, sine_rows)
        .reshape(window_count * SEQ, heads_local * HEAD_DIM)
        .astype(jnp.bfloat16)
    )
    v_raw_grad = value_grad.reshape(window_count * SEQ, heads_local * HEAD_DIM)
    norm_one_rows = norm_one[rows_index]
    qkv_grad = jnp.stack(
        [
            dot_leading(norm_one_rows, q_raw_grad),
            dot_leading(norm_one, k_raw_grad),
            dot_leading(norm_one, v_raw_grad),
        ]
    )
    norm_one_part = dot_transposed(k_raw_grad, qkv_w[1]) + dot_transposed(v_raw_grad, qkv_w[2])
    norm_one_part = norm_one_part.at[rows_index].add(dot_transposed(q_raw_grad, qkv_w[0]))
    norm_one_share = lax.psum_scatter(
        norm_one_part.astype(jnp.bfloat16), "mp", scatter_dimension=1, tiled=True
    ).astype(jnp.float32)
    normed_share = tokens_share * scale_one
    gain_one_share = lax.dynamic_slice_in_dim(gains_f[0], col_start, share, 0)
    scaled_share = norm_one_share * gain_one_share
    gain_one_part = jnp.sum(norm_one_share * normed_share, axis=0)
    gain_one_padded = lax.dynamic_update_slice_in_dim(
        jnp.zeros((width,), jnp.float32), gain_one_part, col_start, 0
    )
    row_terms, gain_one_grad = lax.psum(
        (jnp.sum(scaled_share * normed_share, axis=1), gain_one_padded), "mp"
    )
    input_grad = scale_one * (scaled_share - normed_share * (row_terms[:, None] / width))
    residual_grad_share = lax.dynamic_slice_in_dim(residual_grad, col_start, share, 1)
    input_grad = input_grad.at[rows_index].add(residual_grad_share)
    input_grad_b = input_grad.astype(jnp.bfloat16)
    gains_grad = jnp.stack([gain_one_grad, gain_two_grad])
    qkv_sum, proj_sum, gate_up_sum, down_sum, gains_sum = (
        lax.psum_scatter(reorder(qkv_grad, owner, dp_count), "dp", scatter_dimension=1, tiled=True),
        lax.psum_scatter(
            reorder(proj_grad, owner, dp_count), "dp", scatter_dimension=1, tiled=True
        ),
        lax.psum_scatter(
            reorder(gate_up_grad, owner, dp_count), "dp", scatter_dimension=1, tiled=True
        ),
        lax.psum_scatter(
            reorder(down_grad, owner, dp_count), "dp", scatter_dimension=1, tiled=True
        ),
        lax.psum_scatter(
            reorder(gains_grad, owner, dp_count), "dp", scatter_dimension=1, tiled=True
        ),
    )
    qkv_out = adam_step(
        qkv_sum, qkv_master, qkv_first, qkv_second, qkv_average, D ** (-0.5), DECAY_RATE
    )
    proj_out = adam_step(
        proj_sum,
        proj_master,
        proj_first,
        proj_second,
        proj_average,
        (3.0 * D / SEQ) ** (-0.5),
        DECAY_RATE,
    )
    gate_up_out = adam_step(
        gate_up_sum,
        gate_up_master,
        gate_up_first,
        gate_up_second,
        gate_up_average,
        D ** (-0.5),
        DECAY_RATE,
    )
    down_out = adam_step(
        down_sum, down_master, down_first, down_second, down_average, FF ** (-0.5), DECAY_RATE
    )
    gains_out = adam_step(
        gains_sum, gains_master, gains_first, gains_second, gains_average, GAIN_RATE, 0.0
    )
    return (output, input_grad_b, *qkv_out, *proj_out, *gate_up_out, *down_out, *gains_out)


def solution(mesh):
    in_specs = (
        P("dp", "mp"),
        P("dp", "mp"),
        P("dp", None),
        P("dp"),
        P(),
        P(),
        P(None, "dp", "mp"),
        P(None, "dp", "mp"),
        P(None, "dp", "mp"),
        P(None, "dp", "mp"),
        P("mp", "dp"),
        P("mp", "dp"),
        P("mp", "dp"),
        P("mp", "dp"),
        P(None, "dp", "mp"),
        P(None, "dp", "mp"),
        P(None, "dp", "mp"),
        P(None, "dp", "mp"),
        P("mp", "dp"),
        P("mp", "dp"),
        P("mp", "dp"),
        P("mp", "dp"),
        P(None, "dp"),
        P(None, "dp"),
        P(None, "dp"),
        P(None, "dp"),
    )
    out_specs = (
        P("dp", "mp"),
        P("dp", "mp"),
        P(None, "dp", "mp"),
        P(None, "dp", "mp"),
        P(None, "dp", "mp"),
        P(None, "dp", "mp"),
        P(None, "dp", "mp"),
        P(None, "dp", "mp"),
        P("mp", "dp"),
        P("mp", "dp"),
        P("mp", "dp"),
        P("mp", "dp"),
        P("mp", "dp"),
        P("mp", "dp"),
        P(None, "dp", "mp"),
        P(None, "dp", "mp"),
        P(None, "dp", "mp"),
        P(None, "dp", "mp"),
        P(None, "dp", "mp"),
        P(None, "dp", "mp"),
        P("mp", "dp"),
        P("mp", "dp"),
        P("mp", "dp"),
        P("mp", "dp"),
        P("mp", "dp"),
        P("mp", "dp"),
        P(None, "dp"),
        P(None, "dp"),
        P(None, "dp"),
        P(None, "dp"),
        P(None, "dp"),
        P(None, "dp"),
    )
    return jax.shard_map(local, mesh=mesh, in_specs=in_specs, out_specs=out_specs, check_vma=False)
```

profile of v0, /device:TPU:0, one launch (start us, length us, event | category | flops | bytes accessed | tf_op | source)
XLA Modules:
  0.0 1132.6 jit_solution(4849944218146858405)
XLA Ops:
  13.1 22.1 %all_gather.23 = bf16[2,1024]{1,0:T(2,128)(2,1)S(1)} all-gather(bf16[2,128]{1,0:T(2,128)(2,1)S(1)} %convert_element_type.151), channel_id=1, replica_groups=mesh['dp'=8,'mp'=4] {'dp'}, dimensions={1}, use_global_device_ids=true | all-gather | bytes 4608 | tf_op jit(solution)/shard_map/all_gather | solution.py:125
  37.0 29.4 %all_gather.24 = bf16[256,1024]{1,0:T(8,128)(2,1)S(1)} all-gather(bf16[256,128]{1,0:T(8,128)(2,1)S(1)} %convert_element_type.157), channel_id=1, replica_groups=mesh['dp'=8,'mp'=4] {'dp'}, dimensions={1}, use_global_device_ids=true | all-gather | bytes 589824 | tf_op jit(solution)/shard_map/all_gather | solution.py:122
  75.2 24.8 %all-gather.5.cloned.1.call-done = bf16[2048,1024]{1,0:T(8,128)(2,1)} async-done(((bf16[2048,256]{1,0:T(8,128)(2,1)}), bf16[2048,1024]{1,0:T(8,128)(2,1)}) %all-gather.5.cloned.1.call-update) | async-done | bytes 4194320 | tf_op jit(solution)/shard_map/all_gather | solution.py:132
  125.9 69.1 %while.24 = (s32[]{:T(128)}, bf16[2,1024,4,64]{1,3,2,0:T(8,128)(2,1)S(1)}, bf16[2,1024,4,64]{1,3,2,0:T(8,128)(2,1)}, bf16[2,1024,4,64]{1,3,2,0:T(8,128)(2,1)S(1)...) while((s32[]{:T(128)}, bf16[2,1024,4,64]{1,3,2,0:T(8,128)(2,1)S(1)}, bf16[2,1024,4,64]{1,3,2,0:T(8,128)(2,1)}, ...), condition=%wide.region_5.6_spmd, body=%wide.region_2.5_spmd.sunk | while | flops 1111758848 | bytes 69240904 | solution.py:168
  126.3 8.2 fusion.182
  134.5 13.2 %fusion.183 = f32[4,1024]{1,0:T(4,128)S(1)} fusion(f32[4,1024,1024]{1,2,0:T(8,128)} %fusion.182), kind=kOutput, calls=%fused_computation.230.clone.1 | output fusion | flops 16778240 | bytes 16793600 | tf_op jit(solution)/shard_map/while/body/eval_jaxpr/sub | solution.py:163
  147.6 13.3 %fusion.184 = bf16[2,1024,4,64]{1,3,2,0:T(8,128)(2,1)S(1)} fusion(bf16[2,1024,4,64]{1,3,2,0:T(8,128)(2,1)S(1)} %get-tuple-element.380, s32[]{:T(128)S(6)} %copy.305, f32[4,1024]{1,0:T(4,128)S(1)} %fusion.183, bf16[2,1024,4,64]{1,3,2,0:T(8,128)(2,1)} %get-tuple-element.387, f32[4,1024,1024]{1,2,0:T(8,128)} %fusion.182), kind=kOutput, calls=%fused_computation.32.clone.1 | convolution fusion | flops 558109696 | bytes 34620416 | tf_op jit(solution)/shard_map/while/body/eval_jaxpr/hqk,khd->qhd/dot_general | solution.py:164
  161.0 8.2 fusion.182
  169.2 12.6 %fusion.183 = f32[4,1024]{1,0:T(4,128)S(1)} fusion(f32[4,1024,1024]{1,2,0:T(8,128)} %fusion.182), kind=kOutput, calls=%fused_computation.230.clone.1 | output fusion | flops 16778240 | bytes 16793600 | tf_op jit(solution)/shard_map/while/body/eval_jaxpr/sub | solution.py:163
  181.7 13.3 %fusion.184 = bf16[2,1024,4,64]{1,3,2,0:T(8,128)(2,1)S(1)} fusion(bf16[2,1024,4,64]{1,3,2,0:T(8,128)(2,1)S(1)} %get-tuple-element.380, s32[]{:T(128)S(6)} %copy.305, f32[4,1024]{1,0:T(4,128)S(1)} %fusion.183, bf16[2,1024,4,64]{1,3,2,0:T(8,128)(2,1)} %get-tuple-element.387, f32[4,1024,1024]{1,2,0:T(8,128)} %fusion.182), kind=kOutput, calls=%fused_computation.32.clone.1 | convolution fusion | flops 558109696 | bytes 34620416 | tf_op jit(solution)/shard_map/while/body/eval_jaxpr/hqk,khd->qhd/dot_general | solution.py:164
  197.4 4.6 fusion.128
  204.5 10.4 all_gather.27
  214.9 4.8 copy.249
  219.8 5.2 gather_fusion.3
  230.3 126.7 %all-reduce.4.cloned.1.call-done = f32[2048,1024]{1,0:T(8,128)} async-done(((f32[2048,1024]{1,0:T(8,128)}), f32[2048,1024]{1,0:T(8,128)}) %all-reduce.4.cloned.1.call-update) | async-done | bytes 8388624 | tf_op jit(solution)/shard_map/psum | solution.py:173
  357.0 5.8 multiply_reduce_fusion.3
  368.2 4.5 fusion.86
  372.8 8.5 multiply_convert_fusion.1
  381.3 5.5 gather_fusion.18
  390.2 5.0 gather_fusion.19
  395.3 5.3 copy.280
  400.6 5.0 select_bitcast_fusion
  406.1 88.3 %reduce-scatter.20.cloned.1.call-done = f32[1024,128]{1,0:T(8,128)} async-done(((f32[1024,1024]{1,0:T(8,128)}), f32[1024,128]{1,0:T(8,128)}) %reduce-scatter.20.cloned.1.call-update) | async-done | bytes 524304 | tf_op jit(solution)/shard_map/reduce_scatter | solution.py:311
  497.4 6.7 gather_fusion.8
  504.1 6.9 gather_fusion.7
  511.0 37.3 %all-gather.11.cloned.1.call-done = bf16[1024,1024]{1,0:T(8,128)(2,1)} async-done(((bf16[1024,128]{1,0:T(8,128)(2,1)}), bf16[1024,1024]{1,0:T(8,128)(2,1)}) %all-gather.11.cloned.1.call-update) | async-done | bytes 2097168 | tf_op jit(solution)/shard_map/all_gather | solution.py:124
  583.8 6.2 gather_fusion.9
  589.9 11.7 %all-reduce.6.cloned.1.call-done = f32[306,1024]{1,0:T(8,128)} async-done(((f32[306,1024]{1,0:T(8,128)}), f32[306,1024]{1,0:T(8,128)}) %all-reduce.6.cloned.1.call-update) | async-done | bytes 1253392 | tf_op jit(solution)/shard_map/psum | solution.py:212
  607.6 27.1 %while.25 = (s32[]{:T(128)}, f32[2,153,4,64]{1,3,2,0:T(8,128)S(1)}, f32[2,1024,4,64]{1,3,2,0:T(8,128)}, bf16[2,1024,4,64]{1,3,2,0:T(8,128)(2,1)}, bf16[2,1024,4,...) while((s32[]{:T(128)}, f32[2,153,4,64]{1,3,2,0:T(8,128)S(1)}, ...), condition=%wide.region_17.18_spmd, body=%wide.region_13.17_spmd.sunk | while | flops 411672832 | bytes 65810000 | solution.py:259
  610.6 4.7 fusion.198
  624.1 4.7 fusion.198
  643.7 4.6 convolution_add_fusion
  648.4 9.6 scatter_fusion
  658.0 6.0 convert_element_type.177
  672.1 6.4 gather_fusion.12
  692.4 8.3 convolution_convert_fusion
  701.5 5.9 gather_fusion.16
  710.1 4.2 pad_maximum_fusion
  714.2 7.8 gather_fusion.17
  722.0 8.4 copy.271
  732.6 11.2 all-reduce
  745.5 7.3 bitcast_select_fusion
  754.9 22.7 %reduce-scatter.16.cloned.1.call-done = f32[256,128]{1,0:T(8,128)} async-done(((f32[256,1024]{1,0:T(8,128)}), f32[256,128]{1,0:T(8,128)}) %reduce-scatter.16.cloned.1.call-update) | async-done | bytes 131088 | tf_op jit(solution)/shard_map/reduce_scatter | solution.py:305
  780.0 75.6 %reduce-scatter.14.cloned.1.call-done = f32[3,128,256]{2,1,0:T(8,128)} async-done(((f32[3,1024,256]{2,1,0:T(8,128)}), f32[3,128,256]{2,1,0:T(8,128)}) %reduce-scatter.14.cloned.1.call-update) | async-done | bytes 393232 | tf_op jit(solution)/shard_map/reduce_scatter | solution.py:304
  858.9 43.0 %reduce-scatter.10.cloned.1.call-done = bf16[2048,256]{1,0:T(8,128)(2,1)} async-done(((bf16[2048,1024]{1,0:T(8,128)(2,1)}), bf16[2048,256]{1,0:T(8,128)(2,1)}) %reduce-scatter.10.cloned.1.call-update) | async-done | bytes 1048592 | tf_op jit(solution)/shard_map/reduce_scatter | solution.py:183
  911.4 56.5 %reduce-scatter.22.cloned.1.call-done = f32[128,2]{1,0:T(8,128)} async-done(((f32[1024,2]{1,0:T(8,128)}), f32[128,2]{1,0:T(8,128)}) %reduce-scatter.22.cloned.1.call-update) | async-done | bytes 1040
  970.0 150.2 %reduce-scatter.18.cloned.1.call-done = f32[2,128,1024]{2,1,0:T(8,128)} async-done(((f32[2,1024,1024]{2,1,0:T(8,128)}), f32[2,128,1024]{2,1,0:T(8,128)}) %reduce-scatter.18.cloned.1.call-update) | async-done | bytes 1048592 | tf_op jit(solution)/shard_map/reduce_scatter | solution.py:308
  1120.2 4.0 fusion.116
  (369 shorter events, 181.3 us)
Async XLA Ops:
  7.2 29.2 %copy-start.51 = (f32[256,128]{1,0:T(8,128)S(1)}, f32[256,128]{1,0:T(8,128)}, u32[]{:S(2)}) copy-start(f32[256,128]{1,0:T(8,128)} %param.40) | copy-start | bytes 393220
  7.2 61.0 %all-gather.7.cloned.1.call-start = ((), (), s32[]{:S(2)}) async-start(), calls=%async_computation.8 | async-start | bytes 1769472 | tf_op jit(solution)/shard_map/all_gather | solution.py:121
  9.0 90.9 %all-gather.5.cloned.1.call-start = ((), (), s32[]{:S(2)}) async-start(), calls=%async_computation.7 | async-start | bytes 5242880 | tf_op jit(solution)/shard_map/all_gather | solution.py:132
  9.8 205.1 %all-gather.9.cloned.1.call-start = ((), (), s32[]{:S(2)}) async-start(), calls=%async_computation.10 | async-start | bytes 4718592 | tf_op jit(solution)/shard_map/all_gather | solution.py:123
  12.0 345.1 %all-reduce.4.cloned.1.call-start = ((), (), s32[]{:S(2)}) async-start(), calls=%async_computation.9 | async-start | bytes 16777216 | tf_op jit(solution)/shard_map/psum | solution.py:173
  13.1 60.4 %copy-start.65 = (pred[1024]{0:T(1024)(128)(4,1)}, pred[1024]{0:T(1024)(128)(4,1)S(1)}, u32[]{:S(2)}) copy-start(pred[1024]{0:T(1024)(128)(4,1)S(1)} %broadcast_bitcast_fusion.1) | copy-start | bytes 3076
  13.1 55.1 %copy-start.70 = (s32[1024]{0:T(1024)}, s32[1024]{0:T(1024)S(1)}, u32[]{:S(2)}) copy-start(s32[1024]{0:T(1024)S(1)} %pad_clamp_fusion.3) | copy-start | bytes 12292
  36.5 66.7 %copy-start.67 = (f32[1,1024]{1,0:T(1,128)}, f32[1,1024]{1,0:T(1,128)S(1)}, u32[]{:S(2)}) copy-start(f32[1,1024]{1,0:T(1,128)S(1)} %get-tuple-element.276) | copy-start | bytes 12292
  37.0 87.8 %copy-start.26 = (f32[1024,32]{0,1:T(8,128)}, f32[1024,32]{0,1:T(8,128)S(1)}, u32[]{:S(2)}) copy-start(f32[1024,32]{0,1:T(8,128)S(1)} %get-tuple-element.279) | copy-start | bytes 393220
  37.0 87.8 %copy-start.29 = (f32[1024,32]{0,1:T(8,128)}, f32[1024,32]{0,1:T(8,128)S(1)}, u32[]{:S(2)}) copy-start(f32[1024,32]{0,1:T(8,128)S(1)} %get-tuple-element.280) | copy-start | bytes 393220
  75.2 29.3 %copy-start.18 = (bf16[3,1024,256]{1,2,0:T(8,128)(2,1)}, bf16[3,1024,256]{1,2,0:T(8,128)(2,1)S(1)}, u32[]{:S(2)}) copy-start(bf16[3,1024,256]{1,2,0:T(8,128)(2,1)S(1)} %select_bitcast_fusion.1) | copy-start | bytes 4718596
  202.0 292.4 %reduce-scatter.20.cloned.1.call-start = ((), (), s32[]{:S(2)}) async-start(), calls=%async_computation.18 | async-start | bytes 4718592 | tf_op jit(solution)/shard_map/reduce_scatter | solution.py:311
  204.4 15.3 %copy-start.68 = (s32[306]{0:T(512)}, s32[306]{0:T(512)S(1)}, u32[]{:S(2)}) copy-start(s32[306]{0:T(512)S(1)} %fusion.109) | copy-start | bytes 3676
  230.3 132.6 %copy-start.64 = (f32[1,1024]{1,0:T(1,128)S(1)}, f32[1,1024]{1,0:T(1,128)}, u32[]{:S(2)}) copy-start(f32[1,1024]{1,0:T(1,128)} %get-tuple-element.275) | copy-start | bytes 12292
  372.7 8.6 copy-start.10
  405.6 88.8 %copy-start.53 = (f32[1024,128]{1,0:T(8,128)S(1)}, f32[1024,128]{1,0:T(8,128)}, u32[]{:S(2)}) copy-start(f32[1024,128]{1,0:T(8,128)} %param.48) | copy-start | bytes 1572868
  405.6 142.7 %all-gather.11.cloned.1.call-start = ((), (), s32[]{:S(2)}) async-start(), calls=%async_computation.11 | async-start | bytes 2359296 | tf_op jit(solution)/shard_map/all_gather | solution.py:124
  497.4 104.2 %all-reduce.6.cloned.1.call-start = ((), (), s32[]{:S(2)}) async-start(), calls=%async_computation.13 | async-start | bytes 2555904 | tf_op jit(solution)/shard_map/psum | solution.py:212
  564.7 165.7 %reduce-scatter.12.cloned.1.call-start = ((), (), s32[]{:S(2)}) async-start(), calls=%async_computation.14 | async-start | bytes 5242880 | tf_op jit(solution)/shard_map/reduce_scatter | solution.py:285
  637.4 6.3 copy-start.24
  664.1 113.6 %reduce-scatter.16.cloned.1.call-start = ((), (), s32[]{:S(2)}) async-start(), calls=%async_computation.16 | async-start | bytes 1179648 | tf_op jit(solution)/shard_map/reduce_scatter | solution.py:305
  672.1 6.5 copy-start.40
  672.1 183.6 %reduce-scatter.14.cloned.1.call-start = ((), (), s32[]{:S(2)}) async-start(), calls=%async_computation.15 | async-start | bytes 3538944 | tf_op jit(solution)/shard_map/reduce_scatter | solution.py:304
  690.8 211.1 %reduce-scatter.10.cloned.1.call-start = ((), (), s32[]{:S(2)}) async-start(), calls=%async_computation.12 | async-start | bytes 5242880 | tf_op jit(solution)/shard_map/reduce_scatter | solution.py:183
  700.8 267.1 %reduce-scatter.22.cloned.1.call-start = ((), (), s32[]{:S(2)}) async-start(), calls=%async_computation.19 | async-start | bytes 589824
  701.5 28.9 %copy-start.71 = (f32[1,256]{1,0:T(1,128)}, f32[1,256]{1,0:T(1,128)S(1)}, u32[]{:S(2)}) copy-start(f32[1,256]{1,0:T(1,128)S(1)} %constant_dynamic-slice_fusion) | copy-start | bytes 3076
  701.5 5.9 copy-start.47
  722.0 8.4 copy-start.13
  722.0 8.4 copy-start.59
  745.5 374.8 %reduce-scatter.18.cloned.1.call-start = ((), (), s32[]{:S(2)}) async-start(), calls=%async_computation.17 | async-start | bytes 9437184 | tf_op jit(solution)/shard_map/reduce_scatter | solution.py:308
  752.8 24.8 %copy-start.52 = (f32[256,128]{1,0:T(8,128)S(1)}, f32[256,128]{1,0:T(8,128)}, u32[]{:S(2)}) copy-start(f32[256,128]{1,0:T(8,128)} %param.40) | copy-start | bytes 393220
  752.8 24.8 %copy-start.61 = (f32[256,128]{1,0:T(8,128)S(1)}, f32[256,128]{1,0:T(8,128)}, u32[]{:S(2)}) copy-start(f32[256,128]{1,0:T(8,128)} %param.41) | copy-start | bytes 393220
  752.8 24.8 %copy-start.62 = (f32[256,128]{1,0:T(8,128)S(1)}, f32[256,128]{1,0:T(8,128)}, u32[]{:S(2)}) copy-start(f32[256,128]{1,0:T(8,128)} %param.42) | copy-start | bytes 393220
  752.8 26.5 %copy-start.63 = (f32[256,128]{1,0:T(8,128)S(1)}, f32[256,128]{1,0:T(8,128)}, u32[]{:S(2)}) copy-start(f32[256,128]{1,0:T(8,128)} %param.43) | copy-start | bytes 393220
  752.9 102.8 %copy-start.41 = (f32[3,128,256]{2,1,0:T(8,128)S(1)}, f32[3,128,256]{2,1,0:T(8,128)}, u32[]{:S(2)}) copy-start(f32[3,128,256]{2,1,0:T(8,128)} %param.36) | copy-start | bytes 1179652
  754.0 104.0 %copy-start.54 = (f32[3,128,256]{2,1,0:T(8,128)S(1)}, f32[3,128,256]{2,1,0:T(8,128)}, u32[]{:S(2)}) copy-start(f32[3,128,256]{2,1,0:T(8,128)} %param.39) | copy-start | bytes 1179652
  779.3 125.7 %copy-start.49 = (f32[256,128]{1,0:T(8,128)}, f32[256,128]{1,0:T(8,128)S(1)}, u32[]{:S(2)}) copy-start(f32[256,128]{1,0:T(8,128)S(1)} %get-tuple-element.245) | copy-start | bytes 393220
  858.0 47.0 %copy-start.42 = (f32[3,128,256]{2,1,0:T(8,128)}, f32[3,128,256]{2,1,0:T(8,128)S(1)}, u32[]{:S(2)}) copy-start(f32[3,128,256]{2,1,0:T(8,128)S(1)} %get-tuple-element.249) | copy-start | bytes 1179652
  858.0 47.0 %copy-start.72 = (f32[2048]{0:T(1024)S(1)}, f32[2048]{0:T(1024)}, u32[]{:S(2)}) copy-start(f32[2048]{0:T(1024)} %get-tuple-element.230) | copy-start | bytes 24580
  858.0 47.0 %copy-start.60 = (f32[2048]{0:T(1024)S(1)}, f32[2048]{0:T(1024)}, u32[]{:S(2)}) copy-start(f32[2048]{0:T(1024)} %copy-done.58) | copy-start | bytes 24580
  906.8 62.0 %copy-start.77 = (f32[2,128]{1,0:T(2,128)S(1)}, f32[2,128]{1,0:T(2,128)}, u32[]{:S(2)}) copy-start(f32[2,128]{1,0:T(2,128)} %param.52) | copy-start | bytes 3076
  906.8 62.0 %copy-start.78 = (f32[2,128]{1,0:T(2,128)S(1)}, f32[2,128]{1,0:T(2,128)}, u32[]{:S(2)}) copy-start(f32[2,128]{1,0:T(2,128)} %param.53) | copy-start | bytes 3076
  906.9 62.0 %copy-start.79 = (f32[2,128]{1,0:T(2,128)S(1)}, f32[2,128]{1,0:T(2,128)}, u32[]{:S(2)}) copy-start(f32[2,128]{1,0:T(2,128)} %param.54) | copy-start | bytes 3076
  906.9 62.5 %copy-start.80 = (f32[2,128]{1,0:T(2,128)S(1)}, f32[2,128]{1,0:T(2,128)}, u32[]{:S(2)}) copy-start(f32[2,128]{1,0:T(2,128)} %param.55) | copy-start | bytes 3076
  906.9 213.3 %copy-start.23 = (f32[2,128,1024]{2,1,0:T(8,128)S(1)}, f32[2,128,1024]{2,1,0:T(8,128)}, u32[]{:S(2)}) copy-start(f32[2,128,1024]{2,1,0:T(8,128)} %param.44) | copy-start | bytes 3145732
  968.8 155.4 %copy-start.73 = (f32[2,128]{1,0:T(2,128)}, f32[2,128]{1,0:T(2,128)S(1)}, u32[]{:S(2)}) copy-start(f32[2,128]{1,0:T(2,128)S(1)} %copy.282) | copy-start | bytes 3076
  969.4 154.9 %copy-start.74 = (f32[2,128]{1,0:T(2,128)}, f32[2,128]{1,0:T(2,128)S(1)}, u32[]{:S(2)}) copy-start(f32[2,128]{1,0:T(2,128)S(1)} %get-tuple-element.233) | copy-start | bytes 3076
  970.0 154.3 %copy-start.45 = (f32[2,128,1024]{2,1,0:T(8,128)S(1)}, f32[2,128,1024]{2,1,0:T(8,128)}, u32[]{:S(2)}) copy-start(f32[2,128,1024]{2,1,0:T(8,128)} %param.47) | copy-start | bytes 3145732
  (57 other events, 139.6 us)
Sparse Core Ops, SparseCore 0:
  10.8 51.6 all-gather.6
  64.1 35.8 all-gather.4
  102.7 73.3 all-gather.8
  202.1 154.8 all-reduce.3
  405.7 88.5 reduce-scatter.19
  497.5 50.8 all-gather.10
  564.9 36.6 all-reduce.5
  664.2 44.5 reduce-scatter.11
  713.7 63.8 reduce-scatter.15
  781.6 73.9 reduce-scatter.13
  858.2 43.6 reduce-scatter.9
  906.0 61.8 reduce-scatter.21
  972.1 148.0 reduce-scatter.17
where the time goes:
time: 1140 us; the launch traced here: 1130 us
  waiting for transfers between devices  638 us (56%)
  local copies, waits for them, and re-layouts  166 us (15%)
  other arithmetic  125 us (11%)
  matrix products  113 us (10%)
  blocking collectives  73.1 us (6%)
  between operations  15.7 us (1%)
    reduce_scatter x1, waiting for transfers between devices, local(): lax.psum_scatter(reorder(gate_up_grad, owner, dp_count), 'dp', scatter_di...  150 us
    psum x1, waiting for transfers between devices, local(): attn_sum = lax.psum(attn_part, 'mp')  127 us
    reduce_scatter x1, waiting for transfers between devices, local(): lax.psum_scatter(reorder(down_grad, owner, dp_count), 'dp', scatter_dimen...  88.3 us
    reduce_scatter x1, waiting for transfers between devices, local(): lax.psum_scatter(reorder(qkv_grad, owner, dp_count), 'dp', scatter_dimens...  75.6 us
    unnamed x14, waiting for transfers between devices  57.4 us
    gather x17, local copies, waits for them, and re-layouts, reorder(): taken = jnp.take(shaped, block_order, axis=0).reshape(moved_axis.shape)  50.6 us
    reduce_scatter x1, waiting for transfers between devices, local(): lax.psum_scatter(ffn_part.astype(jnp.bfloat16), 'mp', scatter_dimension=1...  43 us
    all_gather x1, waiting for transfers between devices, local(): lax.all_gather(down_master.astype(jnp.bfloat16), 'dp', axis=1, tiled=True)  37.3 us
  transfers between devices with their start and end apart: 13, of which 10 were waited for; matrix products, arithmetic and copies ran while one was open for 23% of the time, Pallas kernels for 0%

commit v1 on v0

v1 whole, which is shorter than its diff:
```python
import functools

import jax
import jax.numpy as jnp
from jax import lax
from jax.experimental import pallas as pl
from jax.experimental.pallas import tpu as pltpu
from jax.sharding import PartitionSpec as P

D = 1024
FF = 4096
HEAD_DIM = 64
SEQ = 1024
NGROUP = 16
STEP = 7

EPS = 1e-05
THETA = 10000.0
BETA_ONE = 0.5
BETA_TWO = 0.5
ADAM_EPS = 1e-08
DECAY_RATE = 0.1
EMA_RATE = 0.6
GAIN_RATE = 0.4

BF = jnp.bfloat16
F32 = jnp.float32
LANES = 128
TILE = 256
MIB = 1024 * 1024
SOFT = 1.4426950408889634 * HEAD_DIM**-0.5


def dot(a, b):
    return lax.dot_general(a, b, (((1,), (0,)), ((), ())), preferred_element_type=F32)


def dot_t(a, b):
    return lax.dot_general(a, b, (((1,), (1,)), ((), ())), preferred_element_type=F32)


def dot_l(a, b):
    return lax.dot_general(a, b, (((0,), (0,)), ((), ())), preferred_element_type=F32)


def params(mib, dims=None):
    return pltpu.CompilerParams(vmem_limit_bytes=mib * MIB, dimension_semantics=dims)


def swap(x, axis, bit):
    n = lax.axis_size(axis)
    return lax.ppermute(x, axis, [(i, i ^ bit) for i in range(n)])


def gather_mp(x):
    far = swap(x, "mp", 2)
    near = swap(x, "mp", 1)
    return [x, near, far, swap(far, "mp", 1)]


def whole(shape):
    return pl.BlockSpec(shape, lambda *_: (0,) * len(shape), pipeline_mode=pl.Buffered(1))


def cut(block, where):
    return pl.BlockSpec(block, where)


def rotary_tables(positions):
    half_dim = HEAD_DIM // 2
    frequency = THETA ** (-jnp.arange(half_dim, dtype=F32) / half_dim)
    angles = positions.astype(F32)[:, None] * frequency[None, :]
    cosine, sine = jnp.cos(angles), jnp.sin(angles)
    return (
        jnp.concatenate([cosine] * 4, axis=1),
        jnp.concatenate([-sine, sine, -sine, sine], axis=1),
    )


def turn(x, cos, sin, sign):
    lane = lax.broadcasted_iota(jnp.int32, (x.shape[0], LANES), 1)
    low = (lane % HEAD_DIM) < HEAD_DIM // 2
    parts = []
    for start in range(0, x.shape[1], LANES):
        v = x[:, start : start + LANES]
        other = jnp.where(
            low, pltpu.roll(v, LANES - HEAD_DIM // 2, 1), pltpu.roll(v, HEAD_DIM // 2, 1)
        )
        parts.append(v * cos + (sign * sin) * other)
    return jnp.concatenate(parts, axis=1)


def place_kernel(pos_ref, *refs):
    out = refs[-1]
    for p, piece in enumerate(refs[:-1]):
        rows = piece.shape[1]
        out[:, pl.ds(pl.multiple_of(pos_ref[p], rows), rows), :] = piece[...]


def place_pieces(pos, pieces):
    k, bs, n = pieces[0].shape
    total = bs * len(pieces)
    return pl.pallas_call(
        place_kernel,
        grid_spec=pltpu.PrefetchScalarGridSpec(
            num_scalar_prefetch=1,
            grid=(1,),
            in_specs=[pl.BlockSpec((k, bs, n), lambda i, pos: (0, 0, 0))] * len(pieces),
            out_specs=pl.BlockSpec((k, total, n), lambda i, pos: (0, 0, 0)),
        ),
        out_shape=jax.ShapeDtypeStruct((k, total, n), pieces[0].dtype),
        compiler_params=params(24),
    )(pos, *pieces)


def place_stack_kernel(pos_ref, in_ref, out_ref):
    out_ref[0] = in_ref[0, 0]


def place_stack(pos, stack):
    count, k, bs, n = stack.shape
    return pl.pallas_call(
        place_stack_kernel,
        grid_spec=pltpu.PrefetchScalarGridSpec(
            num_scalar_prefetch=1,
            grid=(count, k),
            in_specs=[pl.BlockSpec((1, 1, bs, n), lambda j, w, pos: (j, w, 0, 0))],
            out_specs=pl.BlockSpec((1, bs, n), lambda j, w, pos: (w, pos[j] // bs, 0)),
        ),
        out_shape=jax.ShapeDtypeStruct((k, count * bs, n), stack.dtype),
        compiler_params=params(16),
    )(pos, stack)


def qkv_kernel(x0, x1, x2, x3, g_ref, w_ref, cos_ref, sin_ref, oh_ref,
               qkv_ref, norm_ref, trow_ref, qrow_ref, tacc, qacc):
    step = pl.program_id(0)
    x = jnp.concatenate([x0[...], x1[...], x2[...], x3[...]], axis=1)
    xf = x.astype(F32)
    scale = lax.rsqrt(jnp.mean(xf * xf, axis=1, keepdims=True) + EPS)
    norm = (xf * scale * g_ref[...]).astype(BF)
    norm_ref[...] = norm
    cos, sin = cos_ref[...], sin_ref[...]
    q = turn(dot(norm, w_ref[0]), cos, sin, 1.0).astype(BF)
    qkv_ref[0] = q
    qkv_ref[1] = turn(dot(norm, w_ref[1]), cos, sin, 1.0).astype(BF)
    qkv_ref[2] = dot(norm, w_ref[2]).astype(BF)
    oh = oh_ref[...]

    @pl.when(step == 0)
    def _():
        tacc[...] = jnp.zeros_like(tacc)
        qacc[...] = jnp.zeros_like(qacc)

    tacc[...] += dot(oh, x)
    qacc[...] += dot(oh, q)

    @pl.when(step == pl.num_programs(0) - 1)
    def _():
        trow_ref[...] = tacc[...].astype(BF)
        qrow_ref[...] = qacc[...].astype(BF)


def qkv_call(pieces, w, gain, weights, cos, sin, onehot):
    share = pieces[0].shape[1]
    rows = onehot.shape[0]
    tiles = SEQ // TILE
    return pl.pallas_call(
        qkv_kernel,
        grid=(tiles,),
        in_specs=[cut((TILE, share), lambda i: (w * tiles + i, 0))] * 4
        + [
            whole((1, D)),
            whole((4, D, share)),
            cut((TILE, LANES), lambda i: (i, 0)),
            cut((TILE, LANES), lambda i: (i, 0)),
            cut((rows, TILE), lambda i: (0, i)),
        ],
        out_specs=[
            cut((3, TILE, share), lambda i: (0, i, 0)),
            cut((TILE, D), lambda i: (i, 0)),
            cut((rows, D), lambda i: (0, 0)),
            cut((rows, share), lambda i: (0, 0)),
        ],
        out_shape=[
            jax.ShapeDtypeStruct((3, SEQ, share), BF),
            jax.ShapeDtypeStruct((SEQ, D), BF),
            jax.ShapeDtypeStruct((rows, D), BF),
            jax.ShapeDtypeStruct((rows, share), BF),
        ],
        scratch_shapes=[pltpu.VMEM((rows, D), F32), pltpu.VMEM((rows, share), F32)],
        compiler_params=params(32),
        cost_estimate=pl.CostEstimate(
            flops=2 * SEQ * D * 3 * share, bytes_accessed=8 * MIB, transcendentals=0
        ),
    )(*pieces, gain, weights, cos, sin, onehot)


def attend_kernel(q_ref, k_ref, v_ref, oh_ref, ctx_ref, crow_ref, acc):
    step = pl.program_id(0)
    lane = lax.broadcasted_iota(jnp.int32, (TILE, LANES), 1)
    first = lane < HEAD_DIM
    ones = jnp.ones((SEQ, LANES), BF)
    parts = []
    for start in range(0, q_ref.shape[2], LANES):
        q = q_ref[0, :, start : start + LANES]
        k = k_ref[0, :, start : start + LANES]
        v = jnp.concatenate([v_ref[0, :, start : start + LANES], ones], axis=1)
        heads = []
        for mine in (first, jnp.logical_not(first)):
            scores = dot_t(jnp.where(mine, q, jnp.zeros_like(q)), k)
            top = jnp.max(scores, axis=1, keepdims=True)
            weight = jnp.exp2((scores - top) * SOFT).astype(BF)
            mixed = dot(weight, v)
            heads.append(mixed[:, :LANES] / mixed[:, LANES:])
        parts.append(jnp.where(first, heads[0], heads[1]))
    context = jnp.concatenate(parts, axis=1).astype(BF)
    ctx_ref[...] = context

    @pl.when(step == 0)
    def _():
        acc[...] = jnp.zeros_like(acc)

    acc[...] += dot(oh_ref[...], context)

    @pl.when(step == pl.num_programs(0) - 1)
    def _():
        crow_ref[...] = acc[...].astype(BF)


def attend_call(qkv, onehot):
    share = qkv.shape[2]
    rows = onehot.shape[0]
    return pl.pallas_call(
        attend_kernel,
        grid=(SEQ // TILE,),
        in_specs=[
            cut((1, TILE, share), lambda i: (0, i, 0)),
            cut((1, SEQ, share), lambda i: (1, 0, 0)),
            cut((1, SEQ, share), lambda i: (2, 0, 0)),
            cut((rows, TILE), lambda i: (0, i)),
        ],
        out_specs=[
            cut((TILE, share), lambda i: (i, 0)),
            cut((rows, share), lambda i: (0, 0)),
        ],
        out_shape=[
            jax.ShapeDtypeStruct((SEQ, share), BF),
            jax.ShapeDtypeStruct((rows, share), BF),
        ],
        scratch_shapes=[pltpu.VMEM((rows, share), F32)],
        compiler_params=params(32),
        cost_estimate=pl.CostEstimate(
            flops=16 * SEQ * SEQ * share, bytes_accessed=3 * MIB, transcendentals=4 * SEQ * SEQ
        ),
    )(qkv, qkv, qkv, onehot)


def attended(context_pieces, wo_refs):
    share = context_pieces[0].shape[1]
    chunks = [None] * 4
    for r, (piece, wo) in enumerate(zip(context_pieces, wo_refs, strict=True)):
        for c in range(4):
            own = c ^ r
            term = dot_t(piece, wo[c * share : (c + 1) * share, :])
            chunks[own] = term if chunks[own] is None else chunks[own] + term
    return jnp.concatenate(chunks, axis=1)


def ffn_kernel(x0, x1, x2, x3, c0, c1, c2, c3, o0, o1, o2, o3, g_ref, w_ref,
               send_ref, keep_ref, res_ref):
    share = x0.shape[1]
    x = jnp.concatenate([x0[...], x1[...], x2[...], x3[...]], axis=1).astype(F32)
    residual = x + attended([c0[...], c1[...], c2[...], c3[...]], [o0, o1, o2, o3])
    scale = lax.rsqrt(jnp.mean(residual * residual, axis=1, keepdims=True) + EPS)
    norm = (residual * scale * g_ref[...]).astype(BF)
    res_ref[...] = residual[:, :share]
    total = None
    width = w_ref.shape[2]
    for start in range(0, width, TILE):
        gate = dot(norm, w_ref[0, :, start : start + TILE])
        up = dot(norm, w_ref[1, :, start : start + TILE])
        hidden = (gate * jax.nn.sigmoid(gate) * up).astype(BF)
        term = dot_t(hidden, w_ref[2, :, start : start + TILE])
        total = term if total is None else total + term
    out = total.astype(BF)
    send_ref[...] = jnp.concatenate([out[:, share : 2 * share], out[:, 3 * share :]], axis=1)
    keep_ref[...] = jnp.concatenate([out[:, :share], out[:, 2 * share : 3 * share]], axis=1)


def ffn_call(pieces, w, contexts, wo, gain, weights):
    share = pieces[0].shape[1]
    width = weights.shape[2]
    tiles = SEQ // TILE
    return pl.pallas_call(
        ffn_kernel,
        grid=(tiles,),
        in_specs=[cut((TILE, share), lambda i: (w * tiles + i, 0))] * 4
        + [cut((TILE, share), lambda i: (i, 0))] * 4
        + [whole((D, share))] * 4
        + [whole((1, D)), whole((3, D, width))],
        out_specs=[
            cut((TILE, 2 * share), lambda i: (i, 0)),
            cut((TILE, 2 * share), lambda i: (i, 0)),
            cut((TILE, share), lambda i: (i, 0)),
        ],
        out_shape=[
            jax.ShapeDtypeStruct((SEQ, 2 * share), BF),
            jax.ShapeDtypeStruct((SEQ, 2 * share), BF),
            jax.ShapeDtypeStruct((SEQ, share), F32),
        ],
        compiler_params=params(40),
        cost_estimate=pl.CostEstimate(
            flops=8 * SEQ * D * D, bytes_accessed=16 * MIB, transcendentals=SEQ * width
        ),
    )(*pieces, *contexts, *wo, gain, weights)


def rows_kernel(t_ref, c0, c1, c2, c3, o0, o1, o2, o3, g_ref, seed_ref, w_ref,
                norm_ref, hid_ref, gg_ref, ug_ref, send_ref, keep_ref, unit_ref, scale_ref, acc):
    step = pl.program_id(0)
    share = c0.shape[1]

    @pl.when(step == 0)
    def _():
        residual = t_ref[...].astype(F32) + attended(
            [c0[...], c1[...], c2[...], c3[...]], [o0, o1, o2, o3]
        )
        scale = lax.rsqrt(jnp.mean(residual * residual, axis=1, keepdims=True) + EPS)
        unit = residual * scale
        unit_ref[...] = unit
        scale_ref[...] = jnp.broadcast_to(scale, scale_ref.shape)
        norm_ref[...] = (residual * scale * g_ref[...]).astype(BF)
        acc[...] = jnp.zeros_like(acc)

    norm = norm_ref[...]
    gate = dot(norm, w_ref[0])
    up = dot(norm, w_ref[1])
    sigmoid = jax.nn.sigmoid(gate)
    silu = gate * sigmoid
    hid_ref[...] = (silu * up).astype(BF)
    hidden_grad = dot(seed_ref[...], w_ref[2])
    gate_grad = (hidden_grad * up * sigmoid * (1.0 + gate * (1.0 - sigmoid))).astype(BF)
    up_grad = (hidden_grad * silu).astype(BF)
    gg_ref[...] = gate_grad
    ug_ref[...] = up_grad
    acc[...] += dot_t(gate_grad, w_ref[0]) + dot_t(up_grad, w_ref[1])

    @pl.when(step == pl.num_programs(0) - 1)
    def _():
        out = acc[...].astype(BF)
        send_ref[...] = jnp.concatenate([out[:, share : 2 * share], out[:, 3 * share :]], axis=1)
        keep_ref[...] = jnp.concatenate([out[:, :share], out[:, 2 * share : 3 * share]], axis=1)


def rows_call(token_rows, context_rows, wo, gain, seed, weights):
    rows = token_rows.shape[0]
    share = context_rows[0].shape[1]
    width = weights.shape[2]
    part = 256
    fixed = lambda shape: pl.BlockSpec(shape, lambda i: (0,) * len(shape))
    return pl.pallas_call(
        rows_kernel,
        grid=(width // part,),
        in_specs=[whole((rows, D))]
        + [whole((rows, share))] * 4
        + [whole((D, share))] * 4
        + [whole((1, D)), whole((rows, D)), cut((3, D, part), lambda i: (0, 0, i))],
        out_specs=[
            fixed((rows, D)),
            cut((rows, part), lambda i: (0, i)),
            cut((rows, part), lambda i: (0, i)),
            cut((rows, part), lambda i: (0, i)),
            fixed((rows, 2 * share)),
            fixed((rows, 2 * share)),
            fixed((rows, D)),
            fixed((rows, LANES)),
        ],
        out_shape=[
            jax.ShapeDtypeStruct((rows, D), BF),
            jax.ShapeDtypeStruct((rows, width), BF),
            jax.ShapeDtypeStruct((rows, width), BF),
            jax.ShapeDtypeStruct((rows, width), BF),
            jax.ShapeDtypeStruct((rows, 2 * share), BF),
            jax.ShapeDtypeStruct((rows, 2 * share), BF),
            jax.ShapeDtypeStruct((rows, D), F32),
            jax.ShapeDtypeStruct((rows, LANES), F32),
        ],
        scratch_shapes=[pltpu.VMEM((rows, D), F32)],
        compiler_params=params(40),
        cost_estimate=pl.CostEstimate(
            flops=12 * rows * D * D, bytes_accessed=12 * MIB, transcendentals=rows * width
        ),
    )(token_rows, *context_rows, *wo, gain, seed, weights)


def pack_kernel(pos_ref, lhs_ref, rhs_ref, out_ref):
    out_ref[0] = dot_l(lhs_ref[...], rhs_ref[...]).astype(BF)


def pack_send(pos, lhs, rhs):
    count = pos.shape[0]
    rows, n = rhs.shape
    return pl.pallas_call(
        pack_kernel,
        grid_spec=pltpu.PrefetchScalarGridSpec(
            num_scalar_prefetch=1,
            grid=(count,),
            in_specs=[
                pl.BlockSpec((rows, LANES), lambda i, pos: (0, pos[i] // LANES)),
                pl.BlockSpec((rows, n), lambda i, pos: (0, 0)),
            ],
            out_specs=pl.BlockSpec((1, LANES, n), lambda i, pos: (i, 0, 0)),
        ),
        out_shape=jax.ShapeDtypeStruct((count, LANES, n), BF),
        compiler_params=params(24),
        cost_estimate=pl.CostEstimate(
            flops=2 * rows * n * LANES * count, bytes_accessed=2 * MIB, transcendentals=0
        ),
    )(pos, lhs, rhs)


def pack_add_kernel(pos_ref, lhs_ref, rhs_ref, recv_ref, *outs):
    step = pl.program_id(0)
    value = dot_l(lhs_ref[...], rhs_ref[...]) + recv_ref[0].astype(F32)
    for k, out in enumerate(outs):

        @pl.when(step == k)
        def _(out=out):
            out[...] = value.astype(out.dtype)


def pack_keep(pos, lhs, rhs, received):
    count = pos.shape[0]
    rows, n = rhs.shape
    fixed = pl.BlockSpec((LANES, n), lambda i, pos: (0, 0))
    return pl.pallas_call(
        pack_add_kernel,
        grid_spec=pltpu.PrefetchScalarGridSpec(
            num_scalar_prefetch=1,
            grid=(count,),
            in_specs=[
                pl.BlockSpec((rows, LANES), lambda i, pos: (0, pos[i] // LANES)),
                pl.BlockSpec((rows, n), lambda i, pos: (0, 0)),
                pl.BlockSpec((1, LANES, n), lambda i, pos: (i, 0, 0)),
            ],
            out_specs=[fixed] * count,
        ),
        out_shape=[
            jax.ShapeDtypeStruct((LANES, n), F32 if k == 0 else BF) for k in range(count)
        ],
        compiler_params=params(24),
        cost_estimate=pl.CostEstimate(
            flops=2 * rows * n * LANES * count, bytes_accessed=3 * MIB, transcendentals=0
        ),
    )(pos, lhs, rhs, received)


def back_kernel(q_ref, do_ref, k_ref, v_ref, oh_ref, cosm_ref, sinm_ref, cos_ref, sin_ref, out_ref):
    rows, share = q_ref.shape
    lane = lax.broadcasted_iota(jnp.int32, (rows, LANES), 1)
    first = lane < HEAD_DIM
    scale = HEAD_DIM**-0.5
    dq_parts, dk_parts, dv_parts = [], [], []
    for start in range(0, share, LANES):
        q = q_ref[:, start : start + LANES]
        do = do_ref[:, start : start + LANES]
        k = k_ref[0, :, start : start + LANES]
        v = v_ref[0, :, start : start + LANES]
        dqs, dk, dv = [], None, None
        for mine in (first, jnp.logical_not(first)):
            qm = jnp.where(mine, q, jnp.zeros_like(q))
            dm = jnp.where(mine, do, jnp.zeros_like(do))
            scores = dot_t(qm, k)
            top = jnp.max(scores, axis=1, keepdims=True)
            weight = jnp.exp2((scores - top) * SOFT)
            prob = weight * (1.0 / jnp.sum(weight, axis=1, keepdims=True))
            prob_grad = dot_t(dm, v)
            delta = jnp.sum(prob * prob_grad, axis=1, keepdims=True)
            score_grad = (prob * (prob_grad - delta)).astype(BF)
            dqs.append(dot(score_grad, k))
            term = dot_l(score_grad, qm)
            dk = term if dk is None else dk + term
            term = dot_l(prob.astype(BF), dm)
            dv = term if dv is None else dv + term
        dq_parts.append(jnp.where(first, dqs[0], dqs[1]) * scale)
        dk_parts.append(dk * scale)
        dv_parts.append(dv)
    dq = turn(jnp.concatenate(dq_parts, axis=1), cosm_ref[...], sinm_ref[...], -1.0).astype(BF)
    out_ref[:, :share] = dot_l(oh_ref[...], dq).astype(BF)
    dk = turn(jnp.concatenate(dk_parts, axis=1), cos_ref[...], sin_ref[...], -1.0)
    out_ref[:, share : 2 * share] = dk.astype(BF)
    out_ref[:, 2 * share :] = jnp.concatenate(dv_parts, axis=1).astype(BF)


def back_call(q_rows, context_grad, w, qkv, onehot, cosm, sinm, cos, sin):
    rows, share = q_rows.shape
    here = lambda shape: pl.BlockSpec(shape, lambda i: (w,) + (0,) * (len(shape) - 1))
    zero = lambda shape: pl.BlockSpec(shape, lambda i: (0,) * len(shape))
    return pl.pallas_call(
        back_kernel,
        grid=(1,),
        in_specs=[
            zero((rows, share)),
            here((rows, share)),
            pl.BlockSpec((1, SEQ, share), lambda i: (1, 0, 0)),
            pl.BlockSpec((1, SEQ, share), lambda i: (2, 0, 0)),
            zero((rows, SEQ)),
            here((rows, LANES)),
            here((rows, LANES)),
            zero((SEQ, LANES)),
            zero((SEQ, LANES)),
        ],
        out_specs=zero((SEQ, 3 * share)),
        out_shape=jax.ShapeDtypeStruct((SEQ, 3 * share), BF),
        compiler_params=params(40),
        cost_estimate=pl.CostEstimate(
            flops=40 * rows * SEQ * share, bytes_accessed=4 * MIB, transcendentals=4 * rows * SEQ
        ),
    )(q_rows, context_grad, qkv, qkv, onehot, cosm, sinm, cos, sin)


def first_grad_kernel(d_ref, w_ref, x0, x1, x2, x3, g_ref, send_ref, keep_ref, dot_ref, col_ref):
    share = x0.shape[1]
    grad = None
    for t in range(3):
        term = dot_t(d_ref[:, t * share : (t + 1) * share], w_ref[t])
        grad = term if grad is None else grad + term
    x = jnp.concatenate([x0[...], x1[...], x2[...], x3[...]], axis=1).astype(F32)
    scale = lax.rsqrt(jnp.mean(x * x, axis=1, keepdims=True) + EPS)
    gz = grad * (x * scale)
    dot_ref[...] = jnp.sum(gz * g_ref[...], axis=1, keepdims=True)
    out = grad.astype(BF)
    send_ref[...] = jnp.concatenate([out[:, share : 2 * share], out[:, 3 * share :]], axis=1)
    keep_ref[...] = jnp.concatenate([out[:, :share], out[:, 2 * share : 3 * share]], axis=1)

    @pl.when(pl.program_id(0) == 0)
    def _():
        col_ref[...] = jnp.zeros_like(col_ref)

    col_ref[...] += jnp.sum(gz, axis=0, keepdims=True)


def first_grad_call(dqkv, weights, pieces, w, gain):
    share = pieces[0].shape[1]
    tiles = SEQ // TILE
    return pl.pallas_call(
        first_grad_kernel,
        grid=(tiles,),
        in_specs=[cut((TILE, 3 * share), lambda i: (i, 0)), whole((4, D, share))]
        + [cut((TILE, share), lambda i: (w * tiles + i, 0))] * 4
        + [whole((1, D))],
        out_specs=[
            cut((TILE, 2 * share), lambda i: (i, 0)),
            cut((TILE, 2 * share), lambda i: (i, 0)),
            cut((TILE, 1), lambda i: (i, 0)),
            pl.BlockSpec((1, D), lambda i: (0, 0)),
        ],
        out_shape=[
            jax.ShapeDtypeStruct((SEQ, 2 * share), BF),
            jax.ShapeDtypeStruct((SEQ, 2 * share), BF),
            jax.ShapeDtypeStruct((SEQ, 1), F32),
            jax.ShapeDtypeStruct((1, D), F32),
        ],
        compiler_params=params(32),
        cost_estimate=pl.CostEstimate(
            flops=6 * SEQ * D * share, bytes_accessed=8 * MIB, transcendentals=0
        ),
    )(dqkv, weights, *pieces, gain)


def adam_step(summed, master, first_old, second, average, step_rate, weight_decay):
    new_first = BETA_ONE * first_old + (1.0 - BETA_ONE) * summed
    new_second = BETA_TWO * second + (1.0 - BETA_TWO) * summed * summed
    update = (
        new_first
        / (1.0 - BETA_ONE**STEP)
        / (jnp.sqrt(new_second / (1.0 - BETA_TWO**STEP)) + ADAM_EPS)
    )
    new_master = master - step_rate * (update + weight_decay * master)
    new_average = EMA_RATE * average + (1.0 - EMA_RATE) * new_master
    return (summed, new_master, new_first, new_second, new_average, new_master.astype(BF))


def scatter_mp(send, keep):
    share = keep.shape[1] // 2
    near = swap(send, "mp", 1)
    half = keep.astype(F32) + near.astype(F32)
    far = swap(half[:, share:].astype(BF), "mp", 2)
    return half[:, :share] + far.astype(F32)


def local(
    tokens,
    cotangent,
    mask_rows,
    genome,
    group_tokens,
    owner,
    qkv_master,
    qkv_first,
    qkv_second,
    qkv_average,
    proj_master,
    proj_first,
    proj_second,
    proj_average,
    gate_up_master,
    gate_up_first,
    gate_up_second,
    gate_up_average,
    down_master,
    down_first,
    down_second,
    down_average,
    gains_master,
    gains_first,
    gains_second,
    gains_average,
    short=None,
):
    ndp = lax.axis_size("dp")
    me = lax.axis_index("dp")
    m = lax.axis_index("mp")
    share = tokens.shape[1]
    block = qkv_master.shape[1]
    windows, masked = mask_rows.shape
    rows = -(-masked // 32) * 32
    if short is None:
        short = ndp == 8 and block == LANES

    def start(b):
        at = b * block
        return ((at // share) ^ m) * share + at % share

    device = jnp.arange(ndp, dtype=jnp.int32)
    owner_x = jnp.sum(
        jnp.where((device[:, None] ^ me) == device[None, :], owner[None, :], 0), axis=1
    )
    pos = start(owner)
    pos_x = start(owner_x)

    attn_block = jnp.concatenate(
        [qkv_master.astype(BF), proj_master.T.astype(BF)[None]], axis=0
    )
    ffn_block = jnp.concatenate(
        [gate_up_master.astype(BF), down_master.T.astype(BF)[None]], axis=0
    )
    ffn_stack = lax.all_gather(ffn_block, "dp", axis=0, tiled=False)
    far = swap(tokens, "mp", 2)
    near = swap(tokens, "mp", 1)
    if short:
        z_pieces = [attn_block] + [swap(attn_block, "dp", bit) for bit in (2, 4, 6)]
        x_pieces = [swap(piece, "dp", 1) for piece in z_pieces]
        order = [None] * 8
        for k in range(4):
            order[2 * k], order[2 * k + 1] = z_pieces[k], x_pieces[k]
        attn_w = place_pieces(pos_x, order)
    else:
        attn_w = place_stack(pos, lax.all_gather(attn_block, "dp", axis=0, tiled=False))
    gains_x = gains_master.astype(BF)[:, None, :]
    bit = 1
    while bit < ndp:
        gains_x = jnp.concatenate([gains_x, swap(gains_x, "dp", bit)], axis=1)
        bit *= 2
    slot = (device * block)[:, None] == pos_x[None, :]
    gains = jnp.sum(
        jnp.where(slot[None, :, :, None], gains_x.astype(F32)[:, None], 0.0), axis=2
    ).reshape(2, 1, D)

    tokens_p = [tokens, near, far, swap(far, "mp", 1)]
    padded = jnp.pad(mask_rows, ((0, 0), (0, rows - masked)), constant_values=-1)
    onehot = (
        padded[:, :, None] == lax.broadcasted_iota(jnp.int32, (1, 1, SEQ), 2)
    ).astype(BF)
    cos, sin = rotary_tables(jnp.arange(SEQ))
    cosm, sinm = rotary_tables(padded.reshape(-1))
    qkv, norm_one, token_rows, q_rows, context, context_rows = [], [], [], [], [], []
    for w in range(windows):
        a, b, c, d = qkv_call(tokens_p, w, gains[0], attn_w, cos, sin, onehot[w])
        qkv.append(a)
        norm_one.append(b)
        token_rows.append(c)
        q_rows.append(d)
    for w in range(windows):
        a, b = attend_call(qkv[w], onehot[w])
        context.append(a)
        context_rows.append(b)
    wo_p = gather_mp(attn_w[3])
    context_p = [gather_mp(c) for c in context]
    context_rows = jnp.concatenate(context_rows, axis=0)
    context_rows_p = gather_mp(context_rows)
    token_rows = jnp.concatenate(token_rows, axis=0)

    cot = jnp.pad(cotangent.reshape(windows, masked, share), ((0, 0), (0, rows - masked), (0, 0)))
    cot = jnp.concatenate(gather_mp(cot.reshape(windows * rows, share)), axis=1)
    counts = group_tokens.astype(F32)
    picked = jnp.sum(
        jnp.where(
            genome[:, None] == jnp.arange(NGROUP, dtype=jnp.int32)[None, :], counts[None, :], 0.0
        ),
        axis=1,
    )
    window_scale = NGROUP * picked / jnp.sum(counts)
    seed = jnp.repeat(window_scale, rows)[:, None] * cot.astype(F32)
    seed_low = seed.astype(BF)

    ffn_w = place_stack(pos, ffn_stack)
    norm_rows, hidden_rows, gate_grad, up_grad, n2_send, n2_keep, unit, scale_rows = rows_call(
        token_rows, context_rows_p, wo_p, gains[1], seed_low, ffn_w
    )

    def reduce_blocks(lhs, rhs, after=None):
        if short:
            send = pack_send(pos_x[1::2], lhs, rhs)
            if after is not None:
                send, _ = lax.optimization_barrier((send, after))
            received = swap(send, "dp", 1)
            terms = pack_keep(pos_x[0::2], lhs, rhs, received)
            total = terms[0]
            for k in range(1, 4):
                total = total + swap(terms[k], "dp", 2 * k).astype(F32)
            return total, received
        grad = dot_l(lhs, rhs).reshape(ndp, block, rhs.shape[1])
        grad = jnp.take(grad, pos // block, axis=0, mode="clip")
        summed = lax.psum_scatter(grad, "dp", scatter_dimension=0, tiled=True)
        return summed[0], None

    down_sum, after = reduce_blocks(seed_low, hidden_rows)
    gate_sum, after = reduce_blocks(norm_rows, gate_grad, after)
    up_sum, after = reduce_blocks(norm_rows, up_grad, after)

    n2_half = n2_keep.astype(F32) + swap(n2_send, "mp", 1).astype(F32)
    n2_far = swap(n2_half.astype(BF), "mp", 2).astype(F32)
    n2_own = n2_half + jnp.concatenate([n2_far[:, share:], n2_far[:, :share]], axis=1)
    n2_near = swap(n2_own.astype(BF), "mp", 1).astype(F32)
    n2_grad = jnp.concatenate(
        [n2_own[:, :share], n2_near[:, :share], n2_own[:, share:], n2_near[:, share:]], axis=1
    )
    gain_two = jnp.sum(n2_grad * unit, axis=0)
    scaled = n2_grad * gains[1]
    residual_grad = seed + scale_rows[:, :1] * (
        scaled - unit * jnp.mean(scaled * unit, axis=1, keepdims=True)
    )
    attn_seed = residual_grad.astype(BF)
    context_grad = dot(attn_seed, attn_w[3]).astype(BF)

    dqkv = [
        back_call(q_rows[w], context_grad, w, qkv[w], onehot[w], cosm, sinm, cos, sin)
        for w in range(windows)
    ]
    dqkv_all = jnp.concatenate(dqkv, axis=0)
    norm_all = jnp.concatenate(norm_one, axis=0)
    proj_sum, after = reduce_blocks(attn_seed, context_rows, after)
    qkv_sum, after = reduce_blocks(norm_all, dqkv_all, after)

    outputs = []
    for w in range(windows):
        send, keep, residual = ffn_call(
            tokens_p, w, [piece for piece in context_p[w]], wo_p, gains[1], ffn_w
        )
        outputs.append((residual + scatter_mp(send, keep)).astype(BF))
    output = jnp.concatenate(outputs, axis=0)

    own_gain = gains[0][:, :share]
    high = attn_seed[:, :share]
    low = (residual_grad[:, :share] - high.astype(F32)).astype(BF)
    gain_one = None
    inputs = []
    for w in range(windows):
        send, keep, row_dot, col = first_grad_call(dqkv[w], attn_w, tokens_p, w, gains[0])
        gain_one = col if gain_one is None else gain_one + col
        n1_own = scatter_mp(send, keep)
        row_dot = row_dot[:, 0]
        row_dot = row_dot + swap(row_dot, "mp", 1)
        row_dot = row_dot + swap(row_dot, "mp", 2)
        x_own = lax.slice_in_dim(tokens, w * SEQ, (w + 1) * SEQ, axis=0).astype(F32)
        sq = jnp.zeros((SEQ,), F32)
        for piece in tokens_p:
            part = lax.slice_in_dim(piece, w * SEQ, (w + 1) * SEQ, axis=0).astype(F32)
            sq = sq + jnp.sum(part * part, axis=1)
        scale = lax.rsqrt(sq / D + EPS)[:, None]
        part = slice(w * rows, (w + 1) * rows)
        back = dot_l(onehot[w], jnp.concatenate([high[part], low[part]], axis=1))
        back = back[:, :share] + back[:, share:]
        inputs.append(
            (back + scale * (n1_own * own_gain - x_own * scale * (row_dot[:, None] / D))).astype(BF)
        )
    input_grad = jnp.concatenate(inputs, axis=0)

    gain_two = gain_two * (1.0 / lax.axis_size("mp"))
    gains_part = jnp.stack([gain_one[0], gain_two]).reshape(2, 4, share)
    chunk = jnp.arange(4, dtype=jnp.int32)
    natural = jnp.sum(
        jnp.where(
            ((chunk[:, None] ^ m) == chunk[None, :])[None, :, :, None], gains_part[:, None], 0.0
        ),
        axis=2,
    ).reshape(2, ndp, block)
    for axis in ("mp", "dp"):
        bit = 1
        while bit < lax.axis_size(axis):
            natural = natural + swap(natural, axis, bit)
            bit *= 2
    own_block = jnp.sum(jnp.where(device == me, owner, 0))
    gains_sum = jnp.sum(jnp.where((device == own_block)[None, :, None], natural, 0.0), axis=1)

    qkv_sum = jnp.moveaxis(qkv_sum.reshape(block, 3, share), 1, 0)
    gate_up_sum = jnp.stack([gate_sum, up_sum])
    qkv_out = adam_step(
        qkv_sum, qkv_master, qkv_first, qkv_second, qkv_average, D ** (-0.5), DECAY_RATE
    )
    proj_out = adam_step(
        proj_sum.T,
        proj_master,
        proj_first,
        proj_second,
        proj_average,
        (3.0 * D / SEQ) ** (-0.5),
        DECAY_RATE,
    )
    gate_up_out = adam_step(
        gate_up_sum,
        gate_up_master,
        gate_up_first,
        gate_up_second,
        gate_up_average,
        D ** (-0.5),
        DECAY_RATE,
    )
    down_out = adam_step(
        down_sum.T, down_master, down_first, down_second, down_average, FF ** (-0.5), DECAY_RATE
    )
    gains_out = adam_step(
        gains_sum, gains_master, gains_first, gains_second, gains_average, GAIN_RATE, 0.0
    )
    return (output, input_grad, *qkv_out, *proj_out, *gate_up_out, *down_out, *gains_out)


def solution(mesh, short=None):
    tokens = P("dp", "mp")
    cols = P(None, "dp", "mp")
    lines = P("mp", "dp")
    gains = P(None, "dp")
    in_specs = (tokens, tokens, P("dp", None), P("dp"), P(), P())
    in_specs += (cols,) * 4 + (lines,) * 4 + (cols,) * 4 + (lines,) * 4 + (gains,) * 4
    out_specs = (tokens, tokens)
    out_specs += (cols,) * 6 + (lines,) * 6 + (cols,) * 6 + (lines,) * 6 + (gains,) * 6
    return jax.shard_map(
        functools.partial(local, short=short),
        mesh=mesh,
        in_specs=in_specs,
        out_specs=out_specs,
        check_vma=False,
    )
```

time: 1140 us -> 471 us (0.41)
  waiting for transfers between devices: 638 us -> 114 us
  Pallas kernels: 0 us -> 123 us
  matrix products: 113 us -> 5.23 us
  other arithmetic: 125 us -> 46.7 us
  local copies, waits for them, and re-layouts: 166 us -> 88.8 us
  blocking collectives: 73.1 us -> 0 us
  starting transfers between devices: 0.94 us -> 73.1 us
    reduce_scatter x6 -> x0, waiting for transfers between devices: 380 us -> none  [the longest x1 150 us: local(): lax.psum_scatter(reorder(gate_up_grad, owner, dp_count), 'dp', scatter_di...]
    psum x2 -> x0, waiting for transfers between devices: 138 us -> none  [the longest x1 127 us: local(): attn_sum = lax.psum(attn_part, 'mp')]
    pallas_call x0 -> x23, Pallas kernels: none -> 123 us  [the longest x2 31.6 us: ffn_call(): pl.pallas_call(ffn_kernel, grid=(tiles,), in_specs=[cut((TILE, share), la...]
    ppermute x0 -> x68, waiting for transfers between devices: none -> 114 us  [swap(): return lax.ppermute(x, axis, [(i, i ^ bit) for i in range(n)])]
    dot_general x33 -> x3, matrix products: 113 us -> 5.23 us  [the longest x2 4.9 us: dot_l(): lax.dot_general(a, b, (((0,), (0,)), ((), ())), preferred_element_type=F32)]
    gather x34 -> x0, local copies, waits for them, and re-layouts: 100 us -> none  [the longest x17 50.6 us: reorder(): taken = jnp.take(shaped, block_order, axis=0).reshape(moved_axis.shape)]
    ppermute x0 -> x68, starting transfers between devices: none -> 73.1 us  [swap(): return lax.ppermute(x, axis, [(i, i ^ bit) for i in range(n)])]
    all_gather x4 -> x1, waiting for transfers between devices: 62.1 us -> 0.01 us  [local(): ffn_stack = lax.all_gather(ffn_block, 'dp', axis=0, tiled=False)]
  transfers between devices with their start and end apart: 13 -> 69, of which waited for: 10 -> 18; matrix products, arithmetic and copies ran while one was open for 23% -> 21% of each run, Pallas kernels for 0% -> 25%
where the time goes in v1:
time: 471 us; the launch traced here: 466 us
  Pallas kernels  123 us (26%)
  waiting for transfers between devices  114 us (24%)
  local copies, waits for them, and re-layouts  88.8 us (19%)
  starting transfers between devices  73.1 us (16%)
  other arithmetic  46.7 us (10%)
  between operations  15.9 us (3%)
  matrix products  5.23 us (1%)
    ppermute x68, waiting for transfers between devices, swap(): return lax.ppermute(x, axis, [(i, i ^ bit) for i in range(n)])  114 us
    unnamed x320, local copies, waits for them, and re-layouts  79 us
    ppermute x68, starting transfers between devices, swap(): return lax.ppermute(x, axis, [(i, i ^ bit) for i in range(n)])  73.1 us
    pallas_call x2, Pallas kernels, ffn_call(): pl.pallas_call(ffn_kernel, grid=(tiles,), in_specs=[cut((TILE, share), la...  31.6 us
    pallas_call x5, Pallas kernels, pack_keep(): pl.pallas_call(pack_add_kernel, grid_spec=pltpu.PrefetchScalarGridSpec(nu...  16.7 us
    pallas_call x2, Pallas kernels, attend_call(): pl.pallas_call(attend_kernel, grid=(SEQ // TILE,), in_specs=[cut((1, TILE...  16.3 us
    pallas_call x5, Pallas kernels, pack_send(): pl.pallas_call(pack_kernel, grid_spec=pltpu.PrefetchScalarGridSpec(num_sc...  14.9 us
    pallas_call x2, Pallas kernels, qkv_call(): pl.pallas_call(qkv_kernel, grid=(tiles,), in_specs=[cut((TILE, share), la...  12 us
  transfers between devices with their start and end apart: 69, of which 18 were waited for; matrix products, arithmetic and copies ran while one was open for 21% of the time, Pallas kernels for 25%

profile of v1, /device:TPU:0, one launch (start us, length us, event | category | flops | bytes accessed | tf_op | source)
XLA Modules:
  0.0 466.4 jit_solution(465078699365036867)
XLA Ops:
  10.8 3.1 collective-permute-start.7
  13.9 2.6 collective-permute-start.9
  23.6 3.3 fusion.26
  29.0 11.0 %collective-permute-done.4 = bf16[2,2,128]{2,1,0:T(2,128)(2,1)S(1)} collective-permute-done((bf16[2,2,128]{2,1,0:T(2,128)(2,1)S(1)}, bf16[2,2,128]{2,1,0:T(2,128)(2,1)S(1)}, u32[]{:S(2)}, u32[]{:S(2)}) %collective-permute-start.4) | collective-permute-done | bytes 1056 | tf_op jit(solution)/shard_map/ppermute | solution.py:52
  40.0 2.4 collective-permute-start.5
  42.8 13.4 %collective-permute-done.5 = bf16[2,4,128]{2,1,0:T(4,128)(2,1)S(1)} collective-permute-done((bf16[2,4,128]{2,1,0:T(4,128)(2,1)S(1)}, bf16[2,4,128]{2,1,0:T(4,128)(2,1)S(1)}, u32[]{:S(2)}, u32[]{:S(2)}) %collective-permute-start.5) | collective-permute-done | bytes 2080 | tf_op jit(solution)/shard_map/ppermute | solution.py:52
  83.8 3.3 pad_maximum_fusion.8
  100.5 10.3 %collective-permute-done.17.o2 = bf16[1024,256]{1,0:T(8,128)(2,1)S(1)} collective-permute-done((bf16[1024,256]{1,0:T(8,128)(2,1)S(1)}, bf16[1024,256]{1,0:T(8,128)(2,1)S(1)}, u32[]{:S(2)}, u32[]{:S(2)}) %collective-permute-start.17) | collective-permute-done | bytes 524320 | tf_op jit(solution)/shard_map/ppermute | solution.py:52
  113.0 6.1 %shard_map.502 = (bf16[3,1024,256]{2,1,0:T(8,128)(2,1)S(1)}, bf16[1024,1024]{1,0:T(8,128)(2,1)S(1)}, bf16[160,1024]{1,0:T(8,128)(2,1)S(1)}, bf16[160,256]{1,0:T(8,128)(2,1)S(1)}) custom-call(bf16[2048,256]{1,0:T(8,128)(2,1)S(1)} %copy-done, bf16[2048,256]{1,0:T(8,128)(2,1)S(1)} %collective-permute-done.x1, bf16[2048,256]{1,0:T(8,128)(2,1)} %collective-permute-done.1.x2, ...), custom_call_target="tpu_custom_call" | custom-call | flops 1610612736 | bytes 8388608 | tf_op jit(solution)/shard_map/pallas_call | solution.py:168
  119.7 8.0 %shard_map.503 = (bf16[1024,256]{1,0:T(8,128)(2,1)}, bf16[160,256]{1,0:T(8,128)(2,1)S(1)}) custom-call(bf16[3,1024,256]{2,1,0:T(8,128)(2,1)S(1)} %get-tuple-element.95.q_ref.k_ref.v_ref, bf16[3,1024,256]{2,1,0:T(8,128)(2,1)S(1)} %get-tuple-element.95.q_ref.k_ref.v_ref, bf16[3,1024,256]{2,1,0:T(8,128)(2,1)S(1)} %get-tuple-element.95.q_ref.k_ref.v_ref, ...), custom_call_target="tpu_custom_call" | custom-call | flops 4294967296 | bytes 3145728 | tf_op jit(solution)/shard_map/pallas_call | solution.py:234
  128.4 5.9 %shard_map.498 = (bf16[3,1024,256]{2,1,0:T(8,128)(2,1)S(1)}, bf16[1024,1024]{1,0:T(8,128)(2,1)S(1)}, bf16[160,1024]{1,0:T(8,128)(2,1)S(1)}, bf16[160,256]{1,0:T(8,128)(2,1)S(1)}) custom-call(bf16[2048,256]{1,0:T(8,128)(2,1)S(1)} %copy-done, bf16[2048,256]{1,0:T(8,128)(2,1)S(1)} %collective-permute-done.x1, bf16[2048,256]{1,0:T(8,128)(2,1)} %collective-permute-done.1.x2, ...), custom_call_target="tpu_custom_call" | custom-call | flops 1610612736 | bytes 8388608 | tf_op jit(solution)/shard_map/pallas_call | solution.py:168
  134.3 8.3 %shard_map.499 = (bf16[1024,256]{1,0:T(8,128)(2,1)}, bf16[160,256]{1,0:T(8,128)(2,1)S(1)}) custom-call(bf16[3,1024,256]{2,1,0:T(8,128)(2,1)S(1)} %get-tuple-element.90.q_ref.k_ref.v_ref, bf16[3,1024,256]{2,1,0:T(8,128)(2,1)S(1)} %get-tuple-element.90.q_ref.k_ref.v_ref, bf16[3,1024,256]{2,1,0:T(8,128)(2,1)S(1)} %get-tuple-element.90.q_ref.k_ref.v_ref, ...), custom_call_target="tpu_custom_call" | custom-call | flops 4294967296 | bytes 3145728 | tf_op jit(solution)/shard_map/pallas_call | solution.py:234
  147.1 13.2 %collective-permute-done.30.c2 = bf16[320,256]{1,0:T(8,128)(2,1)} collective-permute-done((bf16[320,256]{1,0:T(8,128)(2,1)}, bf16[320,256]{1,0:T(8,128)(2,1)}, u32[]{:S(2)}, u32[]{:S(2)}) %collective-permute-start.30) | collective-permute-done | bytes 163872 | tf_op jit(solution)/shard_map/ppermute | solution.py:52
  164.0 2.8 copy-done.24
  168.4 2.7 copy-done.25
  171.6 10.3 %shard_map.505 = (bf16[320,1024]{1,0:T(8,128)(2,1)S(1)}, bf16[320,1024]{1,0:T(8,128)(2,1)S(1)}, bf16[320,1024]{1,0:T(8,128)(2,1)S(1)}, bf16[320,1024]{1,0:T(8,12...) custom-call(bf16[320,1024]{1,0:T(8,128)(2,1)S(1)} %copy-done.64, ...), custom_call_target="tpu_custom_call" | custom-call | flops 4026531840 | bytes 12582912 | tf_op jit(solution)/shard_map/pallas_call | solution.py:362
  182.2 16.2 %shard_map.504 = (bf16[1024,512]{1,0:T(8,128)(2,1)}, bf16[1024,512]{1,0:T(8,128)(2,1)S(1)}, f32[1024,256]{1,0:T(8,128)S(1)}) custom-call(bf16[2048,256]{1,0:T(8,128)(2,1)S(1)} %copy-done, bf16[2048,256]{1,0:T(8,128)(2,1)S(1)} %copy-done.4, bf16[2048,256]{1,0:T(8,128)(2,1)} %collective-permute-done.1.x2, bf16[2048,256]{1,0:T(8,128)(2,1)S(1)} %copy-done.7, ...), custom_call_target="tpu_custom_call" | custom-call | flops 8589934592 | bytes 16777216 | tf_op jit(solution)/shard_map/pallas_call | solution.py:295
  202.0 15.4 %shard_map.501 = (bf16[1024,512]{1,0:T(8,128)(2,1)}, bf16[1024,512]{1,0:T(8,128)(2,1)S(1)}, f32[1024,256]{1,0:T(8,128)S(1)}) custom-call(bf16[2048,256]{1,0:T(8,128)(2,1)S(1)} %copy-done, bf16[2048,256]{1,0:T(8,128)(2,1)S(1)} %copy-done.4, bf16[2048,256]{1,0:T(8,128)(2,1)} %collective-permute-done.1.x2, bf16[2048,256]{1,0:T(8,128)(2,1)S(1)} %copy-done.7, ...), custom_call_target="tpu_custom_call" | custom-call | flops 8589934592 | bytes 16777216 | tf_op jit(solution)/shard_map/pallas_call | solution.py:295
  219.7 3.1 shard_map.513
  222.9 2.6 shard_map.514
  231.9 4.5 shard_map.506.d_ref
  236.3 5.1 %shard_map.507 = (bf16[1024,512]{1,0:T(8,128)(2,1)}, bf16[1024,512]{1,0:T(8,128)(2,1)S(1)}, f32[1024,1]{1,0:T(8,128)S(1)}, f32[1,1024]{1,0:T(1,128)S(1)}) custom-call(bf16[1024,768]{1,0:T(8,128)(2,1)S(1)} %shard_map.506.d_ref, bf16[4,1024,256]{2,1,0:T(8,128)(2,1)S(1)} %shard_map.497.w_ref, bf16[2048,256]{1,0:T(8,128)(2,1)S(1)} %copy-done, ...), custom_call_target="tpu_custom_call" | custom-call | flops 1610612736 | bytes 8388608 | tf_op jit(solution)/shard_map/pallas_call | solution.py:547
  252.0 4.5 shard_map.508.d_ref
  259.0 5.0 %shard_map.509 = (bf16[1024,512]{1,0:T(8,128)(2,1)}, bf16[1024,512]{1,0:T(8,128)(2,1)S(1)}, f32[1024,1]{1,0:T(8,128)S(1)}, f32[1,1024]{1,0:T(1,128)S(1)}) custom-call(bf16[1024,768]{1,0:T(8,128)(2,1)S(1)} %shard_map.508.d_ref, bf16[4,1024,256]{2,1,0:T(8,128)(2,1)S(1)} %shard_map.497.w_ref, bf16[2048,256]{1,0:T(8,128)(2,1)S(1)} %copy-done, ...), custom_call_target="tpu_custom_call" | custom-call | flops 1610612736 | bytes 8388608 | tf_op jit(solution)/shard_map/pallas_call | solution.py:547
  267.9 3.0 fusion.21
  275.5 4.5 shard_map.510
  283.1 2.6 shard_map.511
  290.5 3.3 collective-permute-start.67
  296.7 2.9 convert_add_fusion.2
  301.9 8.3 %collective-permute-done.43.recv_ref = bf16[4,128,1024]{2,1,0:T(8,128)(2,1)S(1)} collective-permute-done((bf16[4,128,1024]{2,1,0:T(8,128)(2,1)S(1)}, bf16[4,128,1024]{2,1,0:T(8,128)(2,1)S(1)}, u32[]{:S(2)}, u32[]{:S(2)}) %collective-permute-start.43) | collective-permute-done | bytes 1048608 | tf_op jit(solution)/shard_map/ppermute | solution.py:52
  310.2 2.2 shard_map.519
  312.4 4.8 %collective-permute-start.62 = (bf16[128,1024]{1,0:T(8,128)(2,1)S(1)}, bf16[128,1024]{1,0:T(8,128)(2,1)S(1)}, u32[]{:S(2)}, u32[]{:S(2)}) collective-permute-start(bf16[128,1024]{1,0:T(8,128)(2,1)S(1)} %get-tuple-element.145), channel_id=1, source_target_pairs={{0,24},{4,28},{8,16},{12,20},{16,8},{20,12},{24,0},{28,4},{1,25},{... | collective-permute-start | bytes 786440 | tf_op jit(solution)/shard_map/ppermute | solution.py:52
  320.6 4.0 collective-permute-done.62
  325.1 12.2 %collective-permute-done.61 = bf16[128,1024]{1,0:T(8,128)(2,1)S(1)} collective-permute-done((bf16[128,1024]{1,0:T(8,128)(2,1)S(1)}, bf16[128,1024]{1,0:T(8,128)(2,1)S(1)}, u32[]{:S(2)}, u32[]{:S(2)}) %collective-permute-start.61) | collective-permute-done | bytes 262176 | tf_op jit(solution)/shard_map/ppermute | solution.py:52
  353.6 7.8 %collective-permute-done.44.recv_ref = bf16[4,128,1024]{2,1,0:T(8,128)(2,1)} collective-permute-done((bf16[4,128,1024]{2,1,0:T(8,128)(2,1)}, bf16[4,128,1024]{2,1,0:T(8,128)(2,1)}, u32[]{:S(2)}, u32[]{:S(2)}) %collective-permute-start.44) | collective-permute-done | bytes 1048608 | tf_op jit(solution)/shard_map/ppermute | solution.py:52
  365.3 3.7 shard_map.517
  370.3 3.2 collective-permute-start.54
  375.1 5.0 %collective-permute-done.56 = bf16[128,1024]{1,0:T(8,128)(2,1)S(1)} collective-permute-done((bf16[128,1024]{1,0:T(8,128)(2,1)S(1)}, bf16[128,1024]{1,0:T(8,128)(2,1)S(1)}, u32[]{:S(2)}, u32[]{:S(2)}) %collective-permute-start.56) | collective-permute-done | bytes 262176 | tf_op jit(solution)/shard_map/ppermute | solution.py:52
  381.6 7.0 %collective-permute-done.55 = bf16[128,1024]{1,0:T(8,128)(2,1)S(1)} collective-permute-done((bf16[128,1024]{1,0:T(8,128)(2,1)S(1)}, bf16[128,1024]{1,0:T(8,128)(2,1)S(1)}, u32[]{:S(2)}, u32[]{:S(2)}) %collective-permute-start.55) | collective-permute-done | bytes 262176 | tf_op jit(solution)/shard_map/ppermute | solution.py:52
  390.4 2.2 shard_map.518
  392.7 2.3 collective-permute-start.59
  399.9 2.8 shard_map.516
  402.7 2.3 collective-permute-start.53
  405.1 9.1 %collective-permute-start.52 = (bf16[128,256]{1,0:T(8,128)(2,1)S(1)}, bf16[128,256]{1,0:T(8,128)(2,1)S(1)}, u32[]{:S(2)}, u32[]{:S(2)}) collective-permute-start(bf16[128,256]{1,0:T(8,128)(2,1)S(1)} %get-tuple-element.132), channel_id=1, source_target_pairs={{0,16},{4,20},{8,24},{12,28},{16,0},{20,4},{24,8},{28,12},{1,17},{... | collective-permute-start | bytes 196616 | tf_op jit(solution)/shard_map/ppermute | solution.py:52
  414.1 4.9 %collective-permute-done.58 = bf16[128,1024]{1,0:T(8,128)(2,1)S(1)} collective-permute-done((bf16[128,1024]{1,0:T(8,128)(2,1)S(1)}, bf16[128,1024]{1,0:T(8,128)(2,1)S(1)}, u32[]{:S(2)}, u32[]{:S(2)}) %collective-permute-start.58) | collective-permute-done | bytes 262176 | tf_op jit(solution)/shard_map/ppermute | solution.py:52
  419.2 2.2 fusion.47
  431.1 5.7 %shard_map.515 = (f32[128,768]{1,0:T(8,128)S(1)}, bf16[128,768]{1,0:T(8,128)(2,1)}, bf16[128,768]{1,0:T(8,128)(2,1)}, bf16[128,768]{1,0:T(8,128)(2,1)}) custom-call(s32[4]{0:T(128)S(1)} %slice.200.pos_ref, bf16[2048,1024]{1,0:T(8,128)(2,1)S(1)} %copy-done.11, bf16[2048,768]{1,0:T(8,128)(2,1)S(1)} %copy-done.2, ...), custom_call_target="tpu_custom_call" | custom-call | flops 1610612736 | bytes 3145728 | tf_op jit(solution)/shard_map/pallas_call | solution.py:437
  445.8 7.4 %collective-permute-done.49 = bf16[128,768]{1,0:T(8,128)(2,1)S(1)} collective-permute-done((bf16[128,768]{1,0:T(8,128)(2,1)}, bf16[128,768]{1,0:T(8,128)(2,1)S(1)}, u32[]{:S(2)}, u32[]{:S(2)}) %collective-permute-start.49) | collective-permute-done | bytes 196640 | tf_op jit(solution)/shard_map/ppermute | solution.py:52
  (548 shorter events, 173.9 us)
Async XLA Ops:
  7.2 156.7 %all-gather.3.cloned.1.call-start = ((), (), s32[]{:S(2)}) async-start(), calls=%async_computation | async-start | bytes 7077888 | tf_op jit(solution)/shard_map/all_gather | solution.py:649
  10.8 47.9 %collective-permute-start.7 = (bf16[4,128,256]{2,1,0:T(8,128)(2,1)S(1)}, bf16[4,128,256]{2,1,0:T(8,128)(2,1)S(1)}, u32[]{:S(2)}, u32[]{:S(2)}) collective-permute-start(bf16[4,128,256]{2,1,0:T(8,128)(2,1)S(1)} %pad_maximum_fusion.10.refs_0_), channel_id=1, source_target_pairs={{0,8},{4,12},{8,0},{12,4},{16,24},{20,28},{24,16},{28,20},{1,9},{5... | collective-permute-start | bytes 786440 | tf_op jit(solution)/shard_map/ppermute | solution.py:52
  13.9 45.3 %collective-permute-start.9 = (bf16[4,128,256]{2,1,0:T(8,128)(2,1)S(1)}, bf16[4,128,256]{2,1,0:T(8,128)(2,1)S(1)}, u32[]{:S(2)}, u32[]{:S(2)}) collective-permute-start(bf16[4,128,256]{2,1,0:T(8,128)(2,1)S(1)} %pad_maximum_fusion.10.refs_0_), channel_id=1, source_target_pairs={{0,16},{4,20},{8,24},{12,28},{16,0},{20,4},{24,8},{28,12},{1,17},{... | collective-permute-start | bytes 786440 | tf_op jit(solution)/shard_map/ppermute | solution.py:52
  16.5 44.2 %collective-permute-start.11 = (bf16[4,128,256]{2,1,0:T(8,128)(2,1)S(1)}, bf16[4,128,256]{2,1,0:T(8,128)(2,1)S(1)}, u32[]{:S(2)}, u32[]{:S(2)}) collective-permute-start(bf16[4,128,256]{2,1,0:T(8,128)(2,1)S(1)} %pad_maximum_fusion.10.refs_0_), channel_id=1, source_target_pairs={{0,24},{4,28},{8,16},{12,20},{16,8},{20,12},{24,0},{28,4},{1,25},{... | collective-permute-start | bytes 786440 | tf_op jit(solution)/shard_map/ppermute | solution.py:52
  16.5 79.7 %collective-permute-start.1 = (bf16[2048,256]{1,0:T(8,128)(2,1)S(1)}, bf16[2048,256]{1,0:T(8,128)(2,1)}, u32[]{:S(2)}, u32[]{:S(2)}) collective-permute-start(bf16[2048,256]{1,0:T(8,128)(2,1)S(1)} %copy-done), channel_id=1, source_target_pairs={{0,2},{1,3},{2,0},{3,1},{4,6},{5,7},{6,4},{7,5},{8,10},{9,11},{10,... | collective-permute-start | bytes 3145736 | tf_op jit(solution)/shard_map/ppermute | solution.py:52
  40.0 16.2 %collective-permute-start.5 = (bf16[2,4,128]{2,1,0:T(4,128)(2,1)S(1)}, bf16[2,4,128]{2,1,0:T(4,128)(2,1)S(1)}, u32[]{:S(2)}, u32[]{:S(2)}) collective-permute-start(bf16[2,4,128]{2,1,0:T(4,128)(2,1)S(1)} %pad_maximum_fusion.13), channel_id=1, source_target_pairs={{0,16},{4,20},{8,24},{12,28},{16,0},{20,4},{24,8},{28,12},{1,17},{... | collective-permute-start | bytes 6152 | tf_op jit(solution)/shard_map/ppermute | solution.py:52
  56.2 30.9 %collective-permute-start.6 = (bf16[4,128,256]{2,1,0:T(8,128)(2,1)S(1)}, bf16[4,128,256]{2,1,0:T(8,128)(2,1)S(1)}, u32[]{:S(2)}, u32[]{:S(2)}) collective-permute-start(bf16[4,128,256]{2,1,0:T(8,128)(2,1)S(1)} %pad_maximum_fusion.10.refs_0_), channel_id=1, source_target_pairs={{0,4},{4,0},{8,12},{12,8},{16,20},{20,16},{24,28},{28,24},{1,5},{5... | collective-permute-start | bytes 786440 | tf_op jit(solution)/shard_map/ppermute | solution.py:52
  58.7 29.2 %collective-permute-start.8 = (bf16[4,128,256]{2,1,0:T(8,128)(2,1)S(1)}, bf16[4,128,256]{2,1,0:T(8,128)(2,1)S(1)}, u32[]{:S(2)}, u32[]{:S(2)}) collective-permute-start(bf16[4,128,256]{2,1,0:T(8,128)(2,1)S(1)} %collective-permute-done.7.refs_2_), channel_id=1, source_target_pairs={{0,4},{4,0},{8,12},{12,8},{16,20},{20,16},{24,28},{28,24},{1,5},{5... | collective-permute-start | bytes 786440 | tf_op jit(solution)/shard_map/ppermute | solution.py:52
  59.3 30.9 %collective-permute-start.10 = (bf16[4,128,256]{2,1,0:T(8,128)(2,1)S(1)}, bf16[4,128,256]{2,1,0:T(8,128)(2,1)S(1)}, u32[]{:S(2)}, u32[]{:S(2)}) collective-permute-start(bf16[4,128,256]{2,1,0:T(8,128)(2,1)S(1)} %collective-permute-done.9.refs_4_), channel_id=1, source_target_pairs={{0,4},{4,0},{8,12},{12,8},{16,20},{20,16},{24,28},{28,24},{1,5},{5... | collective-permute-start | bytes 786440 | tf_op jit(solution)/shard_map/ppermute | solution.py:52
  60.7 30.3 %collective-permute-start.12 = (bf16[4,128,256]{2,1,0:T(8,128)(2,1)S(1)}, bf16[4,128,256]{2,1,0:T(8,128)(2,1)S(1)}, u32[]{:S(2)}, u32[]{:S(2)}) collective-permute-start(bf16[4,128,256]{2,1,0:T(8,128)(2,1)S(1)} %collective-permute-done.11.refs_6_), channel_id=1, source_target_pairs={{0,4},{4,0},{8,12},{12,8},{16,20},{20,16},{24,28},{28,24},{1,5},{5... | collective-permute-start | bytes 786440 | tf_op jit(solution)/shard_map/ppermute | solution.py:52
  87.9 24.7 %collective-permute-start = (bf16[2048,256]{1,0:T(8,128)(2,1)S(1)}, bf16[2048,256]{1,0:T(8,128)(2,1)S(1)}, u32[]{:S(2)}, u32[]{:S(2)}) collective-permute-start(bf16[2048,256]{1,0:T(8,128)(2,1)S(1)} %copy-done), channel_id=1, source_target_pairs={{0,1},{1,0},{2,3},{3,2},{4,5},{5,4},{6,7},{7,6},{8,9},{9,8},{10,11... | collective-permute-start | bytes 3145736 | tf_op jit(solution)/shard_map/ppermute | solution.py:52
  96.3 16.7 %collective-permute-start.2 = (bf16[2048,256]{1,0:T(8,128)(2,1)}, bf16[2048,256]{1,0:T(8,128)(2,1)S(1)}, u32[]{:S(2)}, u32[]{:S(2)}) collective-permute-start(bf16[2048,256]{1,0:T(8,128)(2,1)} %collective-permute-done.1.x2), channel_id=1, source_target_pairs={{0,1},{1,0},{2,3},{3,2},{4,5},{5,4},{6,7},{7,6},{8,9},{9,8},{10,11... | collective-permute-start | bytes 3145736 | tf_op jit(solution)/shard_map/ppermute | solution.py:52
  96.7 14.1 %collective-permute-start.17 = (bf16[1024,256]{1,0:T(8,128)(2,1)S(1)}, bf16[1024,256]{1,0:T(8,128)(2,1)S(1)}, u32[]{:S(2)}, u32[]{:S(2)}) collective-permute-start(bf16[1024,256]{1,0:T(8,128)(2,1)S(1)} %slice_bitcast_fusion.4.o0), channel_id=1, source_target_pairs={{0,2},{1,3},{2,0},{3,1},{4,6},{5,7},{6,4},{7,5},{8,10},{9,11},{10,... | collective-permute-start | bytes 1572872 | tf_op jit(solution)/shard_map/ppermute | solution.py:52
  100.3 46.3 %collective-permute-start.16 = (bf16[1024,256]{1,0:T(8,128)(2,1)S(1)}, bf16[1024,256]{1,0:T(8,128)(2,1)S(1)}, u32[]{:S(2)}, u32[]{:S(2)}) collective-permute-start(bf16[1024,256]{1,0:T(8,128)(2,1)S(1)} %slice_bitcast_fusion.4.o0), channel_id=1, source_target_pairs={{0,1},{1,0},{2,3},{3,2},{4,5},{5,4},{6,7},{7,6},{8,9},{9,8},{10,11... | collective-permute-start | bytes 1572872 | tf_op jit(solution)/shard_map/ppermute | solution.py:52
  110.8 35.8 %collective-permute-start.18 = (bf16[1024,256]{1,0:T(8,128)(2,1)S(1)}, bf16[1024,256]{1,0:T(8,128)(2,1)S(1)}, u32[]{:S(2)}, u32[]{:S(2)}) collective-permute-start(bf16[1024,256]{1,0:T(8,128)(2,1)S(1)} %collective-permute-done.17.o2), channel_id=1, source_target_pairs={{0,1},{1,0},{2,3},{3,2},{4,5},{5,4},{6,7},{7,6},{8,9},{9,8},{10,11... | collective-permute-start | bytes 1572872 | tf_op jit(solution)/shard_map/ppermute | solution.py:52
  127.8 32.6 %collective-permute-start.22 = (bf16[1024,256]{1,0:T(8,128)(2,1)}, bf16[1024,256]{1,0:T(8,128)(2,1)}, u32[]{:S(2)}, u32[]{:S(2)}) collective-permute-start(bf16[1024,256]{1,0:T(8,128)(2,1)} %get-tuple-element.96.c0), channel_id=1, source_target_pairs={{0,2},{1,3},{2,0},{3,1},{4,6},{5,7},{6,4},{7,5},{8,10},{9,11},{10,... | collective-permute-start | bytes 1572872 | tf_op jit(solution)/shard_map/ppermute | solution.py:52
  142.6 28.5 %collective-permute-start.14 = (bf16[1024,256]{1,0:T(8,128)(2,1)}, bf16[1024,256]{1,0:T(8,128)(2,1)}, u32[]{:S(2)}, u32[]{:S(2)}) collective-permute-start(bf16[1024,256]{1,0:T(8,128)(2,1)} %get-tuple-element.91.c0), channel_id=1, source_target_pairs={{0,2},{1,3},{2,0},{3,1},{4,6},{5,7},{6,4},{7,5},{8,10},{9,11},{10,... | collective-permute-start | bytes 1572872 | tf_op jit(solution)/shard_map/ppermute | solution.py:52
  145.4 14.9 %collective-permute-start.30 = (bf16[320,256]{1,0:T(8,128)(2,1)}, bf16[320,256]{1,0:T(8,128)(2,1)}, u32[]{:S(2)}, u32[]{:S(2)}) collective-permute-start(bf16[320,256]{1,0:T(8,128)(2,1)} %constant_dynamic-update-slice_fusion.c0.rhs_ref), channel_id=1, source_target_pairs={{0,2},{1,3},{2,0},{3,1},{4,6},{5,7},{6,4},{7,5},{8,10},{9,11},{10,... | collective-permute-start | bytes 491528 | tf_op jit(solution)/shard_map/ppermute | solution.py:52
  146.5 35.6 %collective-permute-start.21 = (bf16[1024,256]{1,0:T(8,128)(2,1)}, bf16[1024,256]{1,0:T(8,128)(2,1)}, u32[]{:S(2)}, u32[]{:S(2)}) collective-permute-start(bf16[1024,256]{1,0:T(8,128)(2,1)} %get-tuple-element.96.c0), channel_id=1, source_target_pairs={{0,1},{1,0},{2,3},{3,2},{4,5},{5,4},{6,7},{7,6},{8,9},{9,8},{10,11... | collective-permute-start | bytes 1572872 | tf_op jit(solution)/shard_map/ppermute | solution.py:52
  146.6 24.4 %collective-permute-start.29 = (bf16[320,256]{1,0:T(8,128)(2,1)}, bf16[320,256]{1,0:T(8,128)(2,1)}, u32[]{:S(2)}, u32[]{:S(2)}) collective-permute-start(bf16[320,256]{1,0:T(8,128)(2,1)} %constant_dynamic-update-slice_fusion.c0.rhs_ref), channel_id=1, source_target_pairs={{0,1},{1,0},{2,3},{3,2},{4,5},{5,4},{6,7},{7,6},{8,9},{9,8},{10,11... | collective-permute-start | bytes 491528 | tf_op jit(solution)/shard_map/ppermute | solution.py:52
  160.3 21.9 %collective-permute-start.23 = (bf16[1024,256]{1,0:T(8,128)(2,1)}, bf16[1024,256]{1,0:T(8,128)(2,1)}, u32[]{:S(2)}, u32[]{:S(2)}) collective-permute-start(bf16[1024,256]{1,0:T(8,128)(2,1)} %collective-permute-done.22.c2), channel_id=1, source_target_pairs={{0,1},{1,0},{2,3},{3,2},{4,5},{5,4},{6,7},{7,6},{8,9},{9,8},{10,11... | collective-permute-start | bytes 1572872 | tf_op jit(solution)/shard_map/ppermute | solution.py:52
  171.1 30.9 %collective-permute-start.13 = (bf16[1024,256]{1,0:T(8,128)(2,1)}, bf16[1024,256]{1,0:T(8,128)(2,1)S(1)}, u32[]{:S(2)}, u32[]{:S(2)}) collective-permute-start(bf16[1024,256]{1,0:T(8,128)(2,1)} %get-tuple-element.91.c0), channel_id=1, source_target_pairs={{0,1},{1,0},{2,3},{3,2},{4,5},{5,4},{6,7},{7,6},{8,9},{9,8},{10,11... | collective-permute-start | bytes 1572872 | tf_op jit(solution)/shard_map/ppermute | solution.py:52
  171.1 30.9 %collective-permute-start.15 = (bf16[1024,256]{1,0:T(8,128)(2,1)}, bf16[1024,256]{1,0:T(8,128)(2,1)S(1)}, u32[]{:S(2)}, u32[]{:S(2)}) collective-permute-start(bf16[1024,256]{1,0:T(8,128)(2,1)} %collective-permute-done.14.c2), channel_id=1, source_target_pairs={{0,1},{1,0},{2,3},{3,2},{4,5},{5,4},{6,7},{7,6},{8,9},{9,8},{10,11... | collective-permute-start | bytes 1572872 | tf_op jit(solution)/shard_map/ppermute | solution.py:52
  182.0 18.3 %collective-permute-start.32 = (bf16[320,512]{1,0:T(8,128)(2,1)S(1)}, bf16[320,512]{1,0:T(8,128)(2,1)S(1)}, u32[]{:S(2)}, u32[]{:S(2)}) collective-permute-start(bf16[320,512]{1,0:T(8,128)(2,1)S(1)} %get-tuple-element.106), channel_id=1, source_target_pairs={{0,1},{1,0},{2,3},{3,2},{4,5},{5,4},{6,7},{7,6},{8,9},{9,8},{10,11... | collective-permute-start | bytes 983048 | tf_op jit(solution)/shard_map/ppermute | solution.py:52
  200.3 96.4 %collective-permute-start.24 = (bf16[1024,512]{1,0:T(8,128)(2,1)}, bf16[1024,512]{1,0:T(8,128)(2,1)}, u32[]{:S(2)}, u32[]{:S(2)}) collective-permute-start(bf16[1024,512]{1,0:T(8,128)(2,1)} %get-tuple-element.99), channel_id=1, source_target_pairs={{0,1},{1,0},{2,3},{3,2},{4,5},{5,4},{6,7},{7,6},{8,9},{9,8},{10,11... | collective-permute-start | bytes 3145736 | tf_op jit(solution)/shard_map/ppermute | solution.py:52
  200.4 25.0 %collective-permute-start.33 = (bf16[320,512]{1,0:T(8,128)(2,1)S(1)}, bf16[320,512]{1,0:T(8,128)(2,1)S(1)}, u32[]{:S(2)}, u32[]{:S(2)}) collective-permute-start(bf16[320,512]{1,0:T(8,128)(2,1)S(1)} %fusion.22), channel_id=1, source_target_pairs={{0,2},{1,3},{2,0},{3,1},{4,6},{5,7},{6,4},{7,5},{8,10},{9,11},{10,... | collective-permute-start | bytes 983048 | tf_op jit(solution)/shard_map/ppermute | solution.py:52
  217.4 99.9 %collective-permute-start.19 = (bf16[1024,512]{1,0:T(8,128)(2,1)}, bf16[1024,512]{1,0:T(8,128)(2,1)}, u32[]{:S(2)}, u32[]{:S(2)}) collective-permute-start(bf16[1024,512]{1,0:T(8,128)(2,1)} %get-tuple-element.94), channel_id=1, source_target_pairs={{0,1},{1,0},{2,3},{3,2},{4,5},{5,4},{6,7},{7,6},{8,9},{9,8},{10,11... | collective-permute-start | bytes 3145736 | tf_op jit(solution)/shard_map/ppermute | solution.py:52
  244.4 37.2 %collective-permute-start.37 = (f32[1024]{0:T(1024)S(1)}, f32[1024]{0:T(1024)S(1)}, u32[]{:S(2)}, u32[]{:S(2)}) collective-permute-start(f32[1024]{0:T(1024)S(1)} %reduce.1), channel_id=1, source_target_pairs={{0,1},{1,0},{2,3},{3,2},{4,5},{5,4},{6,7},{7,6},{8,9},{9,8},{10,11... | collective-permute-start | bytes 12296 | tf_op jit(solution)/shard_map/ppermute | solution.py:52
  267.1 18.6 %collective-permute-start.41 = (f32[1024]{0:T(1024)S(1)}, f32[1024]{0:T(1024)S(1)}, u32[]{:S(2)}, u32[]{:S(2)}) collective-permute-start(f32[1024]{0:T(1024)S(1)} %reduce.2), channel_id=1, source_target_pairs={{0,1},{1,0},{2,3},{3,2},{4,5},{5,4},{6,7},{7,6},{8,9},{9,8},{10,11... | collective-permute-start | bytes 12296 | tf_op jit(solution)/shard_map/ppermute | solution.py:52
  285.7 24.5 %collective-permute-start.43 = (bf16[4,128,1024]{2,1,0:T(8,128)(2,1)S(1)}, bf16[4,128,1024]{2,1,0:T(8,128)(2,1)S(1)}, u32[]{:S(2)}, u32[]{:S(2)}) collective-permute-start(bf16[4,128,1024]{2,1,0:T(8,128)(2,1)S(1)} %copy-done.51), channel_id=1, source_target_pairs={{0,4},{4,0},{8,12},{12,8},{16,20},{20,16},{24,28},{28,24},{1,5},{5... | collective-permute-start | bytes 3145736 | tf_op jit(solution)/shard_map/ppermute | solution.py:52
  290.5 71.4 %collective-permute-start.35 = (bf16[1024,512]{1,0:T(8,128)(2,1)}, bf16[1024,512]{1,0:T(8,128)(2,1)}, u32[]{:S(2)}, u32[]{:S(2)}) collective-permute-start(bf16[1024,512]{1,0:T(8,128)(2,1)} %get-tuple-element.110), channel_id=1, source_target_pairs={{0,1},{1,0},{2,3},{3,2},{4,5},{5,4},{6,7},{7,6},{8,9},{9,8},{10,11... | collective-permute-start | bytes 3145736 | tf_op jit(solution)/shard_map/ppermute | solution.py:52
  295.5 74.8 %collective-permute-start.39 = (bf16[1024,512]{1,0:T(8,128)(2,1)}, bf16[1024,512]{1,0:T(8,128)(2,1)}, u32[]{:S(2)}, u32[]{:S(2)}) collective-permute-start(bf16[1024,512]{1,0:T(8,128)(2,1)} %get-tuple-element.114), channel_id=1, source_target_pairs={{0,1},{1,0},{2,3},{3,2},{4,5},{5,4},{6,7},{7,6},{8,9},{9,8},{10,11... | collective-permute-start | bytes 3145736 | tf_op jit(solution)/shard_map/ppermute | solution.py:52
  317.3 20.1 %collective-permute-start.61 = (bf16[128,1024]{1,0:T(8,128)(2,1)S(1)}, bf16[128,1024]{1,0:T(8,128)(2,1)S(1)}, u32[]{:S(2)}, u32[]{:S(2)}) collective-permute-start(bf16[128,1024]{1,0:T(8,128)(2,1)S(1)} %get-tuple-element.144), channel_id=1, source_target_pairs={{0,16},{4,20},{8,24},{12,28},{16,0},{20,4},{24,8},{28,12},{1,17},{... | collective-permute-start | bytes 786440 | tf_op jit(solution)/shard_map/ppermute | solution.py:52
  317.3 20.6 %collective-permute-start.60 = (bf16[128,1024]{1,0:T(8,128)(2,1)S(1)}, bf16[128,1024]{1,0:T(8,128)(2,1)S(1)}, u32[]{:S(2)}, u32[]{:S(2)}) collective-permute-start(bf16[128,1024]{1,0:T(8,128)(2,1)S(1)} %get-tuple-element.143), channel_id=1, source_target_pairs={{0,8},{4,12},{8,0},{12,4},{16,24},{20,28},{24,16},{28,20},{1,9},{5... | collective-permute-start | bytes 786440 | tf_op jit(solution)/shard_map/ppermute | solution.py:52
  324.6 25.1 %collective-permute-start.25 = (bf16[1024,256]{1,0:T(8,128)(2,1)}, bf16[1024,256]{1,0:T(8,128)(2,1)}, u32[]{:S(2)}, u32[]{:S(2)}) collective-permute-start(bf16[1024,256]{1,0:T(8,128)(2,1)} %slice.298), channel_id=1, source_target_pairs={{0,2},{1,3},{2,0},{3,1},{4,6},{5,7},{6,4},{7,5},{8,10},{9,11},{10,... | collective-permute-start | bytes 1572872 | tf_op jit(solution)/shard_map/ppermute | solution.py:52
  337.3 14.1 %collective-permute-start.20 = (bf16[1024,256]{1,0:T(8,128)(2,1)}, bf16[1024,256]{1,0:T(8,128)(2,1)}, u32[]{:S(2)}, u32[]{:S(2)}) collective-permute-start(bf16[1024,256]{1,0:T(8,128)(2,1)} %slice.299), channel_id=1, source_target_pairs={{0,2},{1,3},{2,0},{3,1},{4,6},{5,7},{6,4},{7,5},{8,10},{9,11},{10,... | collective-permute-start | bytes 1572872 | tf_op jit(solution)/shard_map/ppermute | solution.py:52
  337.9 23.5 %collective-permute-start.44 = (bf16[4,128,1024]{2,1,0:T(8,128)(2,1)}, bf16[4,128,1024]{2,1,0:T(8,128)(2,1)}, u32[]{:S(2)}, u32[]{:S(2)}) collective-permute-start(bf16[4,128,1024]{2,1,0:T(8,128)(2,1)} %shard_map.513), channel_id=1, source_target_pairs={{0,4},{4,0},{8,12},{12,8},{16,20},{20,16},{24,28},{28,24},{1,5},{5... | collective-permute-start | bytes 3145736 | tf_op jit(solution)/shard_map/ppermute | solution.py:52
  361.4 27.5 %collective-permute-start.45 = (bf16[4,128,1024]{2,1,0:T(8,128)(2,1)S(1)}, bf16[4,128,1024]{2,1,0:T(8,128)(2,1)S(1)}, u32[]{:S(2)}, u32[]{:S(2)}) collective-permute-start(bf16[4,128,1024]{2,1,0:T(8,128)(2,1)S(1)} %copy-done.49), channel_id=1, source_target_pairs={{0,4},{4,0},{8,12},{12,8},{16,20},{20,16},{24,28},{28,24},{1,5},{5... | collective-permute-start | bytes 3145736 | tf_op jit(solution)/shard_map/ppermute | solution.py:52
  363.7 31.3 %collective-permute-start.36 = (bf16[1024,256]{1,0:T(8,128)(2,1)S(1)}, bf16[1024,256]{1,0:T(8,128)(2,1)S(1)}, u32[]{:S(2)}, u32[]{:S(2)}) collective-permute-start(bf16[1024,256]{1,0:T(8,128)(2,1)S(1)} %slice.297), channel_id=1, source_target_pairs={{0,2},{1,3},{2,0},{3,1},{4,6},{5,7},{6,4},{7,5},{8,10},{9,11},{10,... | collective-permute-start | bytes 1572872 | tf_op jit(solution)/shard_map/ppermute | solution.py:52
  370.3 18.4 %collective-permute-start.55 = (bf16[128,1024]{1,0:T(8,128)(2,1)S(1)}, bf16[128,1024]{1,0:T(8,128)(2,1)S(1)}, u32[]{:S(2)}, u32[]{:S(2)}) collective-permute-start(bf16[128,1024]{1,0:T(8,128)(2,1)S(1)} %get-tuple-element.136), channel_id=1, source_target_pairs={{0,16},{4,20},{8,24},{12,28},{16,0},{20,4},{24,8},{28,12},{1,17},{... | collective-permute-start | bytes 786440 | tf_op jit(solution)/shard_map/ppermute | solution.py:52
  370.3 18.4 %collective-permute-start.54 = (bf16[128,1024]{1,0:T(8,128)(2,1)S(1)}, bf16[128,1024]{1,0:T(8,128)(2,1)S(1)}, u32[]{:S(2)}, u32[]{:S(2)}) collective-permute-start(bf16[128,1024]{1,0:T(8,128)(2,1)S(1)} %get-tuple-element.135), channel_id=1, source_target_pairs={{0,8},{4,12},{8,0},{12,4},{16,24},{20,28},{24,16},{28,20},{1,9},{5... | collective-permute-start | bytes 786440 | tf_op jit(solution)/shard_map/ppermute | solution.py:52
  380.1 17.0 %collective-permute-start.40 = (bf16[1024,256]{1,0:T(8,128)(2,1)S(1)}, bf16[1024,256]{1,0:T(8,128)(2,1)S(1)}, u32[]{:S(2)}, u32[]{:S(2)}) collective-permute-start(bf16[1024,256]{1,0:T(8,128)(2,1)S(1)} %slice.296), channel_id=1, source_target_pairs={{0,2},{1,3},{2,0},{3,1},{4,6},{5,7},{6,4},{7,5},{8,10},{9,11},{10,... | collective-permute-start | bytes 1572872 | tf_op jit(solution)/shard_map/ppermute | solution.py:52
  395.0 24.0 %collective-permute-start.58 = (bf16[128,1024]{1,0:T(8,128)(2,1)S(1)}, bf16[128,1024]{1,0:T(8,128)(2,1)S(1)}, u32[]{:S(2)}, u32[]{:S(2)}) collective-permute-start(bf16[128,1024]{1,0:T(8,128)(2,1)S(1)} %get-tuple-element.140), channel_id=1, source_target_pairs={{0,16},{4,20},{8,24},{12,28},{16,0},{20,4},{24,8},{28,12},{1,17},{... | collective-permute-start | bytes 786440 | tf_op jit(solution)/shard_map/ppermute | solution.py:52
  395.0 24.0 %collective-permute-start.57 = (bf16[128,1024]{1,0:T(8,128)(2,1)S(1)}, bf16[128,1024]{1,0:T(8,128)(2,1)S(1)}, u32[]{:S(2)}, u32[]{:S(2)}) collective-permute-start(bf16[128,1024]{1,0:T(8,128)(2,1)S(1)} %get-tuple-element.139), channel_id=1, source_target_pairs={{0,8},{4,12},{8,0},{12,4},{16,24},{20,28},{24,16},{28,20},{1,9},{5... | collective-permute-start | bytes 786440 | tf_op jit(solution)/shard_map/ppermute | solution.py:52
  399.4 29.6 %collective-permute-start.47 = (bf16[4,128,768]{2,1,0:T(8,128)(2,1)}, bf16[4,128,768]{2,1,0:T(8,128)(2,1)}, u32[]{:S(2)}, u32[]{:S(2)}) collective-permute-start(bf16[4,128,768]{2,1,0:T(8,128)(2,1)} %shard_map.510), channel_id=1, source_target_pairs={{0,4},{4,0},{8,12},{12,8},{16,20},{20,16},{24,28},{28,24},{1,5},{5... | collective-permute-start | bytes 2359304 | tf_op jit(solution)/shard_map/ppermute | solution.py:52
  402.7 20.0 %collective-permute-start.53 = (bf16[128,256]{1,0:T(8,128)(2,1)S(1)}, bf16[128,256]{1,0:T(8,128)(2,1)S(1)}, u32[]{:S(2)}, u32[]{:S(2)}) collective-permute-start(bf16[128,256]{1,0:T(8,128)(2,1)S(1)} %get-tuple-element.133), channel_id=1, source_target_pairs={{0,24},{4,28},{8,16},{12,20},{16,8},{20,12},{24,0},{28,4},{1,25},{... | collective-permute-start | bytes 196616 | tf_op jit(solution)/shard_map/ppermute | solution.py:52
  405.1 17.7 %collective-permute-start.52 = (bf16[128,256]{1,0:T(8,128)(2,1)S(1)}, bf16[128,256]{1,0:T(8,128)(2,1)S(1)}, u32[]{:S(2)}, u32[]{:S(2)}) collective-permute-start(bf16[128,256]{1,0:T(8,128)(2,1)S(1)} %get-tuple-element.132), channel_id=1, source_target_pairs={{0,16},{4,20},{8,24},{12,28},{16,0},{20,4},{24,8},{28,12},{1,17},{... | collective-permute-start | bytes 196616 | tf_op jit(solution)/shard_map/ppermute | solution.py:52
  438.1 15.1 %collective-permute-start.49 = (bf16[128,768]{1,0:T(8,128)(2,1)}, bf16[128,768]{1,0:T(8,128)(2,1)S(1)}, u32[]{:S(2)}, u32[]{:S(2)}) collective-permute-start(bf16[128,768]{1,0:T(8,128)(2,1)} %get-tuple-element.128), channel_id=1, source_target_pairs={{0,16},{4,20},{8,24},{12,28},{16,0},{20,4},{24,8},{28,12},{1,17},{... | collective-permute-start | bytes 589832 | tf_op jit(solution)/shard_map/ppermute | solution.py:52
  (165 other events, 1414.9 us)
Sparse Core Ops, SparseCore 0:
  10.8 116.5 all-gather.2

commit v2 on v1

v2 whole, which is shorter than its diff:
```python
import functools

import jax
import jax.numpy as jnp
from jax import lax
from jax.experimental import pallas as pl
from jax.experimental.pallas import tpu as pltpu
from jax.sharding import PartitionSpec as P

D = 1024
FF = 4096
HEAD_DIM = 64
SEQ = 1024
NGROUP = 16
STEP = 7

EPS = 1e-05
THETA = 10000.0
BETA_ONE = 0.5
BETA_TWO = 0.5
ADAM_EPS = 1e-08
DECAY_RATE = 0.1
EMA_RATE = 0.6
GAIN_RATE = 0.4

BF = jnp.bfloat16
F32 = jnp.float32
LANES = 128
TILE = 256
TALL = 512
MIB = 1024 * 1024
SOFT = 1.4426950408889634 * HEAD_DIM**-0.5


def dot(a, b):
    return lax.dot_general(a, b, (((1,), (0,)), ((), ())), preferred_element_type=F32)


def dot_t(a, b):
    return lax.dot_general(a, b, (((1,), (1,)), ((), ())), preferred_element_type=F32)


def dot_l(a, b):
    return lax.dot_general(a, b, (((0,), (0,)), ((), ())), preferred_element_type=F32)


def params(mib, dims=None):
    return pltpu.CompilerParams(vmem_limit_bytes=mib * MIB, dimension_semantics=dims)


def swap(x, axis, bit):
    n = lax.axis_size(axis)
    return lax.ppermute(x, axis, [(i, i ^ bit) for i in range(n)])


def gather_mp(x):
    far = swap(x, "mp", 2)
    near = swap(x, "mp", 1)
    return [x, near, far, swap(far, "mp", 1)]


def whole(shape):
    return pl.BlockSpec(shape, lambda *_: (0,) * len(shape), pipeline_mode=pl.Buffered(1))


def cut(block, where):
    return pl.BlockSpec(block, where)


def rotary_tables(positions):
    half_dim = HEAD_DIM // 2
    frequency = THETA ** (-jnp.arange(half_dim, dtype=F32) / half_dim)
    angles = positions.astype(F32)[:, None] * frequency[None, :]
    cosine, sine = jnp.cos(angles), jnp.sin(angles)
    return (
        jnp.concatenate([cosine] * 4, axis=1),
        jnp.concatenate([-sine, sine, -sine, sine], axis=1),
    )


def turn(x, cos, sin, sign):
    lane = lax.broadcasted_iota(jnp.int32, (x.shape[0], LANES), 1)
    low = (lane % HEAD_DIM) < HEAD_DIM // 2
    parts = []
    for start in range(0, x.shape[1], LANES):
        v = x[:, start : start + LANES]
        other = jnp.where(
            low, pltpu.roll(v, LANES - HEAD_DIM // 2, 1), pltpu.roll(v, HEAD_DIM // 2, 1)
        )
        parts.append(v * cos + (sign * sin) * other)
    return jnp.concatenate(parts, axis=1)


def place_kernel(pos_ref, *refs):
    out, gains = refs[-2:]
    for p, piece in enumerate(refs[:-2]):
        bs = out.shape[1] // (len(refs) - 2)
        at = pl.multiple_of(pos_ref[p], bs)
        for k in range(4):
            out[k, pl.ds(at, bs), :] = piece[k * bs : (k + 1) * bs, :]
        gains[:, pl.ds(at, bs)] = piece[4 * bs : 4 * bs + 16, :bs].astype(F32)[:2, :]


def place_pieces(pos, pieces, bs):
    rows, n = pieces[0].shape
    total = bs * len(pieces)
    return pl.pallas_call(
        place_kernel,
        name="place_attention",
        grid_spec=pltpu.PrefetchScalarGridSpec(
            num_scalar_prefetch=1,
            grid=(1,),
            in_specs=[pl.BlockSpec((rows, n), lambda i, pos: (0, 0))] * len(pieces),
            out_specs=[
                pl.BlockSpec((4, total, n), lambda i, pos: (0, 0, 0)),
                pl.BlockSpec((2, total), lambda i, pos: (0, 0)),
            ],
        ),
        out_shape=[
            jax.ShapeDtypeStruct((4, total, n), BF),
            jax.ShapeDtypeStruct((2, total), F32),
        ],
        compiler_params=params(24),
    )(pos, *pieces)


def flip_kernel(in_ref, out_ref):
    out_ref[0] = in_ref[0].T


def flip(stack):
    k, a, b = stack.shape
    return pl.pallas_call(
        flip_kernel,
        name="flip",
        grid=(k,),
        in_specs=[cut((1, a, b), lambda i: (i, 0, 0))],
        out_specs=cut((1, b, a), lambda i: (i, 0, 0)),
        out_shape=jax.ShapeDtypeStruct((k, b, a), stack.dtype),
        compiler_params=params(16),
    )(stack)


def place_ffn_kernel(pos_ref, in_ref, wide_ref, down_ref):
    wide_ref[...] = in_ref[0, :2]
    down_ref[...] = in_ref[0, 2].T


def place_ffn(pos, stack):
    count, k, bs, n = stack.shape
    return pl.pallas_call(
        place_ffn_kernel,
        name="place_feed_forward",
        grid_spec=pltpu.PrefetchScalarGridSpec(
            num_scalar_prefetch=1,
            grid=(count,),
            in_specs=[pl.BlockSpec((1, k, bs, n), lambda j, pos: (j, 0, 0, 0))],
            out_specs=[
                pl.BlockSpec((2, bs, n), lambda j, pos: (0, pos[j] // bs, 0)),
                pl.BlockSpec((n, bs), lambda j, pos: (0, pos[j] // bs)),
            ],
        ),
        out_shape=[
            jax.ShapeDtypeStruct((2, count * bs, n), stack.dtype),
            jax.ShapeDtypeStruct((n, count * bs), stack.dtype),
        ],
        compiler_params=params(16),
    )(pos, stack)


def place_stack_kernel(pos_ref, in_ref, out_ref):
    out_ref[0] = in_ref[0, 0]


def place_stack(pos, stack):
    count, k, bs, n = stack.shape
    return pl.pallas_call(
        place_stack_kernel,
        name="place_stack",
        grid_spec=pltpu.PrefetchScalarGridSpec(
            num_scalar_prefetch=1,
            grid=(count, k),
            in_specs=[pl.BlockSpec((1, 1, bs, n), lambda j, w, pos: (j, w, 0, 0))],
            out_specs=pl.BlockSpec((1, bs, n), lambda j, w, pos: (w, pos[j] // bs, 0)),
        ),
        out_shape=jax.ShapeDtypeStruct((k, count * bs, n), stack.dtype),
        compiler_params=params(16),
    )(pos, stack)


def qkv_kernel(x0, x1, x2, x3, g_ref, w_ref, cos_ref, sin_ref, oh_ref,
               qkv_ref, norm_ref, scale_ref, trow_ref, qrow_ref, tacc, qacc):
    step = pl.program_id(1)
    x = jnp.concatenate([x0[...], x1[...], x2[...], x3[...]], axis=1)
    xf = x.astype(F32)
    scale = lax.rsqrt(jnp.mean(xf * xf, axis=1, keepdims=True) + EPS)
    scale_ref[...] = scale
    norm = (xf * scale * g_ref[...]).astype(BF)
    norm_ref[...] = norm
    cos, sin = cos_ref[...], sin_ref[...]
    q = turn(dot(norm, w_ref[0]), cos, sin, 1.0).astype(BF)
    qkv_ref[0] = q
    qkv_ref[1] = turn(dot(norm, w_ref[1]), cos, sin, 1.0).astype(BF)
    qkv_ref[2] = dot(norm, w_ref[2]).astype(BF)
    oh = oh_ref[0]

    @pl.when(step == 0)
    def _():
        tacc[...] = jnp.zeros_like(tacc)
        qacc[...] = jnp.zeros_like(qacc)

    tacc[...] += dot(oh, x)
    qacc[...] += dot(oh, q)

    @pl.when(step == pl.num_programs(1) - 1)
    def _():
        trow_ref[...] = tacc[...].astype(BF)
        qrow_ref[...] = qacc[...].astype(BF)


def qkv_call(pieces, gain, weights, cos, sin, onehot):
    count, share = pieces[0].shape
    windows, rows, _ = onehot.shape
    tiles = SEQ // TALL
    tile = lambda w, i: (w * tiles + i, 0)
    return pl.pallas_call(
        qkv_kernel,
        name="qkv",
        grid=(windows, tiles),
        in_specs=[cut((TALL, share), tile)] * 4
        + [
            whole((1, D)),
            whole((4, D, share)),
            cut((TALL, LANES), lambda w, i: (i, 0)),
            cut((TALL, LANES), lambda w, i: (i, 0)),
            cut((1, rows, TALL), lambda w, i: (w, 0, i)),
        ],
        out_specs=[
            cut((3, TALL, share), lambda w, i: (0, w * tiles + i, 0)),
            cut((TALL, D), tile),
            cut((TALL, 1), tile),
            cut((rows, D), lambda w, i: (w, 0)),
            cut((rows, share), lambda w, i: (w, 0)),
        ],
        out_shape=[
            jax.ShapeDtypeStruct((3, count, share), BF),
            jax.ShapeDtypeStruct((count, D), BF),
            jax.ShapeDtypeStruct((count, 1), F32),
            jax.ShapeDtypeStruct((windows * rows, D), BF),
            jax.ShapeDtypeStruct((windows * rows, share), BF),
        ],
        scratch_shapes=[pltpu.VMEM((rows, D), F32), pltpu.VMEM((rows, share), F32)],
        compiler_params=params(32),
        cost_estimate=pl.CostEstimate(
            flops=1000, bytes_accessed=1000, transcendentals=0
        ),
    )(*pieces, gain, weights, cos, sin, onehot)


def attend_kernel(q_ref, k_ref, v_ref, oh_ref, ctx_ref, crow_ref, acc, turned):
    step = pl.program_id(1)
    lane = lax.broadcasted_iota(jnp.int32, (TILE, LANES), 1)
    first = lane < HEAD_DIM
    ones = jnp.ones((SEQ, LANES), BF)

    @pl.when(step == 0)
    def _():
        acc[...] = jnp.zeros_like(acc)
        turned[...] = k_ref[0].T

    parts = []
    for start in range(0, q_ref.shape[2], LANES):
        q = q_ref[0, :, start : start + LANES]
        k = turned[start : start + LANES, :]
        v = jnp.concatenate([v_ref[0, :, start : start + LANES], ones], axis=1)
        heads = []
        for mine in (first, jnp.logical_not(first)):
            scores = dot(jnp.where(mine, q, jnp.zeros_like(q)), k)
            top = jnp.max(scores, axis=1, keepdims=True)
            weight = jnp.exp2((scores - top) * SOFT).astype(BF)
            mixed = dot(weight, v)
            heads.append(mixed[:, :LANES] / mixed[:, LANES:])
        parts.append(jnp.where(first, heads[0], heads[1]))
    context = jnp.concatenate(parts, axis=1).astype(BF)
    ctx_ref[...] = context
    acc[...] += dot(oh_ref[0], context)

    @pl.when(step == pl.num_programs(1) - 1)
    def _():
        crow_ref[...] = acc[...].astype(BF)


def attend_call(qkv, onehot):
    count, share = qkv.shape[1:]
    windows, rows, _ = onehot.shape
    tiles = SEQ // TILE
    return pl.pallas_call(
        attend_kernel,
        name="attend",
        grid=(windows, tiles),
        in_specs=[
            cut((1, TILE, share), lambda w, i: (0, w * tiles + i, 0)),
            cut((1, SEQ, share), lambda w, i: (1, w, 0)),
            cut((1, SEQ, share), lambda w, i: (2, w, 0)),
            cut((1, rows, TILE), lambda w, i: (w, 0, i)),
        ],
        out_specs=[
            cut((TILE, share), lambda w, i: (w * tiles + i, 0)),
            cut((rows, share), lambda w, i: (w, 0)),
        ],
        out_shape=[
            jax.ShapeDtypeStruct((count, share), BF),
            jax.ShapeDtypeStruct((windows * rows, share), BF),
        ],
        scratch_shapes=[pltpu.VMEM((rows, share), F32), pltpu.VMEM((share, SEQ), BF)],
        compiler_params=params(32),
        cost_estimate=pl.CostEstimate(
            flops=1000, bytes_accessed=1000, transcendentals=0
        ),
    )(qkv, qkv, qkv, onehot)


def split_chunks(value, send_ref, keep_ref, far_ref):
    share = keep_ref.shape[1]
    out = value.astype(BF)
    send_ref[:, :share] = out[:, share : 2 * share]
    send_ref[:, share:] = out[:, 3 * share :]
    keep_ref[...] = out[:, :share]
    far_ref[...] = out[:, 2 * share : 3 * share]


def join_wo(out, pieces):
    share = pieces[0].shape[0]
    for r, piece in enumerate(pieces):
        for c in range(4):
            out[r * share : (r + 1) * share, c * share : (c + 1) * share] = piece[
                :, (c ^ r) * share : ((c ^ r) + 1) * share
            ]


def rows_first_kernel(t_ref, c0, c1, c2, c3, o0, o1, o2, o3, g_ref, norm_ref, unit_ref, scale_ref, wo):
    join_wo(wo, (o0, o1, o2, o3))
    context = jnp.concatenate([c0[...], c1[...], c2[...], c3[...]], axis=1)
    residual = t_ref[...].astype(F32) + dot(context, wo[...])
    scale = lax.rsqrt(jnp.mean(residual * residual, axis=1, keepdims=True) + EPS)
    unit = residual * scale
    unit_ref[...] = unit
    scale_ref[...] = jnp.broadcast_to(scale, scale_ref.shape)
    norm_ref[...] = (unit * g_ref[...]).astype(BF)


def rows_first_call(token_rows, contexts, wo, gain):
    rows = token_rows.shape[0]
    fixed = lambda shape: pl.BlockSpec(shape, lambda i: (0,) * len(shape))
    args = (token_rows, *contexts, *wo, gain)
    return pl.pallas_call(
        rows_first_kernel,
        name="rows_first",
        grid=(1,),
        in_specs=[fixed(a.shape) for a in args],
        out_specs=[fixed((rows, D)), fixed((rows, D)), fixed((rows, LANES))],
        out_shape=[
            jax.ShapeDtypeStruct((rows, D), BF),
            jax.ShapeDtypeStruct((rows, D), F32),
            jax.ShapeDtypeStruct((rows, LANES), F32),
        ],
        scratch_shapes=[pltpu.VMEM((D, D), BF)],
        compiler_params=params(24),
        cost_estimate=pl.CostEstimate(
            flops=1000, bytes_accessed=1000, transcendentals=0
        ),
    )(*args)


def ffn_kernel(x0, x1, x2, x3, c0, c1, c2, c3, o0, o1, o2, o3, g_ref, w_ref, d_ref,
               send_ref, keep_ref, far_ref, res_ref, wo):
    share = x0.shape[1]

    @pl.when(pl.program_id(0) == 0)
    def _():
        join_wo(wo, (o0, o1, o2, o3))

    x = jnp.concatenate([x0[...], x1[...], x2[...], x3[...]], axis=1).astype(F32)
    context = jnp.concatenate([c0[...], c1[...], c2[...], c3[...]], axis=1)
    residual = x + dot(context, wo[...])
    scale = lax.rsqrt(jnp.mean(residual * residual, axis=1, keepdims=True) + EPS)
    norm = (residual * scale * g_ref[...]).astype(BF)
    res_ref[...] = residual[:, :share]
    total = None
    width = w_ref.shape[2]
    for start in range(0, width, TILE):
        gate = dot(norm, w_ref[0, :, start : start + TILE])
        up = dot(norm, w_ref[1, :, start : start + TILE])
        hidden = (gate * jax.nn.sigmoid(gate) * up).astype(BF)
        term = dot(hidden, d_ref[start : start + TILE, :])
        total = term if total is None else total + term
    split_chunks(total, send_ref, keep_ref, far_ref)


def ffn_call(pieces, contexts, wo, gain, weights, down):
    count, share = pieces[0].shape
    width = weights.shape[2]
    tile = lambda i: (i, 0)
    return pl.pallas_call(
        ffn_kernel,
        name="feed_forward",
        grid=(count // TALL,),
        in_specs=[cut((TALL, share), tile)] * 8
        + [whole((share, D))] * 4
        + [whole((1, D)), whole((2, D, width)), whole((width, D))],
        out_specs=[
            cut((TALL, 2 * share), tile),
            cut((TALL, share), tile),
            cut((TALL, share), tile),
            cut((TALL, share), tile),
        ],
        out_shape=[
            jax.ShapeDtypeStruct((count, 2 * share), BF),
            jax.ShapeDtypeStruct((count, share), BF),
            jax.ShapeDtypeStruct((count, share), BF),
            jax.ShapeDtypeStruct((count, share), F32),
        ],
        scratch_shapes=[pltpu.VMEM((D, D), BF)],
        compiler_params=params(48),
        cost_estimate=pl.CostEstimate(
            flops=1000, bytes_accessed=1000, transcendentals=0
        ),
    )(*pieces, *contexts, *wo, gain, weights, down)


def rows_kernel(n_ref, seed_ref, w_ref, d_ref,
                hid_ref, gg_ref, ug_ref, send_ref, keep_ref, far_ref, acc):
    step = pl.program_id(0)

    @pl.when(step == 0)
    def _():
        acc[...] = jnp.zeros_like(acc)

    norm = n_ref[...]
    gate = dot(norm, w_ref[0])
    up = dot(norm, w_ref[1])
    sigmoid = jax.nn.sigmoid(gate)
    silu = gate * sigmoid
    hid_ref[...] = (silu * up).astype(BF)
    hidden_grad = dot_t(seed_ref[...], d_ref[...])
    gate_grad = (hidden_grad * up * sigmoid * (1.0 + gate * (1.0 - sigmoid))).astype(BF)
    up_grad = (hidden_grad * silu).astype(BF)
    gg_ref[...] = gate_grad
    ug_ref[...] = up_grad
    acc[...] += dot_t(gate_grad, w_ref[0]) + dot_t(up_grad, w_ref[1])

    @pl.when(step == pl.num_programs(0) - 1)
    def _():
        split_chunks(acc[...], send_ref, keep_ref, far_ref)


def rows_call(norm_rows, seed, weights, down):
    rows = norm_rows.shape[0]
    width = weights.shape[2]
    share = D // 4
    part = 256
    fixed = lambda shape: pl.BlockSpec(shape, lambda i: (0,) * len(shape))
    return pl.pallas_call(
        rows_kernel,
        name="masked_rows",
        grid=(width // part,),
        in_specs=[whole((rows, D)), whole((rows, D))]
        + [cut((2, D, part), lambda i: (0, 0, i)), cut((part, D), lambda i: (i, 0))],
        out_specs=[
            cut((rows, part), lambda i: (0, i)),
            cut((rows, part), lambda i: (0, i)),
            cut((rows, part), lambda i: (0, i)),
            fixed((rows, 2 * share)),
            fixed((rows, share)),
            fixed((rows, share)),
        ],
        out_shape=[
            jax.ShapeDtypeStruct((rows, width), BF),
            jax.ShapeDtypeStruct((rows, width), BF),
            jax.ShapeDtypeStruct((rows, width), BF),
            jax.ShapeDtypeStruct((rows, 2 * share), BF),
            jax.ShapeDtypeStruct((rows, share), BF),
            jax.ShapeDtypeStruct((rows, share), BF),
        ],
        scratch_shapes=[pltpu.VMEM((rows, D), F32)],
        compiler_params=params(32),
        cost_estimate=pl.CostEstimate(
            flops=1000, bytes_accessed=1000, transcendentals=0
        ),
    )(norm_rows, seed, weights, down)


def seed_kernel(own_ref, near_ref, seed_ref, unit_ref, scale_ref, g_ref, w_ref,
                low_ref, own_seed_ref, ctx_ref, gain_ref):
    share = own_ref.shape[1] // 2
    own, near = own_ref[...], near_ref[...]
    grad = jnp.concatenate(
        [own[:, :share], near[:, :share], own[:, share:], near[:, share:]], axis=1
    ).astype(F32)
    unit = unit_ref[...].astype(F32)
    gain_ref[...] = jnp.sum(grad * unit, axis=0, keepdims=True)
    scaled = grad * g_ref[...]
    back = seed_ref[...] + scale_ref[:, :1] * (
        scaled - unit * jnp.mean(scaled * unit, axis=1, keepdims=True)
    )
    low = back.astype(BF)
    low_ref[...] = low
    high = low[:, :share]
    own_seed_ref[:, :share] = high
    own_seed_ref[:, share:] = (back[:, :share] - high.astype(F32)).astype(BF)
    ctx_ref[...] = dot(low, w_ref[0]).astype(BF)


def seed_call(own, near, seed, unit, scale, gain, weights):
    rows = own.shape[0]
    share = own.shape[1] // 2
    fixed = lambda shape: pl.BlockSpec(shape, lambda i: (0,) * len(shape))
    return pl.pallas_call(
        seed_kernel,
        name="seed_back",
        grid=(1,),
        in_specs=[fixed(a.shape) for a in (own, near, seed, unit, scale, gain)]
        + [pl.BlockSpec((1, D, share), lambda i: (3, 0, 0))],
        out_specs=[fixed((rows, D)), fixed((rows, 2 * share)), fixed((rows, share)), fixed((1, D))],
        out_shape=[
            jax.ShapeDtypeStruct((rows, D), BF),
            jax.ShapeDtypeStruct((rows, 2 * share), BF),
            jax.ShapeDtypeStruct((rows, share), BF),
            jax.ShapeDtypeStruct((1, D), F32),
        ],
        compiler_params=params(24),
        cost_estimate=pl.CostEstimate(
            flops=1000, bytes_accessed=1000, transcendentals=0
        ),
    )(own, near, seed, unit, scale, gain, weights)


def chosen(ref, pos_ref, blocks):
    return jnp.concatenate(
        [ref[:, pl.ds(pl.multiple_of(pos_ref[b], LANES), LANES)] for b in blocks], axis=1
    )


def pack_kernel(halves, rhs_count, pos_ref, lhs_ref, *refs):
    rhs, outs = refs[:rhs_count], refs[rhs_count:]
    size = 8 // halves
    for h, out in enumerate(outs):
        left = chosen(lhs_ref, pos_ref, range(h * size, (h + 1) * size))
        at = 0
        for right in rhs:
            for start in range(0, right.shape[1], 512):
                value = dot_l(left, right[:, start : start + 512]).astype(BF)
                for b in range(size):
                    out[b, :, at + start : at + start + 512] = value[b * LANES : (b + 1) * LANES]
            at += right.shape[1]


def pack(pos, lhs, rhs, halves, name):
    rows = lhs.shape[0]
    n = sum(r.shape[1] for r in rhs)
    size = 8 // halves
    zero = lambda i, pos: (0, 0)
    return pl.pallas_call(
        functools.partial(pack_kernel, halves, len(rhs)),
        name="pack_" + name,
        grid_spec=pltpu.PrefetchScalarGridSpec(
            num_scalar_prefetch=1,
            grid=(1,),
            in_specs=[pl.BlockSpec(a.shape, zero) for a in (lhs, *rhs)],
            out_specs=[pl.BlockSpec((size, LANES, n), lambda i, pos: (0, 0, 0))] * halves,
        ),
        out_shape=[jax.ShapeDtypeStruct((size, LANES, n), BF)] * halves,
        compiler_params=params(32),
        cost_estimate=pl.CostEstimate(
            flops=1000, bytes_accessed=1000, transcendentals=0
        ),
    )(pos, lhs, *rhs)


def pack_attention_kernel(pos_ref, norm_ref, d_ref, seed_ref, ctx_ref, gain_ref, send_ref, keep_ref, acc):
    step = pl.program_id(0)
    n = d_ref.shape[1]
    value = dot_l(chosen(norm_ref, pos_ref, range(8)), d_ref[...])

    @pl.when(step == 0)
    def _():
        acc[...] = value
        proj = dot_l(chosen(seed_ref, pos_ref, range(8)), ctx_ref[...]).astype(BF)
        for b in range(8):
            out = (send_ref, keep_ref)[b // 4]
            out[b % 4, :LANES, n:] = proj[b * LANES : (b + 1) * LANES]
            gain = gain_ref[:, pl.ds(pl.multiple_of(pos_ref[b], LANES), LANES)].astype(BF)
            out[b % 4, LANES:, :] = jnp.zeros((16, out.shape[2]), BF)
            out[b % 4, LANES:, :LANES] = jnp.broadcast_to(gain, (16, LANES))

    @pl.when(step > 0)
    def _():
        acc[...] += value

    @pl.when(step == pl.num_programs(0) - 1)
    def _():
        for b in range(8):
            out = (send_ref, keep_ref)[b // 4]
            out[b % 4, :LANES, :n] = acc[b * LANES : (b + 1) * LANES, :].astype(BF)


def pack_attention(pos, norm, dqkv, seed, context_rows, gain):
    count = norm.shape[0]
    rows, share = context_rows.shape
    n = dqkv.shape[1]
    tile = lambda i, pos: (i, 0)
    zero = lambda i, pos: (0, 0)
    return pl.pallas_call(
        pack_attention_kernel,
        name="pack_attention",
        grid_spec=pltpu.PrefetchScalarGridSpec(
            num_scalar_prefetch=1,
            grid=(count // TALL,),
            in_specs=[
                pl.BlockSpec((TALL, D), tile),
                pl.BlockSpec((TALL, n), tile),
                pl.BlockSpec((rows, D), zero),
                pl.BlockSpec((rows, share), zero),
                pl.BlockSpec((1, D), zero),
            ],
            out_specs=[pl.BlockSpec((4, LANES + 16, n + share), lambda i, pos: (0, 0, 0))] * 2,
            scratch_shapes=[pltpu.VMEM((D, n), F32)],
        ),
        out_shape=[jax.ShapeDtypeStruct((4, LANES + 16, n + share), BF)] * 2,
        compiler_params=params(32),
        cost_estimate=pl.CostEstimate(
            flops=1000, bytes_accessed=1000, transcendentals=0
        ),
    )(pos, norm, dqkv, seed, context_rows, gain)


def add_terms_kernel(keep_ref, recv_ref, *outs):
    for k, out in enumerate(outs):
        out[...] = (keep_ref[k].astype(F32) + recv_ref[k].astype(F32)).astype(out.dtype)


def add_terms(keep, received, name):
    count, rows, n = keep.shape
    block = pl.BlockSpec((count, rows, 512), lambda i: (0, 0, i))
    return pl.pallas_call(
        add_terms_kernel,
        name="add_" + name,
        grid=(n // 512,),
        in_specs=[block] * 2,
        out_specs=[pl.BlockSpec((rows, 512), lambda i: (0, i))] * count,
        out_shape=[jax.ShapeDtypeStruct((rows, n), F32 if k == 0 else BF) for k in range(count)],
        compiler_params=params(16),
    )(keep, received)


def back_kernel(q_ref, do_ref, a_ref, k_ref, v_ref, oh_ref, cosm_ref, sinm_ref, cos_ref, sin_ref,
                out_ref, dot_ref):
    rows, share = q_ref.shape
    lane = lax.broadcasted_iota(jnp.int32, (rows, LANES), 1)
    first = lane < HEAD_DIM
    scale = HEAD_DIM**-0.5
    dq_parts, dk_parts, dv_parts = [], [], []
    for start in range(0, share, LANES):
        q = q_ref[:, start : start + LANES]
        do = do_ref[:, start : start + LANES]
        k = k_ref[0, :, start : start + LANES]
        v = v_ref[0, :, start : start + LANES]
        dqs, dk, dv = [], None, None
        for mine in (first, jnp.logical_not(first)):
            qm = jnp.where(mine, q, jnp.zeros_like(q))
            dm = jnp.where(mine, do, jnp.zeros_like(do))
            scores = dot_t(qm, k)
            top = jnp.max(scores, axis=1, keepdims=True)
            weight = jnp.exp2((scores - top) * SOFT)
            prob = weight * (1.0 / jnp.sum(weight, axis=1, keepdims=True))
            prob_grad = dot_t(dm, v)
            delta = jnp.sum(prob * prob_grad, axis=1, keepdims=True)
            score_grad = (prob * (prob_grad - delta)).astype(BF)
            dqs.append(dot(score_grad, k))
            term = dot_l(score_grad, qm)
            dk = term if dk is None else dk + term
            term = dot_l(prob.astype(BF), dm)
            dv = term if dv is None else dv + term
        dq_parts.append(jnp.where(first, dqs[0], dqs[1]) * scale)
        dk_parts.append(dk * scale)
        dv_parts.append(dv)
    dq = jnp.concatenate(dq_parts, axis=1)
    dk = jnp.concatenate(dk_parts, axis=1)
    dv = jnp.concatenate(dv_parts, axis=1)
    both = jnp.concatenate(
        [turn(dq, cosm_ref[...], sinm_ref[...], -1.0).astype(BF), dq.astype(BF)], axis=1
    )
    both = dot_l(oh_ref[0], both)
    out_ref[:, :share] = both[:, :share].astype(BF)
    out_ref[:, share : 2 * share] = turn(dk, cos_ref[...], sin_ref[...], -1.0).astype(BF)
    out_ref[:, 2 * share :] = dv.astype(BF)
    terms = both[:, share:] * a_ref[0].astype(F32)
    terms = terms + dk * k_ref[0].astype(F32) + dv * v_ref[0].astype(F32)
    high = terms.astype(BF)
    low = (terms - high.astype(F32)).astype(BF)
    ones = jnp.ones((16, share), BF)
    dot_ref[...] = (dot_t(ones, high) + dot_t(ones, low))[:1]


def back_call(q_rows, context_grad, qkv, onehot, cosm, sinm, cos, sin):
    windows, rows, _ = onehot.shape
    count, share = qkv.shape[1:]
    mine = lambda w: (w, 0)
    fixed = lambda w: (0, 0)
    return pl.pallas_call(
        back_kernel,
        name="attend_back",
        grid=(windows,),
        in_specs=[
            cut((rows, share), mine),
            cut((rows, share), mine),
            cut((1, SEQ, share), lambda w: (0, w, 0)),
            cut((1, SEQ, share), lambda w: (1, w, 0)),
            cut((1, SEQ, share), lambda w: (2, w, 0)),
            cut((1, rows, SEQ), lambda w: (w, 0, 0)),
            cut((rows, LANES), mine),
            cut((rows, LANES), mine),
            cut((SEQ, LANES), fixed),
            cut((SEQ, LANES), fixed),
        ],
        out_specs=[cut((SEQ, 3 * share), mine), cut((1, SEQ), lambda w: (0, w))],
        out_shape=[
            jax.ShapeDtypeStruct((count, 3 * share), BF),
            jax.ShapeDtypeStruct((1, count), F32),
        ],
        compiler_params=params(40),
        cost_estimate=pl.CostEstimate(
            flops=1000, bytes_accessed=1000, transcendentals=0
        ),
    )(q_rows, context_grad, qkv, qkv, qkv, onehot, cosm, sinm, cos, sin)


def first_grad_kernel(d_ref, w_ref, send_ref, keep_ref, far_ref):
    share = keep_ref.shape[1]
    grad = None
    for t in range(3):
        term = dot(d_ref[:, t * share : (t + 1) * share], w_ref[t])
        grad = term if grad is None else grad + term
    split_chunks(grad, send_ref, keep_ref, far_ref)


def first_grad_call(dqkv, weights):
    count = dqkv.shape[0]
    share = dqkv.shape[1] // 3
    tile = lambda i: (i, 0)
    return pl.pallas_call(
        first_grad_kernel,
        name="first_grad",
        grid=(count // TALL,),
        in_specs=[cut((TALL, 3 * share), tile), whole((3, share, D))],
        out_specs=[
            cut((TALL, 2 * share), tile),
            cut((TALL, share), tile),
            cut((TALL, share), tile),
        ],
        out_shape=[
            jax.ShapeDtypeStruct((count, 2 * share), BF),
            jax.ShapeDtypeStruct((count, share), BF),
            jax.ShapeDtypeStruct((count, share), BF),
        ],
        compiler_params=params(32),
        cost_estimate=pl.CostEstimate(
            flops=1000, bytes_accessed=1000, transcendentals=0
        ),
    )(dqkv, weights)


def input_kernel(x_ref, s_ref, dot_ref, keep_ref, near_ref, far_ref, g_ref, oh_ref, hl_ref, out_ref):
    share = x_ref.shape[1]
    grad = keep_ref[...].astype(F32) + near_ref[...].astype(F32) + far_ref[...].astype(F32)
    scale = s_ref[...]
    column = jnp.broadcast_to(dot_ref[...], (8, dot_ref.shape[1])).T[:, :1]
    back = dot_l(oh_ref[0], hl_ref[0])
    unit = x_ref[...].astype(F32) * scale
    out = back[:, :share] + back[:, share:] + scale * (grad * g_ref[...] - unit * (column / D))
    out_ref[...] = out.astype(BF)


def input_call(tokens, scale, dots, keep, near, far, gain, onehot, seeds):
    count, share = tokens.shape
    windows, rows, _ = onehot.shape
    tiles = SEQ // TILE
    tile = lambda w, i: (w * tiles + i, 0)
    return pl.pallas_call(
        input_kernel,
        name="input_grad",
        grid=(windows, tiles),
        in_specs=[
            cut((TILE, share), tile),
            cut((TILE, 1), tile),
            cut((1, TILE), lambda w, i: (0, w * tiles + i)),
            cut((TILE, share), tile),
            cut((TILE, share), tile),
            cut((TILE, share), tile),
            cut((1, share), lambda w, i: (0, 0)),
            cut((1, rows, TILE), lambda w, i: (w, 0, i)),
            cut((1, rows, 2 * share), lambda w, i: (w, 0, 0)),
        ],
        out_specs=cut((TILE, share), tile),
        out_shape=jax.ShapeDtypeStruct((count, share), BF),
        compiler_params=params(24),
        cost_estimate=pl.CostEstimate(
            flops=1000, bytes_accessed=1000, transcendentals=0
        ),
    )(tokens, scale, dots, keep, near, far, gain, onehot, seeds)


def adam_step(summed, master, first_old, second, average, step_rate, weight_decay):
    new_first = BETA_ONE * first_old + (1.0 - BETA_ONE) * summed
    new_second = BETA_TWO * second + (1.0 - BETA_TWO) * summed * summed
    update = (
        new_first
        / (1.0 - BETA_ONE**STEP)
        / (jnp.sqrt(new_second / (1.0 - BETA_TWO**STEP)) + ADAM_EPS)
    )
    new_master = master - step_rate * (update + weight_decay * master)
    new_average = EMA_RATE * average + (1.0 - EMA_RATE) * new_master
    return (summed, new_master, new_first, new_second, new_average, new_master.astype(BF))


def adam_cols_kernel(sets, rate, *refs):
    terms, (m, f, s, a), outs = refs[:sets], refs[sets : sets + 4], refs[sets + 4 :]
    grad = sum((t[...].astype(F32) for t in terms[1:]), terms[0][...].astype(F32))
    values = adam_step(grad, m[0], f[0], s[0], a[0], rate, DECAY_RATE)
    for out, value in zip(outs[:6], values, strict=True):
        out[0] = value
    if len(outs) > 6:
        used = m[0].astype(BF).astype(F32)
        part = jnp.broadcast_to(jnp.sum(used * grad, axis=1, keepdims=True), outs[6].shape)

        @pl.when((pl.program_id(0) == 0) & (pl.program_id(1) == 0))
        def _():
            outs[6][...] = jnp.zeros_like(outs[6])

        outs[6][...] += part


def adam_cols(terms, arrays, rate, name, rows=False):
    k, bs, n = arrays[0].shape
    part = min(n, 512)
    tiles = n // part
    term = cut((bs, part), lambda t, j: (0, t * tiles + j))
    spot = cut((1, bs, part), lambda t, j: (t, 0, j))
    return pl.pallas_call(
        functools.partial(adam_cols_kernel, len(terms), rate),
        name="adam_" + name,
        grid=(k, tiles),
        in_specs=[term] * len(terms) + [spot] * 4,
        out_specs=[spot] * 6 + [cut((bs, LANES), lambda t, j: (0, 0))] * rows,
        out_shape=[jax.ShapeDtypeStruct((k, bs, n), BF if i == 5 else F32) for i in range(6)]
        + [jax.ShapeDtypeStruct((bs, LANES), F32)] * rows,
        compiler_params=params(24),
    )(*terms, *arrays)


def adam_rows_kernel(rate, *refs):
    terms, (m, f, s, a), outs = refs[:4], refs[4:8], refs[8:]
    grad = sum((t[...].astype(F32) for t in terms[1:]), terms[0][...]).T
    values = adam_step(grad, m[...], f[...], s[...], a[...], rate, DECAY_RATE)
    for out, value in zip(outs, values, strict=True):
        out[...] = value


def adam_rows(terms, offset, arrays, rate, name):
    n, bs = arrays[0].shape
    term = cut((bs, TILE), lambda i: (0, offset // TILE + i))
    spot = cut((TILE, bs), lambda i: (i, 0))
    return pl.pallas_call(
        functools.partial(adam_rows_kernel, rate),
        name="adam_" + name,
        grid=(n // TILE,),
        in_specs=[term] * 4 + [spot] * 4,
        out_specs=[spot] * 6,
        out_shape=[jax.ShapeDtypeStruct((n, bs), BF if i == 5 else F32) for i in range(6)],
        compiler_params=params(24),
    )(*terms, *arrays)


def at_once(*values):
    return lax.optimization_barrier(values)


def tie(x, *others):
    return lax.optimization_barrier((x, *others))[0]


def local(
    tokens,
    cotangent,
    mask_rows,
    genome,
    group_tokens,
    owner,
    qkv_master,
    qkv_first,
    qkv_second,
    qkv_average,
    proj_master,
    proj_first,
    proj_second,
    proj_average,
    gate_up_master,
    gate_up_first,
    gate_up_second,
    gate_up_average,
    down_master,
    down_first,
    down_second,
    down_average,
    gains_master,
    gains_first,
    gains_second,
    gains_average,
    short=None,
):
    ndp = lax.axis_size("dp")
    me = lax.axis_index("dp")
    m = lax.axis_index("mp")
    count, share = tokens.shape
    block = qkv_master.shape[1]
    windows, masked = mask_rows.shape
    rows = -(-masked // 32) * 32
    if short is None:
        short = ndp == 8 and block == LANES

    def start(b):
        at = b * block
        return ((at // share) ^ m) * share + at % share

    device = jnp.arange(ndp, dtype=jnp.int32)
    owner_x = jnp.sum(
        jnp.where((device[:, None] ^ me) == device[None, :], owner[None, :], 0), axis=1
    )
    pos = start(owner)
    pos_x = start(owner_x)

    attn_block = [qkv_master[0], qkv_master[1], qkv_master[2], proj_master.T]
    ffn_block = jnp.concatenate(
        [gate_up_master.astype(BF), down_master.T.astype(BF)[None]], axis=0
    )
    far = swap(tokens, "mp", 2)
    near = swap(tokens, "mp", 1)
    if short:
        extra = jnp.pad(gains_master, ((0, 14), (0, share - block)))
        message = jnp.concatenate(attn_block + [extra], axis=0).astype(BF)
        z_pieces = [message] + [swap(message, "dp", bit) for bit in (2, 4, 6)]
        x_pieces = [swap(piece, "dp", 1) for piece in z_pieces]
        order = [None] * 8
        for k in range(4):
            order[2 * k], order[2 * k + 1] = z_pieces[k], x_pieces[k]
        attn_w, gains = place_pieces(pos_x, order, block)
        gains = gains.reshape(2, 1, D)
    else:
        attn_block = jnp.stack(attn_block).astype(BF)
        attn_w = place_stack(pos, lax.all_gather(attn_block, "dp", axis=0, tiled=False))
        all_gains = lax.all_gather(gains_master.astype(BF), "dp", axis=1, tiled=False)
        slot = (device * block)[:, None] == pos[None, :]
        gains = jnp.sum(
            jnp.where(slot[None, :, :, None], all_gains.astype(F32)[:, None], 0.0), axis=2
        ).reshape(2, 1, D)
    ffn_stack = lax.all_gather(ffn_block, "dp", axis=0, tiled=False)

    tokens_p = [tokens, near, far, swap(far, "mp", 1)]
    padded = jnp.pad(mask_rows, ((0, 0), (0, rows - masked)), constant_values=-1)
    onehot = (
        padded[:, :, None] == lax.broadcasted_iota(jnp.int32, (1, 1, SEQ), 2)
    ).astype(BF)
    cos, sin = rotary_tables(jnp.arange(SEQ))
    cosm, sinm = rotary_tables(padded.reshape(-1))
    counts = group_tokens.astype(F32)
    picked = jnp.sum(
        jnp.where(
            genome[:, None] == jnp.arange(NGROUP, dtype=jnp.int32)[None, :], counts[None, :], 0.0
        ),
        axis=1,
    )
    window_scale = NGROUP * picked / jnp.sum(counts)
    attn_t = flip(attn_w)
    wo_far = swap(attn_t[3], "mp", 2)
    qkv, norm_one, scale_one, token_rows, q_rows = qkv_call(
        tokens_p, gains[0], tie(attn_w, attn_t), cos, sin, onehot
    )
    context, context_rows = attend_call(tie(qkv, wo_far), onehot)
    wo_p = [attn_t[3], swap(attn_t[3], "mp", 1), wo_far, swap(wo_far, "mp", 1)]
    cot = jnp.pad(cotangent.reshape(windows, masked, share), ((0, 0), (0, rows - masked), (0, 0)))
    both = jnp.concatenate([context_rows, cot.reshape(windows * rows, share)], axis=0)
    both_p = gather_mp(both)
    context_rows_p = [piece[: windows * rows] for piece in both_p]
    cot = jnp.concatenate([piece[windows * rows :] for piece in both_p], axis=1)
    context = tie(context, both_p[3])
    context_far = swap(context, "mp", 2)
    seed = jnp.repeat(window_scale, rows)[:, None] * cot.astype(F32)
    seed_low = seed.astype(BF)
    norm_rows, unit, scale_rows = rows_first_call(token_rows, context_rows_p, wo_p, gains[1])

    ffn_stack = tie(ffn_stack, norm_rows)
    if short:
        wide_w, down_w = place_ffn(pos, ffn_stack)
    else:
        wide_w = place_stack(pos, ffn_stack)
        wide_w, down_w = wide_w[:2], wide_w[2].T
    hidden_rows, gate_grad, up_grad, n2_send, n2_keep, n2_far = rows_call(
        norm_rows, seed_low, wide_w, down_w
    )

    context_near, context_far = at_once(context, context_far, n2_send)[:2]
    context_p = [context, swap(context_near, "mp", 1), context_far, swap(context_far, "mp", 1)]

    def reduce_all(lhs, rhs):
        grad = dot_l(lhs, rhs).reshape(ndp, block, rhs.shape[1])
        grad = jnp.take(grad, pos // block, axis=0, mode="clip")
        return lax.psum_scatter(grad, "dp", scatter_dimension=0, tiled=True)[0]

    n2_near = swap(n2_send, "mp", 1)
    if short:
        sides = jnp.concatenate([pos_x[1::2], pos_x[0::2]])
        (wide_blocks,) = pack(pos, norm_rows, [gate_grad, up_grad], 1, "wide")
        wide_sum = lax.psum_scatter(wide_blocks, "dp", scatter_dimension=0, tiled=False)
        n2_near, hidden_rows = at_once(n2_near, hidden_rows, wide_blocks)[:2]
    n2_near = n2_near.astype(F32)
    n2_half = jnp.concatenate(
        [n2_keep.astype(F32) + n2_near[:, :share], n2_far.astype(F32) + n2_near[:, share:]], axis=1
    ).astype(BF)
    n2_back = swap(n2_half, "mp", 2)
    if short:
        down_send, down_keep = pack(sides, seed_low, [hidden_rows], 2, "down")
        down_x = swap(down_send, "dp", 1)
        n2_back, context_p = at_once(n2_back, context_p, down_send)[:2]
    n2_back = n2_back.astype(F32)
    n2_own = (
        n2_half.astype(F32) + jnp.concatenate([n2_back[:, share:], n2_back[:, :share]], axis=1)
    ).astype(BF)
    attn_seed, own_seed, context_grad, gain_two = seed_call(
        n2_own, swap(n2_own, "mp", 1), seed, unit, scale_rows, gains[1], attn_w
    )
    own_seed = own_seed.reshape(windows, rows, 2 * share)

    dqkv, row_dot = back_call(q_rows, context_grad, qkv, onehot, cosm, sinm, cos, sin)
    n_send, n_keep, n_far = first_grad_call(dqkv, attn_t)
    row_dot = row_dot + swap(row_dot, "mp", 1)
    if short:
        down_added = add_terms(down_keep, down_x, "down")
        n_send, row_dot, down_added = at_once(n_send, row_dot, down_added)
    n_near = swap(n_send, "mp", 1)
    row_far = swap(row_dot, "mp", 2)
    if short:
        attn_send, attn_keep = pack_attention(
            sides, norm_one, tie(dqkv, n_send), attn_seed, context_rows, gain_two
        )
        n_near, row_far, attn_send, down_added = at_once(n_near, row_far, attn_send, down_added)
    row_dot = row_dot + row_far
    n_half = (n_far.astype(F32) + n_near[:, share:].astype(F32)).astype(BF)

    if short:
        n_half, attn_send, down_added, ffn_in = at_once(n_half, attn_send, down_added, context_p)
        attn_x = swap(attn_send, "dp", 1)
        down_terms = [down_added[0]] + [swap(down_added[k], "dp", 2 * k) for k in range(1, 4)]
        n_back = swap(n_half, "mp", 2)
        ffn_out = ffn_call(tokens_p, ffn_in, wo_p, gains[1], wide_w, down_w)
        ffn_out, attn_x, down_terms, n_back = at_once(ffn_out, attn_x, down_terms, n_back)
        attn_added = add_terms(attn_keep, attn_x, "attention")
    else:
        n_back = swap(n_half, "mp", 2)
        ffn_out = ffn_call(tokens_p, context_p, wo_p, gains[1], wide_w, down_w)
    f_send, f_keep, f_far, residual = ffn_out
    f_near = swap(f_send, "mp", 1)
    down_old = (down_master, down_first, down_second, down_average)
    down_rate = FF ** (-0.5)
    if short:
        down_out = adam_rows(down_terms, 0, down_old, down_rate, "down")
        f_near, attn_added, down_out = at_once(f_near, attn_added, down_out)
    f_half = (f_far.astype(F32) + f_near[:, share:].astype(F32)).astype(BF)
    f_part = residual + f_keep.astype(F32) + f_near[:, :share].astype(F32)
    if short:
        f_half, attn_added, f_part = at_once(f_half, attn_added, f_part)
    f_back = swap(f_half, "mp", 2)
    if short:
        attn_terms = [attn_added[0]] + [swap(attn_added[k], "dp", 2 * k) for k in range(1, 4)]
    input_grad = input_call(
        tokens,
        scale_one,
        row_dot,
        n_keep,
        n_near[:, :share],
        n_back,
        gains[0][:, :share],
        onehot,
        own_seed,
    )
    if short:
        gate_up_old = (gate_up_master, gate_up_first, gate_up_second, gate_up_average)
        gate_up_out = adam_cols([wide_sum], gate_up_old, D ** (-0.5), "gate_up")
        f_back, attn_terms, input_grad, gate_up_out = at_once(
            f_back, attn_terms, input_grad, gate_up_out
        )
    output = (f_part + f_back.astype(F32)).astype(BF)
    qkv_old = (qkv_master, qkv_first, qkv_second, qkv_average)
    proj_old = (proj_master, proj_first, proj_second, proj_average)
    gate_up_old = (gate_up_master, gate_up_first, gate_up_second, gate_up_average)
    wide_rate = D ** (-0.5)
    proj_rate = (3.0 * D / SEQ) ** (-0.5)
    if short:
        *qkv_out, first_rows = adam_cols(attn_terms, qkv_old, wide_rate, "qkv", True)
        proj_out = adam_rows(attn_terms, 3 * share, proj_old, proj_rate, "proj")
        gain_two = sum(term[LANES : LANES + 1, :LANES].astype(F32) for term in attn_terms)
        gain_one = first_rows[:, :1].T
    else:
        qkv_sum = reduce_all(norm_one, dqkv)
        qkv_sum = jnp.moveaxis(qkv_sum.reshape(block, 3, share), 1, 0)
        gate_up_sum = jnp.stack([reduce_all(norm_rows, gate_grad), reduce_all(norm_rows, up_grad)])
        proj_sum = reduce_all(attn_seed, context_rows).T
        down_sum = reduce_all(seed_low, hidden_rows).T
        gain_one = jnp.sum(
            qkv_master.astype(BF).astype(F32) * qkv_sum, axis=(0, 2)
        )[None]
        all_two = jnp.take(gain_two.reshape(ndp, block), pos // block, axis=0, mode="clip")
        gain_two = lax.psum_scatter(all_two, "dp", scatter_dimension=0, tiled=True)
        down_out = adam_step(down_sum, *down_old, down_rate, DECAY_RATE)
        gate_up_out = adam_step(gate_up_sum, *gate_up_old, wide_rate, DECAY_RATE)
        qkv_out = adam_step(qkv_sum, *qkv_old, wide_rate, DECAY_RATE)
        proj_out = adam_step(proj_sum, *proj_old, proj_rate, DECAY_RATE)
    gain_one = gain_one + swap(gain_one, "mp", 1)
    gain_one = (gain_one + swap(gain_one, "mp", 2)) / gains_master[:1].astype(BF).astype(F32)
    gains_sum = jnp.concatenate([gain_one, gain_two], axis=0)
    gains_out = adam_step(
        gains_sum, gains_master, gains_first, gains_second, gains_average, GAIN_RATE, 0.0
    )
    return (output, input_grad, *qkv_out, *proj_out, *gate_up_out, *down_out, *gains_out)


def solution(mesh, short=None):
    tokens = P("dp", "mp")
    cols = P(None, "dp", "mp")
    lines = P("mp", "dp")
    gains = P(None, "dp")
    in_specs = (tokens, tokens, P("dp", None), P("dp"), P(), P())
    in_specs += (cols,) * 4 + (lines,) * 4 + (cols,) * 4 + (lines,) * 4 + (gains,) * 4
    out_specs = (tokens, tokens)
    out_specs += (cols,) * 6 + (lines,) * 6 + (cols,) * 6 + (lines,) * 6 + (gains,) * 6
    return jax.shard_map(
        functools.partial(local, short=short),
        mesh=mesh,
        in_specs=in_specs,
        out_specs=out_specs,
        check_vma=False,
    )
```

time: 471 us -> 309 us (0.66)
  local copies, waits for them, and re-layouts: 88.8 us -> 41.2 us
  starting transfers between devices: 73.1 us -> 36.9 us
  waiting for transfers between devices: 114 us -> 78.8 us
  other arithmetic: 46.7 us -> 27.2 us
  Pallas kernels: 123 us -> 105 us
  matrix products: 5.23 us -> 0 us
    ppermute x68 -> x38, waiting for transfers between devices: 114 us -> 48 us  [swap(): return lax.ppermute(x, axis, [(i, i ^ bit) for i in range(n)])]
    unnamed x320 -> x216, local copies, waits for them, and re-layouts: 79 us -> 30 us
    ppermute x68 -> x38, starting transfers between devices: 73.1 us -> 36.8 us  [swap(): return lax.ppermute(x, axis, [(i, i ^ bit) for i in range(n)])]
    all_gather x1, waiting for transfers between devices: 0.01 us -> 18.1 us  [local(): ffn_stack = lax.all_gather(ffn_block, 'dp', axis=0, tiled=False)]
    pallas_call x23 -> x21, Pallas kernels: 123 us -> 105 us  [the longest x1 23.5 us: ffn_call(): pl.pallas_call(ffn_kernel, name='feed_forward', grid=(count // TALL,), in...]
    reduce_scatter x0 -> x1, waiting for transfers between devices: none -> 12.8 us  [local(): lax.psum_scatter(wide_blocks, 'dp', scatter_dimension=0, tiled=False)]
    add x10 -> x4, other arithmetic: 7.89 us -> 2.19 us  [the longest x1 2.17 us: local(): f_part = residual + f_keep.astype(F32) + f_near[:, :share].astype(F32)]
    dot_general x3 -> x0, matrix products: 5.23 us -> none  [the longest x2 4.9 us: dot_l(): lax.dot_general(a, b, (((0,), (0,)), ((), ())), preferred_element_type=F32)]
  transfers between devices with their start and end apart: 69 -> 40, of which waited for: 18 -> 14; matrix products, arithmetic and copies ran while one was open for 21% -> 11% of each run, Pallas kernels for 25% -> 34%
where the time goes in v2:
time: 309 us; the launch traced here: 305 us
  Pallas kernels  105 us (34%)
  waiting for transfers between devices  78.8 us (26%)
  local copies, waits for them, and re-layouts  41.2 us (13%)
  starting transfers between devices  36.9 us (12%)
  other arithmetic  27.2 us (9%)
  between operations  15.4 us (5%)
    ppermute x38, waiting for transfers between devices, swap(): return lax.ppermute(x, axis, [(i, i ^ bit) for i in range(n)])  48 us
    ppermute x38, starting transfers between devices, swap(): return lax.ppermute(x, axis, [(i, i ^ bit) for i in range(n)])  36.8 us
    unnamed x216, local copies, waits for them, and re-layouts  30 us
    pallas_call x1, Pallas kernels, ffn_call(): pl.pallas_call(ffn_kernel, name='feed_forward', grid=(count // TALL,), in...  23.5 us
    all_gather x1, waiting for transfers between devices, local(): ffn_stack = lax.all_gather(ffn_block, 'dp', axis=0, tiled=False)  18.1 us
    pallas_call x1, Pallas kernels, attend_call(): pl.pallas_call(attend_kernel, name='attend', grid=(windows, tiles), in_sp...  15.9 us
    reduce_scatter x1, waiting for transfers between devices, local(): lax.psum_scatter(wide_blocks, 'dp', scatter_dimension=0, tiled=False)  12.8 us
    pallas_call x1, Pallas kernels, back_call(): pl.pallas_call(back_kernel, name='attend_back', grid=(windows,), in_specs...  9.49 us
  transfers between devices with their start and end apart: 40, of which 14 were waited for; matrix products, arithmetic and copies ran while one was open for 11% of the time, Pallas kernels for 34%

profile of v2, /device:TPU:0, one launch (start us, length us, event | category | flops | bytes accessed | tf_op | source)
XLA Modules:
  0.0 304.6 jit_solution(4725358401875071567)
XLA Ops:
  10.9 3.0 collective-permute-start.1
  14.2 1.6 collective-permute-start.4
  15.9 2.6 collective-permute-start.6
  18.7 1.5 collective-permute-start.3
  20.2 3.2 %fusion.4 = (f32[1024,32]{1,0:T(8,128)}, f32[1024,32]{1,0:T(8,128)}, f32[1024,32]{1,0:T(8,128)}) fusion(f32[32]{0:T(128)S(1)} %multiply_power_fusion, f32[1024]{0:T(1024)S(1)} %iota_convert_fusion), kind=kLoop, calls=%fused_computation.24 | loop fusion | flops 65536 | bytes 397440 | tf_op jit(solution)/shard_map/neg | solution.py:77
  23.4 4.2 %pad_maximum_fusion.1 = (f32[1024,128]{1,0:T(8,128)}, f32[1024,128]{1,0:T(8,128)}) fusion(f32[1024,32]{1,0:T(8,128)} %get-tuple-element.347, f32[1024,32]{1,0:T(8,128)} %get-tuple-element.346, f32[1024,32]{1,0:T(8,128)} %get-tuple-element.345), kind=kLoop, calls=%fused_computation.13 | loop fusion | flops 786432 | bytes 1441792 | tf_op jit(solution)/shard_map/concatenate | solution.py:76
  27.6 3.6 %collective-permute-done.4.refs_2_ = bf16[528,256]{1,0:T(8,128)(2,1)S(1)} collective-permute-done((bf16[528,256]{1,0:T(8,128)(2,1)S(1)}, bf16[528,256]{1,0:T(8,128)(2,1)S(1)}, u32[]{:S(2)}, u32[]{:S(2)}) %collective-permute-start.4) | collective-permute-done | bytes 270368 | tf_op jit(solution)/shard_map/ppermute | solution.py:53
  31.3 1.5 collective-permute-start.5
  32.8 9.6 %collective-permute-done.6.refs_4_ = bf16[528,256]{1,0:T(8,128)(2,1)S(1)} collective-permute-done((bf16[528,256]{1,0:T(8,128)(2,1)S(1)}, bf16[528,256]{1,0:T(8,128)(2,1)S(1)}, u32[]{:S(2)}, u32[]{:S(2)}) %collective-permute-start.6) | collective-permute-done | bytes 270368 | tf_op jit(solution)/shard_map/ppermute | solution.py:53
  43.9 2.4 collective-permute-done.8.refs_6_
  46.3 1.5 collective-permute-start.9
  50.7 2.9 collective-permute-done.9.refs_7_
  53.6 2.0 place_attention.1
  58.9 2.0 copy-done.24
  60.9 8.3 %qkv.1 = (bf16[3,2048,256]{2,1,0:T(8,128)(2,1)S(1)}, bf16[2048,1024]{1,0:T(8,128)(2,1)S(1)}, f32[2048,1]{1,0:T(8,128)S(1)}, bf16[320,1024]{1,0:T(8,128)(2,1)S(1)}, bf16[320,256]{1,0:T(8,128)(2,1)S(1)}) custom-call(bf16[2048,256]{1,0:T(8,128)(2,1)S(1)} %copy-done.9, bf16[2048,256]{1,0:T(8,128)(2,1)S(1)} %collective-permute-done.x1, ...), custom_call_target="tpu_custom_call" | custom-call | flops 1000 | bytes 1000 | tf_op jit(solution)/shard_map/qkv/pallas_call | solution.py:226
  70.3 15.9 %attend.1 = (bf16[2048,256]{1,0:T(8,128)(2,1)}, bf16[320,256]{1,0:T(8,128)(2,1)S(1)}) custom-call(bf16[3,2048,256]{2,1,0:T(8,128)(2,1)S(1)} %get-tuple-element.184.q_ref.k_ref.v_ref.a_ref, bf16[3,2048,256]{2,1,0:T(8,128)(2,1)S(1)} %get-tuple-element.184.q_ref.k_ref.v_ref.a_ref, bf16[3,2048,256]{2,1,0:T(8,128)(2,1)S(1)} %get-tuple-element.184.q_ref.k_ref.v_ref.a_ref, ...), custom_call_target="tpu_custom_call" | custom-call | flops 1000 | bytes 1000 | tf_op jit(solution)/shard_map/attend/pallas_call | solution.py:297
  87.6 2.0 collective-permute-start.12
  89.8 5.2 %collective-permute-done.12 = bf16[640,256]{1,0:T(8,128)(2,1)} collective-permute-done((bf16[640,256]{1,0:T(8,128)(2,1)}, bf16[640,256]{1,0:T(8,128)(2,1)}, u32[]{:S(2)}, u32[]{:S(2)}) %collective-permute-start.12) | collective-permute-done | bytes 327712 | tf_op jit(solution)/shard_map/ppermute | solution.py:53
  99.2 2.0 collective-permute-start.18
  109.2 1.5 convert_multiply_fusion
  110.7 18.1 %all-gather.3.cloned.1.call-done = bf16[24,128,1024]{2,1,0:T(8,128)(2,1)} async-done(((bf16[3,128,1024]{2,1,0:T(8,128)(2,1)}), bf16[24,128,1024]{2,1,0:T(8,128)(2,1)}) %all-gather.3.cloned.1.call-update) | async-done | bytes 6291472 | tf_op jit(solution)/shard_map/all_gather | solution.py:966
  128.7 2.8 copy-done.12
  131.5 2.8 place_feed_forward.1
  134.4 8.7 %masked_rows.1 = (bf16[320,1024]{1,0:T(8,128)(2,1)S(1)}, bf16[320,1024]{1,0:T(8,128)(2,1)S(1)}, bf16[320,1024]{1,0:T(8,128)(2,1)S(1)}, bf16[320,512]{1,0:T(8,128...) custom-call(bf16[320,1024]{1,0:T(8,128)(2,1)S(1)} %copy-done.31, bf16[320,1024]{1,0:T(8,128)(2,1)S(1)} %copy-done.13, ...), custom_call_target="tpu_custom_call" | custom-call | flops 1000 | bytes 1000 | tf_op jit(solution)/shard_map/masked_rows/pallas_call | solution.py:463
  153.2 2.9 pack_wide.1
  156.2 2.0 copy-done.3
  163.5 2.3 pack_down.1
  168.6 3.0 collective-permute-done.17
  178.4 9.5 %attend_back.1 = (bf16[2048,768]{1,0:T(8,128)(2,1)S(1)}, f32[1,2048]{1,0:T(1,128)S(1)}) custom-call(bf16[320,256]{1,0:T(8,128)(2,1)S(1)} %copy-done.76, bf16[320,256]{1,0:T(8,128)(2,1)S(1)} %get-tuple-element.206.do_ref, bf16[3,2048,256]{2,1,0:T(8,128)(2,1)S(1)} %get-tuple-element.184.q_ref.k_ref.v_ref.a_ref, ...), custom_call_target="tpu_custom_call" | custom-call | flops 1000 | bytes 1000 | tf_op jit(solution)/shard_map/attend_back/pallas_call | solution.py:710
  188.4 3.9 %first_grad.1 = (bf16[2048,512]{1,0:T(8,128)(2,1)S(1)}, bf16[2048,256]{1,0:T(8,128)(2,1)S(1)}, bf16[2048,256]{1,0:T(8,128)(2,1)S(1)}) custom-call(bf16[2048,768]{1,0:T(8,128)(2,1)S(1)} %get-tuple-element.219.d_ref, bf16[4,256,1024]{2,1,0:T(8,128)(2,1)S(1)} %copy-done.7), custom_call_target="tpu_custom_call" | custom-call | flops 1000 | bytes 1000 | tf_op jit(solution)/shard_map/first_grad/pallas_call | solution.py:751
  192.4 9.2 %collective-permute-done.23.recv_ref = bf16[4,128,1024]{2,1,0:T(8,128)(2,1)} collective-permute-done((bf16[4,128,1024]{2,1,0:T(8,128)(2,1)}, bf16[4,128,1024]{2,1,0:T(8,128)(2,1)}, u32[]{:S(2)}, u32[]{:S(2)}) %collective-permute-start.23) | collective-permute-done | bytes 1048608 | tf_op jit(solution)/shard_map/ppermute | solution.py:53
  203.2 6.8 %pack_attention.1 = (bf16[4,144,1024]{2,1,0:T(8,128)(2,1)S(1)}, bf16[4,144,1024]{2,1,0:T(8,128)(2,1)S(1)}) custom-call(s32[8]{0:T(128)S(1)} %pad_add_fusion.pos_ref, bf16[2048,1024]{1,0:T(8,128)(2,1)S(1)} %copy-done.28, bf16[2048,768]{1,0:T(8,128)(2,1)S(1)} %get-tuple-element.219.d_ref, bf16[320,1024]{1,0:T(8,128)(2,1)S(1)} %get-tuple-element.220.seed_ref, ...), custom_call_target="tpu_custom_call" | custom-call | flops 1000 | bytes 1000 | tf_op jit(solution)/shard_map/pack_attention/pallas_call | solution.py:613
  210.5 2.1 collective-permute-start.30
  212.5 1.8 collective-permute-start.28
  214.4 2.6 collective-permute-start.29
  217.0 23.5 %feed_forward.1 = (bf16[2048,512]{1,0:T(8,128)(2,1)}, bf16[2048,256]{1,0:T(8,128)(2,1)S(1)}, bf16[2048,256]{1,0:T(8,128)(2,1)S(1)}, f32[2048,256]{1,0:T(8,128)}) custom-call(bf16[2048,256]{1,0:T(8,128)(2,1)S(1)} %copy-done.10, bf16[2048,256]{1,0:T(8,128)(2,1)} %copy-done.25, bf16[2048,256]{1,0:T(8,128)(2,1)} %copy-done.23, bf16[2048,256]{1,0:T(8,128)(2,1)} %copy-done.26, ...), custom_call_target="tpu_custom_call" | custom-call | flops 1000 | bytes 1000 | tf_op jit(solution)/shard_map/feed_forward/pallas_call | solution.py:404
  240.5 7.5 %collective-permute-done.26.recv_ref = bf16[4,144,1024]{2,1,0:T(8,128)(2,1)S(1)} collective-permute-done((bf16[4,144,1024]{2,1,0:T(8,128)(2,1)S(1)}, bf16[4,144,1024]{2,1,0:T(8,128)(2,1)S(1)}, u32[]{:S(2)}, u32[]{:S(2)}) %collective-permute-start.26) | collective-permute-done | bytes 1179680 | tf_op jit(solution)/shard_map/ppermute | solution.py:53
  249.2 2.4 adam_down.1
  252.3 2.2 convert_add_fusion
  254.5 2.0 collective-permute-start.32
  257.0 1.8 collective-permute-start.34
  258.8 2.1 collective-permute-start.35
  261.0 4.4 %input_grad.1 = bf16[2048,256]{1,0:T(8,128)(2,1)} custom-call(bf16[2048,256]{1,0:T(8,128)(2,1)S(1)} %copy-done.10, f32[2048,1]{1,0:T(8,128)S(1)} %copy-done.53, f32[1,2048]{1,0:T(1,128)S(1)} %add.101.dot_ref, bf16[2048,256]{1,0:T(8,128)(2,1)S(1)} %get-tuple-element.284.keep_ref, bf16[2048,256]{1,0:T(8,128)(2,1)S(1)} %slice.120.near_ref, ...), custom_call_target="tpu_custom_call" | custom-call | flops 1000 | bytes 1000 | tf_op jit(solution)/shard_map/input_grad/pallas_call | solution.py:789
  265.4 12.8 %reduce-scatter.2.cloned.1.call-done = bf16[1,128,2048]{2,1,0:T(8,128)(2,1)} async-done(((bf16[8,128,2048]{2,1,0:T(8,128)(2,1)}), bf16[1,128,2048]{2,1,0:T(8,128)(2,1)}) %reduce-scatter.2.cloned.1.call-update) | async-done | bytes 524304 | tf_op jit(solution)/shard_map/reduce_scatter | solution.py:1023
  282.8 3.4 %adam_gate_up.1 = (f32[2,128,1024]{2,1,0:T(8,128)}, f32[2,128,1024]{2,1,0:T(8,128)}, f32[2,128,1024]{2,1,0:T(8,128)}, f32[2,128,1024]{2,1,0:T(8,128)}, f32[2,128...) custom-call(bf16[128,2048]{1,0:T(8,128)(2,1)S(1)} %bitcast.28, f32[2,128,1024]{2,1,0:T(8,128)S(1)} %copy-done.29, ...), custom_call_target="tpu_custom_call" | custom-call | tf_op jit(solution)/shard_map/adam_gate_up/pallas_call | solution.py:849
  286.3 1.6 collective-permute-done.35.refs_3_
  287.9 2.3 adam_qkv.1
  290.5 2.6 add_convert_fusion
  (325 shorter events, 65.9 us)
Async XLA Ops:
  7.2 121.5 %all-gather.3.cloned.1.call-start = ((), (), s32[]{:S(2)}) async-start(), calls=%async_computation.2 | async-start | bytes 7077888 | tf_op jit(solution)/shard_map/all_gather | solution.py:966
  10.9 267.2 %reduce-scatter.2.cloned.1.call-start = ((), (), s32[]{:S(2)}) async-start(), calls=%async_computation.1 | async-start | bytes 4718592 | tf_op jit(solution)/shard_map/reduce_scatter | solution.py:1023
  10.9 38.2 %collective-permute-start.1 = (bf16[2048,256]{1,0:T(8,128)(2,1)S(1)}, bf16[2048,256]{1,0:T(8,128)(2,1)S(1)}, u32[]{:S(2)}, u32[]{:S(2)}) collective-permute-start(bf16[2048,256]{1,0:T(8,128)(2,1)S(1)} %copy-done.8), channel_id=1, source_target_pairs={{0,2},{1,3},{2,0},{3,1},{4,6},{5,7},{6,4},{7,5},{8,10},{9,11},{10,... | collective-permute-start | bytes 3145736 | tf_op jit(solution)/shard_map/ppermute | solution.py:53
  14.2 17.0 %collective-permute-start.4 = (bf16[528,256]{1,0:T(8,128)(2,1)S(1)}, bf16[528,256]{1,0:T(8,128)(2,1)S(1)}, u32[]{:S(2)}, u32[]{:S(2)}) collective-permute-start(bf16[528,256]{1,0:T(8,128)(2,1)S(1)} %constant_dynamic-update-slice_fusion.refs_0_), channel_id=1, source_target_pairs={{0,8},{4,12},{8,0},{12,4},{16,24},{20,28},{24,16},{28,20},{1,9},{5... | collective-permute-start | bytes 811016 | tf_op jit(solution)/shard_map/ppermute | solution.py:53
  15.9 26.5 %collective-permute-start.6 = (bf16[528,256]{1,0:T(8,128)(2,1)S(1)}, bf16[528,256]{1,0:T(8,128)(2,1)S(1)}, u32[]{:S(2)}, u32[]{:S(2)}) collective-permute-start(bf16[528,256]{1,0:T(8,128)(2,1)S(1)} %constant_dynamic-update-slice_fusion.refs_0_), channel_id=1, source_target_pairs={{0,16},{4,20},{8,24},{12,28},{16,0},{20,4},{24,8},{28,12},{1,17},{... | collective-permute-start | bytes 811016 | tf_op jit(solution)/shard_map/ppermute | solution.py:53
  18.5 27.9 %collective-permute-start.8 = (bf16[528,256]{1,0:T(8,128)(2,1)S(1)}, bf16[528,256]{1,0:T(8,128)(2,1)}, u32[]{:S(2)}, u32[]{:S(2)}) collective-permute-start(bf16[528,256]{1,0:T(8,128)(2,1)S(1)} %constant_dynamic-update-slice_fusion.refs_0_), channel_id=1, source_target_pairs={{0,24},{4,28},{8,16},{12,20},{16,8},{20,12},{24,0},{28,4},{1,25},{... | collective-permute-start | bytes 811016 | tf_op jit(solution)/shard_map/ppermute | solution.py:53
  18.7 30.4 %collective-permute-start.3 = (bf16[528,256]{1,0:T(8,128)(2,1)S(1)}, bf16[528,256]{1,0:T(8,128)(2,1)}, u32[]{:S(2)}, u32[]{:S(2)}) collective-permute-start(bf16[528,256]{1,0:T(8,128)(2,1)S(1)} %constant_dynamic-update-slice_fusion.refs_0_), channel_id=1, source_target_pairs={{0,4},{4,0},{8,12},{12,8},{16,20},{20,16},{24,28},{28,24},{1,5},{5... | collective-permute-start | bytes 811016 | tf_op jit(solution)/shard_map/ppermute | solution.py:53
  20.2 27.6 %copy-start.101 = (s32[8]{0:T(128)S(1)}, s32[8]{0:T(128)}, u32[]{:S(2)}) copy-start(s32[8]{0:T(128)} %param.31) | copy-start | bytes 100
  20.2 28.8 %copy-start.103 = (s32[16]{0:T(128)S(1)}, s32[16]{0:T(128)}, u32[]{:S(2)}) copy-start(s32[16]{0:T(128)} %param.30) | copy-start | bytes 196
  31.3 18.4 %collective-permute-start.5 = (bf16[528,256]{1,0:T(8,128)(2,1)S(1)}, bf16[528,256]{1,0:T(8,128)(2,1)}, u32[]{:S(2)}, u32[]{:S(2)}) collective-permute-start(bf16[528,256]{1,0:T(8,128)(2,1)S(1)} %collective-permute-done.4.refs_2_), channel_id=1, source_target_pairs={{0,4},{4,0},{8,12},{12,8},{16,20},{20,16},{24,28},{28,24},{1,5},{5... | collective-permute-start | bytes 811016 | tf_op jit(solution)/shard_map/ppermute | solution.py:53
  42.4 8.3 %collective-permute-start.7 = (bf16[528,256]{1,0:T(8,128)(2,1)S(1)}, bf16[528,256]{1,0:T(8,128)(2,1)}, u32[]{:S(2)}, u32[]{:S(2)}) collective-permute-start(bf16[528,256]{1,0:T(8,128)(2,1)S(1)} %collective-permute-done.6.refs_4_), channel_id=1, source_target_pairs={{0,4},{4,0},{8,12},{12,8},{16,20},{20,16},{24,28},{28,24},{1,5},{5... | collective-permute-start | bytes 811016 | tf_op jit(solution)/shard_map/ppermute | solution.py:53
  46.3 7.3 %collective-permute-start.9 = (bf16[528,256]{1,0:T(8,128)(2,1)}, bf16[528,256]{1,0:T(8,128)(2,1)}, u32[]{:S(2)}, u32[]{:S(2)}) collective-permute-start(bf16[528,256]{1,0:T(8,128)(2,1)} %collective-permute-done.8.refs_6_), channel_id=1, source_target_pairs={{0,4},{4,0},{8,12},{12,8},{16,20},{20,16},{24,28},{28,24},{1,5},{5... | collective-permute-start | bytes 811016 | tf_op jit(solution)/shard_map/ppermute | solution.py:53
  49.0 37.1 %copy-start.85 = (bf16[2,160,256]{2,1,0:T(8,128)(2,1)}, bf16[2,160,256]{2,1,0:T(8,128)(2,1)S(1)}, u32[]{:S(2)}) copy-start(bf16[2,160,256]{2,1,0:T(8,128)(2,1)S(1)} %pad.15) | copy-start | bytes 491524
  49.0 9.7 %collective-permute-start = (bf16[2048,256]{1,0:T(8,128)(2,1)S(1)}, bf16[2048,256]{1,0:T(8,128)(2,1)S(1)}, u32[]{:S(2)}, u32[]{:S(2)}) collective-permute-start(bf16[2048,256]{1,0:T(8,128)(2,1)S(1)} %copy-done.8), channel_id=1, source_target_pairs={{0,1},{1,0},{2,3},{3,2},{4,5},{5,4},{6,7},{7,6},{8,9},{9,8},{10,11... | collective-permute-start | bytes 3145736 | tf_op jit(solution)/shard_map/ppermute | solution.py:53
  49.1 9.6 %collective-permute-start.2 = (bf16[2048,256]{1,0:T(8,128)(2,1)S(1)}, bf16[2048,256]{1,0:T(8,128)(2,1)S(1)}, u32[]{:S(2)}, u32[]{:S(2)}) collective-permute-start(bf16[2048,256]{1,0:T(8,128)(2,1)S(1)} %collective-permute-done.1.x2), channel_id=1, source_target_pairs={{0,1},{1,0},{2,3},{3,2},{4,5},{5,4},{6,7},{7,6},{8,9},{9,8},{10,11... | collective-permute-start | bytes 3145736 | tf_op jit(solution)/shard_map/ppermute | solution.py:53
  57.9 12.3 %collective-permute-start.10 = (bf16[256,1024]{1,0:T(8,128)(2,1)S(1)}, bf16[256,1024]{1,0:T(8,128)(2,1)S(1)}, u32[]{:S(2)}, u32[]{:S(2)}) collective-permute-start(bf16[256,1024]{1,0:T(8,128)(2,1)S(1)} %slice_bitcast_fusion.o0), channel_id=1, source_target_pairs={{0,2},{1,3},{2,0},{3,1},{4,6},{5,7},{6,4},{7,5},{8,10},{9,11},{10,... | collective-permute-start | bytes 1572872 | tf_op jit(solution)/shard_map/ppermute | solution.py:53
  70.2 15.9 %copy-start.75 = (bf16[320,256]{1,0:T(8,128)(2,1)}, bf16[320,256]{1,0:T(8,128)(2,1)S(1)}, u32[]{:S(2)}) copy-start(bf16[320,256]{1,0:T(8,128)(2,1)S(1)} %get-tuple-element.181.q_ref) | copy-start | bytes 491524
  70.2 19.3 %copy-start.100 = (s32[2]{0:T(128)S(1)}, s32[2]{0:T(128)}, u32[]{:S(2)}) copy-start(s32[2]{0:T(128)} %param.29) | copy-start | bytes 28
  70.2 19.5 %copy-start.102 = (s32[8]{0:T(128)S(1)}, s32[8]{0:T(128)}, u32[]{:S(2)}) copy-start(s32[8]{0:T(128)} %param.31) | copy-start | bytes 100
  70.2 24.7 %copy-start.104 = (s32[16]{0:T(128)S(1)}, s32[16]{0:T(128)}, u32[]{:S(2)}) copy-start(s32[16]{0:T(128)} %param.30) | copy-start | bytes 196
  87.6 7.4 %collective-permute-start.12 = (bf16[640,256]{1,0:T(8,128)(2,1)}, bf16[640,256]{1,0:T(8,128)(2,1)}, u32[]{:S(2)}, u32[]{:S(2)}) collective-permute-start(bf16[640,256]{1,0:T(8,128)(2,1)} %pad_maximum_fusion.3), channel_id=1, source_target_pairs={{0,2},{1,3},{2,0},{3,1},{4,6},{5,7},{6,4},{7,5},{8,10},{9,11},{10,... | collective-permute-start | bytes 983048 | tf_op jit(solution)/shard_map/ppermute | solution.py:53
  95.0 4.3 %collective-permute-start.13 = (bf16[640,256]{1,0:T(8,128)(2,1)}, bf16[640,256]{1,0:T(8,128)(2,1)}, u32[]{:S(2)}, u32[]{:S(2)}) collective-permute-start(bf16[640,256]{1,0:T(8,128)(2,1)} %collective-permute-done.12), channel_id=1, source_target_pairs={{0,1},{1,0},{2,3},{3,2},{4,5},{5,4},{6,7},{7,6},{8,9},{9,8},{10,11... | collective-permute-start | bytes 983048 | tf_op jit(solution)/shard_map/ppermute | solution.py:53
  95.6 6.7 %collective-permute-start.11 = (bf16[640,256]{1,0:T(8,128)(2,1)}, bf16[640,256]{1,0:T(8,128)(2,1)}, u32[]{:S(2)}, u32[]{:S(2)}) collective-permute-start(bf16[640,256]{1,0:T(8,128)(2,1)} %pad_maximum_fusion.3), channel_id=1, source_target_pairs={{0,1},{1,0},{2,3},{3,2},{4,5},{5,4},{6,7},{7,6},{8,9},{9,8},{10,11... | collective-permute-start | bytes 983048 | tf_op jit(solution)/shard_map/ppermute | solution.py:53
  98.7 5.6 %collective-permute-start.14 = (bf16[256,1024]{1,0:T(8,128)(2,1)}, bf16[256,1024]{1,0:T(8,128)(2,1)S(1)}, u32[]{:S(2)}, u32[]{:S(2)}) collective-permute-start(bf16[256,1024]{1,0:T(8,128)(2,1)} %copy-done.20), channel_id=1, source_target_pairs={{0,1},{1,0},{2,3},{3,2},{4,5},{5,4},{6,7},{7,6},{8,9},{9,8},{10,11... | collective-permute-start | bytes 1572872 | tf_op jit(solution)/shard_map/ppermute | solution.py:53
  98.7 5.6 %collective-permute-start.15 = (bf16[256,1024]{1,0:T(8,128)(2,1)}, bf16[256,1024]{1,0:T(8,128)(2,1)S(1)}, u32[]{:S(2)}, u32[]{:S(2)}) collective-permute-start(bf16[256,1024]{1,0:T(8,128)(2,1)} %copy-done.33), channel_id=1, source_target_pairs={{0,1},{1,0},{2,3},{3,2},{4,5},{5,4},{6,7},{7,6},{8,9},{9,8},{10,11... | collective-permute-start | bytes 1572872 | tf_op jit(solution)/shard_map/ppermute | solution.py:53
  99.2 47.7 %collective-permute-start.18 = (bf16[2048,256]{1,0:T(8,128)(2,1)}, bf16[2048,256]{1,0:T(8,128)(2,1)}, u32[]{:S(2)}, u32[]{:S(2)}) collective-permute-start(bf16[2048,256]{1,0:T(8,128)(2,1)} %get-tuple-element.237.c0), channel_id=1, source_target_pairs={{0,2},{1,3},{2,0},{3,1},{4,6},{5,7},{6,4},{7,5},{8,10},{9,11},{10,... | collective-permute-start | bytes 3145736 | tf_op jit(solution)/shard_map/ppermute | solution.py:53
  146.9 11.2 %collective-permute-start.16 = (bf16[320,512]{1,0:T(8,128)(2,1)}, bf16[320,512]{1,0:T(8,128)(2,1)}, u32[]{:S(2)}, u32[]{:S(2)}) collective-permute-start(bf16[320,512]{1,0:T(8,128)(2,1)} %get-tuple-element.191), channel_id=1, source_target_pairs={{0,1},{1,0},{2,3},{3,2},{4,5},{5,4},{6,7},{7,6},{8,9},{9,8},{10,11... | collective-permute-start | bytes 983048 | tf_op jit(solution)/shard_map/ppermute | solution.py:53
  146.9 24.7 %collective-permute-start.19 = (bf16[2048,256]{1,0:T(8,128)(2,1)}, bf16[2048,256]{1,0:T(8,128)(2,1)}, u32[]{:S(2)}, u32[]{:S(2)}) collective-permute-start(bf16[2048,256]{1,0:T(8,128)(2,1)} %get-tuple-element.237.c0), channel_id=1, source_target_pairs={{0,1},{1,0},{2,3},{3,2},{4,5},{5,4},{6,7},{7,6},{8,9},{9,8},{10,11... | collective-permute-start | bytes 3145736 | tf_op jit(solution)/shard_map/ppermute | solution.py:53
  147.4 24.2 %collective-permute-start.20 = (bf16[2048,256]{1,0:T(8,128)(2,1)}, bf16[2048,256]{1,0:T(8,128)(2,1)}, u32[]{:S(2)}, u32[]{:S(2)}) collective-permute-start(bf16[2048,256]{1,0:T(8,128)(2,1)} %collective-permute-done.18.c2), channel_id=1, source_target_pairs={{0,1},{1,0},{2,3},{3,2},{4,5},{5,4},{6,7},{7,6},{8,9},{9,8},{10,11... | collective-permute-start | bytes 3145736 | tf_op jit(solution)/shard_map/ppermute | solution.py:53
  161.2 10.4 %collective-permute-start.17 = (bf16[320,512]{1,0:T(8,128)(2,1)}, bf16[320,512]{1,0:T(8,128)(2,1)}, u32[]{:S(2)}, u32[]{:S(2)}) collective-permute-start(bf16[320,512]{1,0:T(8,128)(2,1)} %pad_maximum_fusion.4), channel_id=1, source_target_pairs={{0,2},{1,3},{2,0},{3,1},{4,6},{5,7},{6,4},{7,5},{8,10},{9,11},{10,... | collective-permute-start | bytes 983048 | tf_op jit(solution)/shard_map/ppermute | solution.py:53
  166.7 34.8 %collective-permute-start.23 = (bf16[4,128,1024]{2,1,0:T(8,128)(2,1)}, bf16[4,128,1024]{2,1,0:T(8,128)(2,1)}, u32[]{:S(2)}, u32[]{:S(2)}) collective-permute-start(bf16[4,128,1024]{2,1,0:T(8,128)(2,1)} %get-tuple-element.202), channel_id=1, source_target_pairs={{0,4},{4,0},{8,12},{12,8},{16,20},{20,16},{24,28},{28,24},{1,5},{5... | collective-permute-start | bytes 3145736 | tf_op jit(solution)/shard_map/ppermute | solution.py:53
  173.8 1.8 collective-permute-start.21
  187.9 15.1 %collective-permute-start.22 = (f32[1,2048]{1,0:T(1,128)S(1)}, f32[1,2048]{1,0:T(1,128)S(1)}, u32[]{:S(2)}, u32[]{:S(2)}) collective-permute-start(f32[1,2048]{1,0:T(1,128)S(1)} %get-tuple-element.210), channel_id=1, source_target_pairs={{0,1},{1,0},{2,3},{3,2},{4,5},{5,4},{6,7},{7,6},{8,9},{9,8},{10,11... | collective-permute-start | bytes 24584 | tf_op jit(solution)/shard_map/ppermute | solution.py:53
  203.0 7.1 %collective-permute-start.24 = (bf16[2048,512]{1,0:T(8,128)(2,1)S(1)}, bf16[2048,512]{1,0:T(8,128)(2,1)S(1)}, u32[]{:S(2)}, u32[]{:S(2)}) collective-permute-start(bf16[2048,512]{1,0:T(8,128)(2,1)S(1)} %get-tuple-element.216), channel_id=1, source_target_pairs={{0,1},{1,0},{2,3},{3,2},{4,5},{5,4},{6,7},{7,6},{8,9},{9,8},{10,11... | collective-permute-start | bytes 6291464 | tf_op jit(solution)/shard_map/ppermute | solution.py:53
  203.1 7.0 %collective-permute-start.25 = (f32[1,2048]{1,0:T(1,128)S(1)}, f32[1,2048]{1,0:T(1,128)S(1)}, u32[]{:S(2)}, u32[]{:S(2)}) collective-permute-start(f32[1,2048]{1,0:T(1,128)S(1)} %add.96), channel_id=1, source_target_pairs={{0,2},{1,3},{2,0},{3,1},{4,6},{5,7},{6,4},{7,5},{8,10},{9,11},{10,... | collective-permute-start | bytes 24584 | tf_op jit(solution)/shard_map/ppermute | solution.py:53
  210.4 37.6 %collective-permute-start.26 = (bf16[4,144,1024]{2,1,0:T(8,128)(2,1)S(1)}, bf16[4,144,1024]{2,1,0:T(8,128)(2,1)S(1)}, u32[]{:S(2)}, u32[]{:S(2)}) collective-permute-start(bf16[4,144,1024]{2,1,0:T(8,128)(2,1)S(1)} %get-tuple-element.245), channel_id=1, source_target_pairs={{0,4},{4,0},{8,12},{12,8},{16,20},{20,16},{24,28},{28,24},{1,5},{5... | collective-permute-start | bytes 3538952 | tf_op jit(solution)/shard_map/ppermute | solution.py:53
  210.5 30.0 %collective-permute-start.30 = (bf16[2048,256]{1,0:T(8,128)(2,1)S(1)}, bf16[2048,256]{1,0:T(8,128)(2,1)S(1)}, u32[]{:S(2)}, u32[]{:S(2)}) collective-permute-start(bf16[2048,256]{1,0:T(8,128)(2,1)S(1)} %add_convert_fusion.2), channel_id=1, source_target_pairs={{0,2},{1,3},{2,0},{3,1},{4,6},{5,7},{6,4},{7,5},{8,10},{9,11},{10,... | collective-permute-start | bytes 3145736 | tf_op jit(solution)/shard_map/ppermute | solution.py:53
  212.5 27.9 %collective-permute-start.27 = (bf16[128,1024]{1,0:T(8,128)(2,1)S(1)}, bf16[128,1024]{1,0:T(8,128)(2,1)S(1)}, u32[]{:S(2)}, u32[]{:S(2)}) collective-permute-start(bf16[128,1024]{1,0:T(8,128)(2,1)S(1)} %get-tuple-element.247), channel_id=1, source_target_pairs={{0,8},{4,12},{8,0},{12,4},{16,24},{20,28},{24,16},{28,20},{1,9},{5... | collective-permute-start | bytes 786440 | tf_op jit(solution)/shard_map/ppermute | solution.py:53
  212.5 27.9 %collective-permute-start.28 = (bf16[128,1024]{1,0:T(8,128)(2,1)S(1)}, bf16[128,1024]{1,0:T(8,128)(2,1)S(1)}, u32[]{:S(2)}, u32[]{:S(2)}) collective-permute-start(bf16[128,1024]{1,0:T(8,128)(2,1)S(1)} %get-tuple-element.248), channel_id=1, source_target_pairs={{0,16},{4,20},{8,24},{12,28},{16,0},{20,4},{24,8},{28,12},{1,17},{... | collective-permute-start | bytes 786440 | tf_op jit(solution)/shard_map/ppermute | solution.py:53
  214.4 26.1 %collective-permute-start.29 = (bf16[128,1024]{1,0:T(8,128)(2,1)S(1)}, bf16[128,1024]{1,0:T(8,128)(2,1)S(1)}, u32[]{:S(2)}, u32[]{:S(2)}) collective-permute-start(bf16[128,1024]{1,0:T(8,128)(2,1)S(1)} %get-tuple-element.249), channel_id=1, source_target_pairs={{0,24},{4,28},{8,16},{12,20},{16,8},{20,12},{24,0},{28,4},{1,25},{... | collective-permute-start | bytes 786440 | tf_op jit(solution)/shard_map/ppermute | solution.py:53
  248.0 4.4 %collective-permute-start.31 = (bf16[2048,512]{1,0:T(8,128)(2,1)}, bf16[2048,512]{1,0:T(8,128)(2,1)S(1)}, u32[]{:S(2)}, u32[]{:S(2)}) collective-permute-start(bf16[2048,512]{1,0:T(8,128)(2,1)} %get-tuple-element.252), channel_id=1, source_target_pairs={{0,1},{1,0},{2,3},{3,2},{4,5},{5,4},{6,7},{7,6},{8,9},{9,8},{10,11... | collective-permute-start | bytes 6291464 | tf_op jit(solution)/shard_map/ppermute | solution.py:53
  254.5 33.4 %collective-permute-start.32 = (bf16[2048,256]{1,0:T(8,128)(2,1)}, bf16[2048,256]{1,0:T(8,128)(2,1)}, u32[]{:S(2)}, u32[]{:S(2)}) collective-permute-start(bf16[2048,256]{1,0:T(8,128)(2,1)} %get-tuple-element.277), channel_id=1, source_target_pairs={{0,2},{1,3},{2,0},{3,1},{4,6},{5,7},{6,4},{7,5},{8,10},{9,11},{10,... | collective-permute-start | bytes 3145736 | tf_op jit(solution)/shard_map/ppermute | solution.py:53
  256.5 29.8 %collective-permute-start.33 = (bf16[144,1024]{1,0:T(8,128)(2,1)}, bf16[144,1024]{1,0:T(8,128)(2,1)S(1)}, u32[]{:S(2)}, u32[]{:S(2)}) collective-permute-start(bf16[144,1024]{1,0:T(8,128)(2,1)} %get-tuple-element.279), channel_id=1, source_target_pairs={{0,8},{4,12},{8,0},{12,4},{16,24},{20,28},{24,16},{28,20},{1,9},{5... | collective-permute-start | bytes 884744 | tf_op jit(solution)/shard_map/ppermute | solution.py:53
  257.0 29.3 %collective-permute-start.34 = (bf16[144,1024]{1,0:T(8,128)(2,1)S(1)}, bf16[144,1024]{1,0:T(8,128)(2,1)S(1)}, u32[]{:S(2)}, u32[]{:S(2)}) collective-permute-start(bf16[144,1024]{1,0:T(8,128)(2,1)S(1)} %get-tuple-element.280), channel_id=1, source_target_pairs={{0,16},{4,20},{8,24},{12,28},{16,0},{20,4},{24,8},{28,12},{1,17},{... | collective-permute-start | bytes 884744 | tf_op jit(solution)/shard_map/ppermute | solution.py:53
  258.8 29.1 %collective-permute-start.35 = (bf16[144,1024]{1,0:T(8,128)(2,1)S(1)}, bf16[144,1024]{1,0:T(8,128)(2,1)S(1)}, u32[]{:S(2)}, u32[]{:S(2)}) collective-permute-start(bf16[144,1024]{1,0:T(8,128)(2,1)S(1)} %get-tuple-element.281), channel_id=1, source_target_pairs={{0,24},{4,28},{8,16},{12,20},{16,8},{20,12},{24,0},{28,4},{1,25},{... | collective-permute-start | bytes 884744 | tf_op jit(solution)/shard_map/ppermute | solution.py:53
  261.0 17.1 %copy-start.29 = (f32[2,128,1024]{2,1,0:T(8,128)S(1)}, f32[2,128,1024]{2,1,0:T(8,128)}, u32[]{:S(2)}) copy-start(f32[2,128,1024]{2,1,0:T(8,128)} %refs_1_.1) | copy-start | bytes 3145732
  290.4 2.7 collective-permute-start.36
  293.1 3.5 %collective-permute-start.37 = (f32[1,128]{1,0:T(1,128)S(1)}, f32[1,128]{1,0:T(1,128)S(1)}, u32[]{:S(2)}, u32[]{:S(2)}) collective-permute-start(f32[1,128]{1,0:T(1,128)S(1)} %bitcast_add_fusion), channel_id=1, source_target_pairs={{0,2},{1,3},{2,0},{3,1},{4,6},{5,7},{6,4},{7,5},{8,10},{9,11},{10,... | collective-permute-start | bytes 1544 | tf_op jit(solution)/shard_map/ppermute | solution.py:53
  (97 other events, 488.7 us)
Sparse Core Ops, SparseCore 0:
  11.0 117.6 all-gather.2
  167.4 110.6 reduce-scatter.1

commit v3 on v2

--- a/solution.py
+++ b/solution.py
@@ -95,7 +95,7 @@
     out, gains = refs[-2:]
     for p, piece in enumerate(refs[:-2]):
         bs = out.shape[1] // (len(refs) - 2)
-        at = pl.multiple_of(pos_ref[p], bs)
+        at = pl.multiple_of(pos_ref[len(refs) - 3 - p], bs)
         for k in range(4):
             out[k, pl.ds(at, bs), :] = piece[k * bs : (k + 1) * bs, :]
         gains[:, pl.ds(at, bs)] = piece[4 * bs : 4 * bs + 16, :bs].astype(F32)[:2, :]
@@ -488,6 +488,83 @@
             flops=1000, bytes_accessed=1000, transcendentals=0
         ),
     )(norm_rows, seed, weights, down)
+
+
+def rows_pack_kernel(pos_ref, n_ref, seed_ref, w_ref, d_ref,
+                     wide_ref, dsend_ref, dkeep_ref, send_ref, keep_ref, far_ref, acc, wide_t, down_t):
+    step = pl.program_id(0)
+
+    @pl.when(step == 0)
+    def _():
+        acc[...] = jnp.zeros_like(acc)
+        wide_t[...] = chosen(n_ref, pos_ref, range(8)).T
+        down_t[...] = chosen(seed_ref, pos_ref, range(8, 16)).T
+
+    norm = n_ref[...]
+    gate = dot(norm, w_ref[0])
+    up = dot(norm, w_ref[1])
+    sigmoid = jax.nn.sigmoid(gate)
+    silu = gate * sigmoid
+    hidden = (silu * up).astype(BF)
+    hidden_grad = dot_t(seed_ref[...], d_ref[...])
+    gate_grad = (hidden_grad * up * sigmoid * (1.0 + gate * (1.0 - sigmoid))).astype(BF)
+    up_grad = (hidden_grad * silu).astype(BF)
+    acc[...] += dot_t(gate_grad, w_ref[0]) + dot_t(up_grad, w_ref[1])
+    left = wide_t[...]
+    part = hidden.shape[1]
+    for k, grad in enumerate((gate_grad, up_grad)):
+        value = dot(left, grad).astype(BF)
+        for b in range(8):
+            wide_ref[b, :, k * part : (k + 1) * part] = value[b * LANES : (b + 1) * LANES]
+    value = dot(down_t[...], hidden).astype(BF)
+    for b in range(8):
+        (dsend_ref, dkeep_ref)[b // 4][b % 4] = value[b * LANES : (b + 1) * LANES]
+
+    @pl.when(step == pl.num_programs(0) - 1)
+    def _():
+        split_chunks(acc[...], send_ref, keep_ref, far_ref)
+
+
+def rows_pack_call(pos, norm_rows, seed, weights, down):
+    rows = norm_rows.shape[0]
+    width = weights.shape[2]
+    share = D // 4
+    part = TALL
+    fixed = lambda shape: pl.BlockSpec(shape, lambda i, pos: (0,) * len(shape))
+    blocks = lambda shape: pl.BlockSpec(shape, lambda i, pos: (0, 0, i))
+    return pl.pallas_call(
+        rows_pack_kernel,
+        name="masked_rows",
+        grid_spec=pltpu.PrefetchScalarGridSpec(
+            num_scalar_prefetch=1,
+            grid=(width // part,),
+            in_specs=[fixed((rows, D)), fixed((rows, D))]
+            + [blocks((2, D, part)), pl.BlockSpec((part, D), lambda i, pos: (i, 0))],
+            out_specs=[
+                blocks((8, LANES, 2 * part)),
+                blocks((4, LANES, part)),
+                blocks((4, LANES, part)),
+                fixed((rows, 2 * share)),
+                fixed((rows, share)),
+                fixed((rows, share)),
+            ],
+            scratch_shapes=[
+                pltpu.VMEM((rows, D), F32),
+                pltpu.VMEM((D, rows), BF),
+                pltpu.VMEM((D, rows), BF),
+            ],
+        ),
+        out_shape=[
+            jax.ShapeDtypeStruct((8, LANES, 2 * width), BF),
+            jax.ShapeDtypeStruct((4, LANES, width), BF),
+            jax.ShapeDtypeStruct((4, LANES, width), BF),
+            jax.ShapeDtypeStruct((rows, 2 * share), BF),
+            jax.ShapeDtypeStruct((rows, share), BF),
+            jax.ShapeDtypeStruct((rows, share), BF),
+        ],
+        compiler_params=params(40),
+        cost_estimate=pl.CostEstimate(flops=1000, bytes_accessed=1000, transcendentals=0),
+    )(pos, norm_rows, seed, weights, down)
 
 
 def seed_kernel(own_ref, near_ref, seed_ref, unit_ref, scale_ref, g_ref, w_ref,
@@ -541,42 +618,6 @@
     )
 
 
-def pack_kernel(halves, rhs_count, pos_ref, lhs_ref, *refs):
-    rhs, outs = refs[:rhs_count], refs[rhs_count:]
-    size = 8 // halves
-    for h, out in enumerate(outs):
-        left = chosen(lhs_ref, pos_ref, range(h * size, (h + 1) * size))
-        at = 0
-        for right in rhs:
-            for start in range(0, right.shape[1], 512):
-                value = dot_l(left, right[:, start : start + 512]).astype(BF)
-                for b in range(size):
-                    out[b, :, at + start : at + start + 512] = value[b * LANES : (b + 1) * LANES]
-            at += right.shape[1]
-
-
-def pack(pos, lhs, rhs, halves, name):
-    rows = lhs.shape[0]
-    n = sum(r.shape[1] for r in rhs)
-    size = 8 // halves
-    zero = lambda i, pos: (0, 0)
-    return pl.pallas_call(
-        functools.partial(pack_kernel, halves, len(rhs)),
-        name="pack_" + name,
-        grid_spec=pltpu.PrefetchScalarGridSpec(
-            num_scalar_prefetch=1,
-            grid=(1,),
-            in_specs=[pl.BlockSpec(a.shape, zero) for a in (lhs, *rhs)],
-            out_specs=[pl.BlockSpec((size, LANES, n), lambda i, pos: (0, 0, 0))] * halves,
-        ),
-        out_shape=[jax.ShapeDtypeStruct((size, LANES, n), BF)] * halves,
-        compiler_params=params(32),
-        cost_estimate=pl.CostEstimate(
-            flops=1000, bytes_accessed=1000, transcendentals=0
-        ),
-    )(pos, lhs, *rhs)
-
-
 def pack_attention_kernel(pos_ref, norm_ref, d_ref, seed_ref, ctx_ref, gain_ref, send_ref, keep_ref, acc):
     step = pl.program_id(0)
     n = d_ref.shape[1]
@@ -634,23 +675,26 @@
     )(pos, norm, dqkv, seed, context_rows, gain)
 
 
-def add_terms_kernel(keep_ref, recv_ref, *outs):
+def add_terms_kernel(parts, keep_ref, *refs):
+    recv, outs = refs[:parts], refs[parts:]
+    size = len(outs) // parts
     for k, out in enumerate(outs):
-        out[...] = (keep_ref[k].astype(F32) + recv_ref[k].astype(F32)).astype(out.dtype)
+        other = recv[k // size][k % size]
+        out[...] = (keep_ref[k].astype(F32) + other.astype(F32)).astype(out.dtype)
 
 
 def add_terms(keep, received, name):
     count, rows, n = keep.shape
-    block = pl.BlockSpec((count, rows, 512), lambda i: (0, 0, i))
-    return pl.pallas_call(
-        add_terms_kernel,
+    block = lambda k: pl.BlockSpec((k, rows, 512), lambda i: (0, 0, i))
+    return pl.pallas_call(
+        functools.partial(add_terms_kernel, len(received)),
         name="add_" + name,
         grid=(n // 512,),
-        in_specs=[block] * 2,
+        in_specs=[block(a.shape[0]) for a in (keep, *received)],
         out_specs=[pl.BlockSpec((rows, 512), lambda i: (0, i))] * count,
         out_shape=[jax.ShapeDtypeStruct((rows, n), F32 if k == 0 else BF) for k in range(count)],
         compiler_params=params(16),
-    )(keep, received)
+    )(keep, *received)
 
 
 def back_kernel(q_ref, do_ref, a_ref, k_ref, v_ref, oh_ref, cosm_ref, sinm_ref, cos_ref, sin_ref,
@@ -840,11 +884,11 @@
         outs[6][...] += part
 
 
-def adam_cols(terms, arrays, rate, name, rows=False):
+def adam_cols(terms, arrays, rate, name, rows=False, mixed=False):
     k, bs, n = arrays[0].shape
-    part = min(n, 512)
+    part = min(n, TALL)
     tiles = n // part
-    term = cut((bs, part), lambda t, j: (0, t * tiles + j))
+    term = cut((bs, part), lambda t, j: (0, j * k + t if mixed else t * tiles + j))
     spot = cut((1, bs, part), lambda t, j: (t, 0, j))
     return pl.pallas_call(
         functools.partial(adam_cols_kernel, len(terms), rate),
@@ -854,7 +898,7 @@
         out_specs=[spot] * 6 + [cut((bs, LANES), lambda t, j: (0, 0))] * rows,
         out_shape=[jax.ShapeDtypeStruct((k, bs, n), BF if i == 5 else F32) for i in range(6)]
         + [jax.ShapeDtypeStruct((bs, LANES), F32)] * rows,
-        compiler_params=params(24),
+        compiler_params=params(60 if mixed else 24),
     )(*terms, *arrays)
 
 
@@ -953,7 +997,7 @@
         order = [None] * 8
         for k in range(4):
             order[2 * k], order[2 * k + 1] = z_pieces[k], x_pieces[k]
-        attn_w, gains = place_pieces(pos_x, order, block)
+        attn_w, gains = place_pieces(pos_x, order[::-1], block)
         gains = gains.reshape(2, 1, D)
     else:
         attn_block = jnp.stack(attn_block).astype(BF)
@@ -1004,9 +1048,15 @@
     else:
         wide_w = place_stack(pos, ffn_stack)
         wide_w, down_w = wide_w[:2], wide_w[2].T
-    hidden_rows, gate_grad, up_grad, n2_send, n2_keep, n2_far = rows_call(
-        norm_rows, seed_low, wide_w, down_w
-    )
+    if short:
+        sides = jnp.concatenate([pos_x[1::2], pos_x[0::2]])
+        wide_blocks, down_send, down_keep, n2_send, n2_keep, n2_far = rows_pack_call(
+            jnp.concatenate([pos, sides]), norm_rows, seed_low, wide_w, down_w
+        )
+    else:
+        hidden_rows, gate_grad, up_grad, n2_send, n2_keep, n2_far = rows_call(
+            norm_rows, seed_low, wide_w, down_w
+        )
 
     context_near, context_far = at_once(context, context_far, n2_send)[:2]
     context_p = [context, swap(context_near, "mp", 1), context_far, swap(context_far, "mp", 1)]
@@ -1018,19 +1068,16 @@
 
     n2_near = swap(n2_send, "mp", 1)
     if short:
-        sides = jnp.concatenate([pos_x[1::2], pos_x[0::2]])
-        (wide_blocks,) = pack(pos, norm_rows, [gate_grad, up_grad], 1, "wide")
         wide_sum = lax.psum_scatter(wide_blocks, "dp", scatter_dimension=0, tiled=False)
-        n2_near, hidden_rows = at_once(n2_near, hidden_rows, wide_blocks)[:2]
+        down_x = swap(down_send[:2], "dp", 1)
+        down_x = (down_x, swap(tie(down_send[2:], down_x), "dp", 1))
     n2_near = n2_near.astype(F32)
     n2_half = jnp.concatenate(
         [n2_keep.astype(F32) + n2_near[:, :share], n2_far.astype(F32) + n2_near[:, share:]], axis=1
     ).astype(BF)
     n2_back = swap(n2_half, "mp", 2)
     if short:
-        down_send, down_keep = pack(sides, seed_low, [hidden_rows], 2, "down")
-        down_x = swap(down_send, "dp", 1)
-        n2_back, context_p = at_once(n2_back, context_p, down_send)[:2]
+        n2_back, context_p = at_once(n2_back, context_p)
     n2_back = n2_back.astype(F32)
     n2_own = (
         n2_half.astype(F32) + jnp.concatenate([n2_back[:, share:], n2_back[:, :share]], axis=1)
@@ -1041,29 +1088,32 @@
     own_seed = own_seed.reshape(windows, rows, 2 * share)
 
     dqkv, row_dot = back_call(q_rows, context_grad, qkv, onehot, cosm, sinm, cos, sin)
-    n_send, n_keep, n_far = first_grad_call(dqkv, attn_t)
+    first_in = dqkv
+    if short:
+        down_added = add_terms(down_keep, at_once(*down_x, dqkv)[:2], "down")
+        attn_send, attn_keep = pack_attention(
+            sides, norm_one, dqkv, attn_seed, context_rows, gain_two
+        )
+        attn_send, down_added, first_in, row_dot = at_once(attn_send, down_added, dqkv, row_dot)
+        attn_x = swap(attn_send, "dp", 1)
+    n_send, n_keep, n_far = first_grad_call(first_in, attn_t)
     row_dot = row_dot + swap(row_dot, "mp", 1)
     if short:
-        down_added = add_terms(down_keep, down_x, "down")
-        n_send, row_dot, down_added = at_once(n_send, row_dot, down_added)
+        n_send, row_dot = at_once(n_send, row_dot)
     n_near = swap(n_send, "mp", 1)
     row_far = swap(row_dot, "mp", 2)
     if short:
-        attn_send, attn_keep = pack_attention(
-            sides, norm_one, tie(dqkv, n_send), attn_seed, context_rows, gain_two
-        )
-        n_near, row_far, attn_send, down_added = at_once(n_near, row_far, attn_send, down_added)
+        n_near, row_far = at_once(n_near, row_far)
     row_dot = row_dot + row_far
     n_half = (n_far.astype(F32) + n_near[:, share:].astype(F32)).astype(BF)
 
     if short:
-        n_half, attn_send, down_added, ffn_in = at_once(n_half, attn_send, down_added, context_p)
-        attn_x = swap(attn_send, "dp", 1)
+        n_half, down_added, ffn_in = at_once(n_half, down_added, context_p)
         down_terms = [down_added[0]] + [swap(down_added[k], "dp", 2 * k) for k in range(1, 4)]
         n_back = swap(n_half, "mp", 2)
         ffn_out = ffn_call(tokens_p, ffn_in, wo_p, gains[1], wide_w, down_w)
         ffn_out, attn_x, down_terms, n_back = at_once(ffn_out, attn_x, down_terms, n_back)
-        attn_added = add_terms(attn_keep, attn_x, "attention")
+        attn_added = add_terms(attn_keep, (attn_x,), "attention")
     else:
         n_back = swap(n_half, "mp", 2)
         ffn_out = ffn_call(tokens_p, context_p, wo_p, gains[1], wide_w, down_w)
@@ -1094,7 +1144,7 @@
     )
     if short:
         gate_up_old = (gate_up_master, gate_up_first, gate_up_second, gate_up_average)
-        gate_up_out = adam_cols([wide_sum], gate_up_old, D ** (-0.5), "gate_up")
+        gate_up_out = adam_cols([wide_sum], gate_up_old, D ** (-0.5), "gate_up", mixed=True)
         f_back, attn_terms, input_grad, gate_up_out = at_once(
             f_back, attn_terms, input_grad, gate_up_out
         )

time: 309 us -> 292 us (0.945)
  local copies, waits for them, and re-layouts: 41.2 us -> 26.6 us
    unnamed x216 -> x184, local copies, waits for them, and re-layouts: 30 us -> 17.4 us
    all_gather x1, waiting for transfers between devices: 18.1 us -> 13.8 us  [local(): ffn_stack = lax.all_gather(ffn_block, 'dp', axis=0, tiled=False)]
    pallas_call x5 -> x3, Pallas kernels: 16.5 us -> 12.3 us  [the longest x1 9.53 us: rows_pack_call(): pl.pallas_call(rows_pack_kernel, name='masked_rows', grid_spec=pltpu.Pref...]
    ppermute x38 -> x39, waiting for transfers between devices: 48 us -> 49.5 us  [swap(): return lax.ppermute(x, axis, [(i, i ^ bit) for i in range(n)])]
    ppermute x38 -> x39, starting transfers between devices: 36.8 us -> 37 us  [swap(): return lax.ppermute(x, axis, [(i, i ^ bit) for i in range(n)])]
  transfers between devices with their start and end apart: 40 -> 41, of which waited for: 14 -> 17; matrix products, arithmetic and copies ran while one was open for 11% -> 12% of each run, Pallas kernels for 34% -> 36%
where the time goes in v3:
time: 292 us; the launch traced here: 288 us
  Pallas kernels  105 us (36%)
  waiting for transfers between devices  76.7 us (26%)
  starting transfers between devices  37.1 us (13%)
  other arithmetic  27.5 us (9%)
  local copies, waits for them, and re-layouts  26.6 us (9%)
  between operations  15.3 us (5%)
    ppermute x39, waiting for transfers between devices, swap(): return lax.ppermute(x, axis, [(i, i ^ bit) for i in range(n)])  49.5 us
    ppermute x39, starting transfers between devices, swap(): return lax.ppermute(x, axis, [(i, i ^ bit) for i in range(n)])  37 us
    pallas_call x1, Pallas kernels, ffn_call(): pl.pallas_call(ffn_kernel, name='feed_forward', grid=(count // TALL,), in...  23.6 us
    unnamed x184, local copies, waits for them, and re-layouts  17.4 us
    pallas_call x1, Pallas kernels, attend_call(): pl.pallas_call(attend_kernel, name='attend', grid=(windows, tiles), in_sp...  16.2 us
    all_gather x1, waiting for transfers between devices, local(): ffn_stack = lax.all_gather(ffn_block, 'dp', axis=0, tiled=False)  13.8 us
    reduce_scatter x1, waiting for transfers between devices, local(): lax.psum_scatter(wide_blocks, 'dp', scatter_dimension=0, tiled=False)  13.4 us
    pallas_call x1, Pallas kernels, back_call(): pl.pallas_call(back_kernel, name='attend_back', grid=(windows,), in_specs...  9.83 us
  transfers between devices with their start and end apart: 41, of which 17 were waited for; matrix products, arithmetic and copies ran while one was open for 12% of the time, Pallas kernels for 36%

profile of v3, /device:TPU:0, one launch (start us, length us, event | category | flops | bytes accessed | tf_op | source)
XLA Modules:
  0.0 288.4 jit_solution(2693505896957350904)
XLA Ops:
  8.5 1.4 convert_element_type.127
  10.9 3.0 %collective-permute-start.1 = (bf16[2048,256]{1,0:T(8,128)(2,1)S(1)}, bf16[2048,256]{1,0:T(8,128)(2,1)S(1)}, u32[]{:S(2)}, u32[]{:S(2)}) collective-permute-start(bf16[2048,256]{1,0:T(8,128)(2,1)S(1)} %copy-done.7), channel_id=1, source_target_pairs={{0,2},{1,3},{2,0},{3,1},{4,6},{5,7},{6,4},{7,5},{8,10},{9,11},{10,... | collective-permute-start | bytes 3145736 | tf_op jit(solution)/shard_map/ppermute | solution.py:53
  14.2 1.6 collective-permute-start.9
  15.8 1.6 collective-permute-start.7
  17.3 2.6 collective-permute-start.5
  20.2 3.2 %fusion.4 = (f32[1024,32]{1,0:T(8,128)}, f32[1024,32]{1,0:T(8,128)}, f32[1024,32]{1,0:T(8,128)}) fusion(f32[32]{0:T(128)S(1)} %multiply_power_fusion, f32[1024]{0:T(1024)S(1)} %iota_convert_fusion), kind=kLoop, calls=%fused_computation.24 | loop fusion | flops 65536 | bytes 397440 | tf_op jit(solution)/shard_map/neg | solution.py:77
  23.4 4.5 %pad_maximum_fusion.1 = (f32[1024,128]{1,0:T(8,128)}, f32[1024,128]{1,0:T(8,128)}) fusion(f32[1024,32]{1,0:T(8,128)} %get-tuple-element.339, f32[1024,32]{1,0:T(8,128)} %get-tuple-element.338, f32[1024,32]{1,0:T(8,128)} %get-tuple-element.337), kind=kLoop, calls=%fused_computation.13 | loop fusion | flops 786432 | bytes 1441792 | tf_op jit(solution)/shard_map/concatenate | solution.py:76
  27.9 6.0 %collective-permute-done.7.refs_5_ = bf16[528,256]{1,0:T(8,128)(2,1)S(1)} collective-permute-done((bf16[528,256]{1,0:T(8,128)(2,1)S(1)}, bf16[528,256]{1,0:T(8,128)(2,1)S(1)}, u32[]{:S(2)}, u32[]{:S(2)}) %collective-permute-start.7) | collective-permute-done | bytes 270368 | tf_op jit(solution)/shard_map/ppermute | solution.py:53
  33.8 12.5 %collective-permute-done.5.refs_3_ = bf16[528,256]{1,0:T(8,128)(2,1)} collective-permute-done((bf16[528,256]{1,0:T(8,128)(2,1)S(1)}, bf16[528,256]{1,0:T(8,128)(2,1)}, u32[]{:S(2)}, u32[]{:S(2)}) %collective-permute-start.5) | collective-permute-done | bytes 270368 | tf_op jit(solution)/shard_map/ppermute | solution.py:53
  46.6 2.3 collective-permute-done.3.refs_1_
  50.7 2.4 collective-permute-done.6.refs_2_
  53.1 2.9 %collective-permute-done.4.refs_0_ = bf16[528,256]{1,0:T(8,128)(2,1)} collective-permute-done((bf16[528,256]{1,0:T(8,128)(2,1)}, bf16[528,256]{1,0:T(8,128)(2,1)}, u32[]{:S(2)}, u32[]{:S(2)}) %collective-permute-start.4) | collective-permute-done | bytes 270368 | tf_op jit(solution)/shard_map/ppermute | solution.py:53
  56.0 2.0 place_attention.1
  61.4 2.0 copy-done.21
  63.4 8.5 %qkv.1 = (bf16[3,2048,256]{2,1,0:T(8,128)(2,1)S(1)}, bf16[2048,1024]{1,0:T(8,128)(2,1)S(1)}, f32[2048,1]{1,0:T(8,128)S(1)}, bf16[320,1024]{1,0:T(8,128)(2,1)S(1)}, bf16[320,256]{1,0:T(8,128)(2,1)S(1)}) custom-call(bf16[2048,256]{1,0:T(8,128)(2,1)S(1)} %copy-done.8, bf16[2048,256]{1,0:T(8,128)(2,1)S(1)} %collective-permute-done.x1, ...), custom_call_target="tpu_custom_call" | custom-call | flops 1000 | bytes 1000 | tf_op jit(solution)/shard_map/qkv/pallas_call | solution.py:226
  73.0 16.2 %attend.1 = (bf16[2048,256]{1,0:T(8,128)(2,1)}, bf16[320,256]{1,0:T(8,128)(2,1)S(1)}) custom-call(bf16[3,2048,256]{2,1,0:T(8,128)(2,1)S(1)} %get-tuple-element.180.q_ref.k_ref.v_ref.a_ref, bf16[3,2048,256]{2,1,0:T(8,128)(2,1)S(1)} %get-tuple-element.180.q_ref.k_ref.v_ref.a_ref, bf16[3,2048,256]{2,1,0:T(8,128)(2,1)S(1)} %get-tuple-element.180.q_ref.k_ref.v_ref.a_ref, ...), custom_call_target="tpu_custom_call" | custom-call | flops 1000 | bytes 1000 | tf_op jit(solution)/shard_map/attend/pallas_call | solution.py:297
  90.7 1.8 collective-permute-start.12
  93.2 4.6 %collective-permute-done.12 = bf16[640,256]{1,0:T(8,128)(2,1)} collective-permute-done((bf16[640,256]{1,0:T(8,128)(2,1)S(1)}, bf16[640,256]{1,0:T(8,128)(2,1)}, u32[]{:S(2)}, u32[]{:S(2)}) %collective-permute-start.12) | collective-permute-done | bytes 327712 | tf_op jit(solution)/shard_map/ppermute | solution.py:53
  103.0 1.8 collective-permute-start.18
  113.7 1.5 convert_multiply_fusion
  115.2 13.8 %all-gather.3.cloned.1.call-done = bf16[24,128,1024]{2,1,0:T(8,128)(2,1)} async-done(((bf16[3,128,1024]{2,1,0:T(8,128)(2,1)}), bf16[24,128,1024]{2,1,0:T(8,128)(2,1)}) %all-gather.3.cloned.1.call-update) | async-done | bytes 6291472 | tf_op jit(solution)/shard_map/all_gather | solution.py:1010
  129.0 2.8 copy-done.11
  131.8 2.8 place_feed_forward.1
  134.6 9.5 %masked_rows.1 = (bf16[8,128,2048]{2,1,0:T(8,128)(2,1)S(1)}, bf16[4,128,1024]{2,1,0:T(8,128)(2,1)S(1)}, bf16[4,128,1024]{2,1,0:T(8,128)(2,1)S(1)}, bf16[320,512]...) custom-call(s32[16]{0:T(128)S(1)} %copy-done.65, bf16[320,1024]{1,0:T(8,128)(2,1)S(1)} %copy-done.49, ...), custom_call_target="tpu_custom_call" | custom-call | flops 1000 | bytes 1000 | tf_op jit(solution)/shard_map/masked_rows/pallas_call | solution.py:535
  145.8 1.5 fusion.16
  150.4 1.5 collective-permute-start.17
  153.5 8.0 %collective-permute-done.22.refs_0_ = bf16[2,128,1024]{2,1,0:T(8,128)(2,1)} collective-permute-done((bf16[2,128,1024]{2,1,0:T(8,128)(2,1)}, bf16[2,128,1024]{2,1,0:T(8,128)(2,1)}, u32[]{:S(2)}, u32[]{:S(2)}) %collective-permute-start.22) | collective-permute-done | bytes 524320 | tf_op jit(solution)/shard_map/ppermute | solution.py:53
  169.3 9.8 %attend_back.1 = (bf16[2048,768]{1,0:T(8,128)(2,1)S(1)}, f32[1,2048]{1,0:T(1,128)S(1)}) custom-call(bf16[320,256]{1,0:T(8,128)(2,1)S(1)} %copy-done.61, bf16[320,256]{1,0:T(8,128)(2,1)S(1)} %get-tuple-element.196.do_ref, bf16[3,2048,256]{2,1,0:T(8,128)(2,1)S(1)} %get-tuple-element.180.q_ref.k_ref.v_ref.a_ref, ...), custom_call_target="tpu_custom_call" | custom-call | flops 1000 | bytes 1000 | tf_op jit(solution)/shard_map/attend_back/pallas_call | solution.py:754
  179.2 7.9 %pack_attention.1 = (bf16[4,144,1024]{2,1,0:T(8,128)(2,1)}, bf16[4,144,1024]{2,1,0:T(8,128)(2,1)S(1)}) custom-call(s32[8]{0:T(128)S(1)} %pad_add_fusion.pos_ref, bf16[2048,1024]{1,0:T(8,128)(2,1)S(1)} %copy-done.26, bf16[2048,768]{1,0:T(8,128)(2,1)S(1)} %get-tuple-element.211.d_ref, bf16[320,1024]{1,0:T(8,128)(2,1)S(1)} %get-tuple-element.198.seed_ref, ...), custom_call_target="tpu_custom_call" | custom-call | flops 1000 | bytes 1000 | tf_op jit(solution)/shard_map/pack_attention/pallas_call | solution.py:654
  187.1 1.5 add_down.1
  189.1 3.9 %first_grad.1 = (bf16[2048,512]{1,0:T(8,128)(2,1)S(1)}, bf16[2048,256]{1,0:T(8,128)(2,1)S(1)}, bf16[2048,256]{1,0:T(8,128)(2,1)S(1)}) custom-call(bf16[2048,768]{1,0:T(8,128)(2,1)S(1)} %get-tuple-element.211.d_ref, bf16[4,256,1024]{2,1,0:T(8,128)(2,1)S(1)} %copy-done.6), custom_call_target="tpu_custom_call" | custom-call | flops 1000 | bytes 1000 | tf_op jit(solution)/shard_map/first_grad/pallas_call | solution.py:795
  194.3 1.5 collective-permute-start.27
  198.6 5.5 %collective-permute-start.29 = (bf16[128,1024]{1,0:T(8,128)(2,1)S(1)}, bf16[128,1024]{1,0:T(8,128)(2,1)S(1)}, u32[]{:S(2)}, u32[]{:S(2)}) collective-permute-start(bf16[128,1024]{1,0:T(8,128)(2,1)S(1)} %get-tuple-element.237), channel_id=1, source_target_pairs={{0,16},{4,20},{8,24},{12,28},{16,0},{20,4},{24,8},{28,12},{1,17},{... | collective-permute-start | bytes 786440 | tf_op jit(solution)/shard_map/ppermute | solution.py:53
  204.1 1.4 collective-permute-start.30
  205.5 23.6 %feed_forward.1 = (bf16[2048,512]{1,0:T(8,128)(2,1)}, bf16[2048,256]{1,0:T(8,128)(2,1)S(1)}, bf16[2048,256]{1,0:T(8,128)(2,1)S(1)}, f32[2048,256]{1,0:T(8,128)}) custom-call(bf16[2048,256]{1,0:T(8,128)(2,1)S(1)} %copy-done.9, bf16[2048,256]{1,0:T(8,128)(2,1)} %copy-done.22, bf16[2048,256]{1,0:T(8,128)(2,1)} %copy-done.20, bf16[2048,256]{1,0:T(8,128)(2,1)} %copy-done.23, ...), custom_call_target="tpu_custom_call" | custom-call | flops 1000 | bytes 1000 | tf_op jit(solution)/shard_map/feed_forward/pallas_call | solution.py:404
  229.2 2.4 collective-permute-done.27.refs_0_
  233.0 2.4 adam_down.1
  236.0 2.2 convert_add_fusion
  238.2 1.4 collective-permute-start.33
  240.8 1.7 collective-permute-start.35
  242.6 1.5 collective-permute-start.36
  244.2 4.4 %input_grad.1 = bf16[2048,256]{1,0:T(8,128)(2,1)} custom-call(bf16[2048,256]{1,0:T(8,128)(2,1)S(1)} %copy-done.9, f32[2048,1]{1,0:T(8,128)S(1)} %copy-done.45, f32[1,2048]{1,0:T(1,128)S(1)} %add.101.dot_ref, bf16[2048,256]{1,0:T(8,128)(2,1)S(1)} %get-tuple-element.273.keep_ref, bf16[2048,256]{1,0:T(8,128)(2,1)S(1)} %slice.128.near_ref, ...), custom_call_target="tpu_custom_call" | custom-call | flops 1000 | bytes 1000 | tf_op jit(solution)/shard_map/input_grad/pallas_call | solution.py:833
  248.5 13.4 %reduce-scatter.2.cloned.1.call-done = bf16[1,128,2048]{2,1,0:T(8,128)(2,1)} async-done(((bf16[8,128,2048]{2,1,0:T(8,128)(2,1)}), bf16[1,128,2048]{2,1,0:T(8,128)(2,1)}) %reduce-scatter.2.cloned.1.call-update) | async-done | bytes 524304 | tf_op jit(solution)/shard_map/reduce_scatter | solution.py:1071
  261.9 5.6 %adam_gate_up.1 = (f32[2,128,1024]{2,1,0:T(8,128)}, f32[2,128,1024]{2,1,0:T(8,128)}, f32[2,128,1024]{2,1,0:T(8,128)}, f32[2,128,1024]{2,1,0:T(8,128)}, f32[2,128...) custom-call(bf16[128,2048]{1,0:T(8,128)(2,1)} %bitcast.32, f32[2,128,1024]{2,1,0:T(8,128)} %refs_1_.1, ...), custom_call_target="tpu_custom_call" | custom-call | tf_op jit(solution)/shard_map/adam_gate_up/pallas_call | solution.py:893
  267.5 4.0 %collective-permute-done.36.refs_3_ = bf16[144,1024]{1,0:T(8,128)(2,1)S(1)} collective-permute-done((bf16[144,1024]{1,0:T(8,128)(2,1)}, bf16[144,1024]{1,0:T(8,128)(2,1)S(1)}, u32[]{:S(2)}, u32[]{:S(2)}) %collective-permute-start.36) | collective-permute-done | bytes 294944 | tf_op jit(solution)/shard_map/ppermute | solution.py:53
  271.5 2.3 adam_qkv.1
  274.1 2.7 add_convert_fusion
  276.9 1.5 collective-permute-start.38
  (295 shorter events, 50.5 us)
Async XLA Ops:
  7.2 121.8 %all-gather.3.cloned.1.call-start = ((), (), s32[]{:S(2)}) async-start(), calls=%async_computation.2 | async-start | bytes 7077888 | tf_op jit(solution)/shard_map/all_gather | solution.py:1010
  10.9 251.0 %reduce-scatter.2.cloned.1.call-start = ((), (), s32[]{:S(2)}) async-start(), calls=%async_computation.1 | async-start | bytes 4718592 | tf_op jit(solution)/shard_map/reduce_scatter | solution.py:1071
  10.9 39.3 %collective-permute-start.1 = (bf16[2048,256]{1,0:T(8,128)(2,1)S(1)}, bf16[2048,256]{1,0:T(8,128)(2,1)S(1)}, u32[]{:S(2)}, u32[]{:S(2)}) collective-permute-start(bf16[2048,256]{1,0:T(8,128)(2,1)S(1)} %copy-done.7), channel_id=1, source_target_pairs={{0,2},{1,3},{2,0},{3,1},{4,6},{5,7},{6,4},{7,5},{8,10},{9,11},{10,... | collective-permute-start | bytes 3145736 | tf_op jit(solution)/shard_map/ppermute | solution.py:53
  14.2 35.9 %collective-permute-start.9 = (bf16[528,256]{1,0:T(8,128)(2,1)S(1)}, bf16[528,256]{1,0:T(8,128)(2,1)S(1)}, u32[]{:S(2)}, u32[]{:S(2)}) collective-permute-start(bf16[528,256]{1,0:T(8,128)(2,1)S(1)} %constant_dynamic-update-slice_fusion.refs_7_), channel_id=1, source_target_pairs={{0,4},{4,0},{8,12},{12,8},{16,20},{20,16},{24,28},{28,24},{1,5},{5... | collective-permute-start | bytes 811016 | tf_op jit(solution)/shard_map/ppermute | solution.py:53
  15.8 18.0 %collective-permute-start.7 = (bf16[528,256]{1,0:T(8,128)(2,1)S(1)}, bf16[528,256]{1,0:T(8,128)(2,1)S(1)}, u32[]{:S(2)}, u32[]{:S(2)}) collective-permute-start(bf16[528,256]{1,0:T(8,128)(2,1)S(1)} %constant_dynamic-update-slice_fusion.refs_7_), channel_id=1, source_target_pairs={{0,8},{4,12},{8,0},{12,4},{16,24},{20,28},{24,16},{28,20},{1,9},{5... | collective-permute-start | bytes 811016 | tf_op jit(solution)/shard_map/ppermute | solution.py:53
  17.3 29.0 %collective-permute-start.5 = (bf16[528,256]{1,0:T(8,128)(2,1)S(1)}, bf16[528,256]{1,0:T(8,128)(2,1)}, u32[]{:S(2)}, u32[]{:S(2)}) collective-permute-start(bf16[528,256]{1,0:T(8,128)(2,1)S(1)} %constant_dynamic-update-slice_fusion.refs_7_), channel_id=1, source_target_pairs={{0,16},{4,20},{8,24},{12,28},{16,0},{20,4},{24,8},{28,12},{1,17},{... | collective-permute-start | bytes 811016 | tf_op jit(solution)/shard_map/ppermute | solution.py:53
  19.9 29.0 %collective-permute-start.3 = (bf16[528,256]{1,0:T(8,128)(2,1)S(1)}, bf16[528,256]{1,0:T(8,128)(2,1)}, u32[]{:S(2)}, u32[]{:S(2)}) collective-permute-start(bf16[528,256]{1,0:T(8,128)(2,1)S(1)} %constant_dynamic-update-slice_fusion.refs_7_), channel_id=1, source_target_pairs={{0,24},{4,28},{8,16},{12,20},{16,8},{20,12},{24,0},{28,4},{1,25},{... | collective-permute-start | bytes 811016 | tf_op jit(solution)/shard_map/ppermute | solution.py:53
  20.2 28.8 %copy-start.88 = (s32[8]{0:T(128)S(1)}, s32[8]{0:T(128)}, u32[]{:S(2)}) copy-start(s32[8]{0:T(128)} %param.31) | copy-start | bytes 100
  33.8 16.9 %collective-permute-start.8 = (bf16[528,256]{1,0:T(8,128)(2,1)S(1)}, bf16[528,256]{1,0:T(8,128)(2,1)}, u32[]{:S(2)}, u32[]{:S(2)}) collective-permute-start(bf16[528,256]{1,0:T(8,128)(2,1)S(1)} %collective-permute-done.7.refs_5_), channel_id=1, source_target_pairs={{0,4},{4,0},{8,12},{12,8},{16,20},{20,16},{24,28},{28,24},{1,5},{5... | collective-permute-start | bytes 811016 | tf_op jit(solution)/shard_map/ppermute | solution.py:53
  46.4 6.8 %collective-permute-start.6 = (bf16[528,256]{1,0:T(8,128)(2,1)}, bf16[528,256]{1,0:T(8,128)(2,1)}, u32[]{:S(2)}, u32[]{:S(2)}) collective-permute-start(bf16[528,256]{1,0:T(8,128)(2,1)} %collective-permute-done.5.refs_3_), channel_id=1, source_target_pairs={{0,4},{4,0},{8,12},{12,8},{16,20},{20,16},{24,28},{28,24},{1,5},{5... | collective-permute-start | bytes 811016 | tf_op jit(solution)/shard_map/ppermute | solution.py:53
  48.9 7.1 %collective-permute-start.4 = (bf16[528,256]{1,0:T(8,128)(2,1)}, bf16[528,256]{1,0:T(8,128)(2,1)}, u32[]{:S(2)}, u32[]{:S(2)}) collective-permute-start(bf16[528,256]{1,0:T(8,128)(2,1)} %collective-permute-done.3.refs_1_), channel_id=1, source_target_pairs={{0,4},{4,0},{8,12},{12,8},{16,20},{20,16},{24,28},{28,24},{1,5},{5... | collective-permute-start | bytes 811016 | tf_op jit(solution)/shard_map/ppermute | solution.py:53
  50.1 39.1 %copy-start.70 = (bf16[2,160,256]{2,1,0:T(8,128)(2,1)}, bf16[2,160,256]{2,1,0:T(8,128)(2,1)S(1)}, u32[]{:S(2)}) copy-start(bf16[2,160,256]{2,1,0:T(8,128)(2,1)S(1)} %pad.15) | copy-start | bytes 491524
  50.1 11.2 %collective-permute-start = (bf16[2048,256]{1,0:T(8,128)(2,1)S(1)}, bf16[2048,256]{1,0:T(8,128)(2,1)S(1)}, u32[]{:S(2)}, u32[]{:S(2)}) collective-permute-start(bf16[2048,256]{1,0:T(8,128)(2,1)S(1)} %copy-done.7), channel_id=1, source_target_pairs={{0,1},{1,0},{2,3},{3,2},{4,5},{5,4},{6,7},{7,6},{8,9},{9,8},{10,11... | collective-permute-start | bytes 3145736 | tf_op jit(solution)/shard_map/ppermute | solution.py:53
  50.2 11.1 %collective-permute-start.2 = (bf16[2048,256]{1,0:T(8,128)(2,1)S(1)}, bf16[2048,256]{1,0:T(8,128)(2,1)S(1)}, u32[]{:S(2)}, u32[]{:S(2)}) collective-permute-start(bf16[2048,256]{1,0:T(8,128)(2,1)S(1)} %collective-permute-done.1.x2), channel_id=1, source_target_pairs={{0,1},{1,0},{2,3},{3,2},{4,5},{5,4},{6,7},{7,6},{8,9},{9,8},{10,11... | collective-permute-start | bytes 3145736 | tf_op jit(solution)/shard_map/ppermute | solution.py:53
  60.3 12.7 %collective-permute-start.10 = (bf16[256,1024]{1,0:T(8,128)(2,1)S(1)}, bf16[256,1024]{1,0:T(8,128)(2,1)S(1)}, u32[]{:S(2)}, u32[]{:S(2)}) collective-permute-start(bf16[256,1024]{1,0:T(8,128)(2,1)S(1)} %slice_bitcast_fusion.o0), channel_id=1, source_target_pairs={{0,2},{1,3},{2,0},{3,1},{4,6},{5,7},{6,4},{7,5},{8,10},{9,11},{10,... | collective-permute-start | bytes 1572872 | tf_op jit(solution)/shard_map/ppermute | solution.py:53
  73.0 16.2 %copy-start.25 = (bf16[2048,1024]{1,0:T(8,128)(2,1)}, bf16[2048,1024]{1,0:T(8,128)(2,1)S(1)}, u32[]{:S(2)}) copy-start(bf16[2048,1024]{1,0:T(8,128)(2,1)S(1)} %get-tuple-element.176.norm_ref) | copy-start | bytes 12582916
  73.0 16.2 %copy-start.46 = (bf16[320,1024]{1,0:T(8,128)(2,1)}, bf16[320,1024]{1,0:T(8,128)(2,1)S(1)}, u32[]{:S(2)}) copy-start(bf16[320,1024]{1,0:T(8,128)(2,1)S(1)} %get-tuple-element.178.t_ref) | copy-start | bytes 1966084
  73.0 16.2 %copy-start.60 = (bf16[320,256]{1,0:T(8,128)(2,1)}, bf16[320,256]{1,0:T(8,128)(2,1)S(1)}, u32[]{:S(2)}) copy-start(bf16[320,256]{1,0:T(8,128)(2,1)S(1)} %get-tuple-element.177.q_ref) | copy-start | bytes 491524
  73.0 19.4 %copy-start.86 = (s32[16]{0:T(128)S(1)}, s32[16]{0:T(128)}, u32[]{:S(2)}) copy-start(s32[16]{0:T(128)} %param.30) | copy-start | bytes 196
  73.0 20.0 %copy-start.87 = (s32[2]{0:T(128)S(1)}, s32[2]{0:T(128)}, u32[]{:S(2)}) copy-start(s32[2]{0:T(128)} %param.29) | copy-start | bytes 28
  90.7 7.2 %collective-permute-start.12 = (bf16[640,256]{1,0:T(8,128)(2,1)S(1)}, bf16[640,256]{1,0:T(8,128)(2,1)}, u32[]{:S(2)}, u32[]{:S(2)}) collective-permute-start(bf16[640,256]{1,0:T(8,128)(2,1)S(1)} %pad_maximum_fusion.3), channel_id=1, source_target_pairs={{0,2},{1,3},{2,0},{3,1},{4,6},{5,7},{6,4},{7,5},{8,10},{9,11},{10,... | collective-permute-start | bytes 983048 | tf_op jit(solution)/shard_map/ppermute | solution.py:53
  97.9 5.1 %collective-permute-start.13 = (bf16[640,256]{1,0:T(8,128)(2,1)}, bf16[640,256]{1,0:T(8,128)(2,1)}, u32[]{:S(2)}, u32[]{:S(2)}) collective-permute-start(bf16[640,256]{1,0:T(8,128)(2,1)} %collective-permute-done.12), channel_id=1, source_target_pairs={{0,1},{1,0},{2,3},{3,2},{4,5},{5,4},{6,7},{7,6},{8,9},{9,8},{10,11... | collective-permute-start | bytes 983048 | tf_op jit(solution)/shard_map/ppermute | solution.py:53
  102.4 5.1 %collective-permute-start.11 = (bf16[640,256]{1,0:T(8,128)(2,1)}, bf16[640,256]{1,0:T(8,128)(2,1)S(1)}, u32[]{:S(2)}, u32[]{:S(2)}) collective-permute-start(bf16[640,256]{1,0:T(8,128)(2,1)} %copy-done.74), channel_id=1, source_target_pairs={{0,1},{1,0},{2,3},{3,2},{4,5},{5,4},{6,7},{7,6},{8,9},{9,8},{10,11... | collective-permute-start | bytes 983048 | tf_op jit(solution)/shard_map/ppermute | solution.py:53
  103.0 42.2 %collective-permute-start.18 = (bf16[2048,256]{1,0:T(8,128)(2,1)}, bf16[2048,256]{1,0:T(8,128)(2,1)}, u32[]{:S(2)}, u32[]{:S(2)}) collective-permute-start(bf16[2048,256]{1,0:T(8,128)(2,1)} %get-tuple-element.226.c0), channel_id=1, source_target_pairs={{0,2},{1,3},{2,0},{3,1},{4,6},{5,7},{6,4},{7,5},{8,10},{9,11},{10,... | collective-permute-start | bytes 3145736 | tf_op jit(solution)/shard_map/ppermute | solution.py:53
  106.0 2.7 collective-permute-start.14
  106.0 2.9 collective-permute-start.15
  145.2 17.5 %collective-permute-start.19 = (bf16[2048,256]{1,0:T(8,128)(2,1)}, bf16[2048,256]{1,0:T(8,128)(2,1)}, u32[]{:S(2)}, u32[]{:S(2)}) collective-permute-start(bf16[2048,256]{1,0:T(8,128)(2,1)} %get-tuple-element.226.c0), channel_id=1, source_target_pairs={{0,1},{1,0},{2,3},{3,2},{4,5},{5,4},{6,7},{7,6},{8,9},{9,8},{10,11... | collective-permute-start | bytes 3145736 | tf_op jit(solution)/shard_map/ppermute | solution.py:53
  145.2 17.5 %collective-permute-start.20 = (bf16[2048,256]{1,0:T(8,128)(2,1)}, bf16[2048,256]{1,0:T(8,128)(2,1)}, u32[]{:S(2)}, u32[]{:S(2)}) collective-permute-start(bf16[2048,256]{1,0:T(8,128)(2,1)} %collective-permute-done.18.c2), channel_id=1, source_target_pairs={{0,1},{1,0},{2,3},{3,2},{4,5},{5,4},{6,7},{7,6},{8,9},{9,8},{10,11... | collective-permute-start | bytes 3145736 | tf_op jit(solution)/shard_map/ppermute | solution.py:53
  145.7 3.1 %collective-permute-start.16 = (bf16[320,512]{1,0:T(8,128)(2,1)S(1)}, bf16[320,512]{1,0:T(8,128)(2,1)S(1)}, u32[]{:S(2)}, u32[]{:S(2)}) collective-permute-start(bf16[320,512]{1,0:T(8,128)(2,1)S(1)} %get-tuple-element.187), channel_id=1, source_target_pairs={{0,1},{1,0},{2,3},{3,2},{4,5},{5,4},{6,7},{7,6},{8,9},{9,8},{10,11... | collective-permute-start | bytes 983048 | tf_op jit(solution)/shard_map/ppermute | solution.py:53
  147.3 14.2 %collective-permute-start.22 = (bf16[2,128,1024]{2,1,0:T(8,128)(2,1)}, bf16[2,128,1024]{2,1,0:T(8,128)(2,1)}, u32[]{:S(2)}, u32[]{:S(2)}) collective-permute-start(bf16[2,128,1024]{2,1,0:T(8,128)(2,1)} %get-tuple-element.322), channel_id=1, source_target_pairs={{0,4},{4,0},{8,12},{12,8},{16,20},{20,16},{24,28},{28,24},{1,5},{5... | collective-permute-start | bytes 1572872 | tf_op jit(solution)/shard_map/ppermute | solution.py:53
  150.4 12.3 %collective-permute-start.17 = (bf16[320,512]{1,0:T(8,128)(2,1)}, bf16[320,512]{1,0:T(8,128)(2,1)}, u32[]{:S(2)}, u32[]{:S(2)}) collective-permute-start(bf16[320,512]{1,0:T(8,128)(2,1)} %pad_maximum_fusion.4), channel_id=1, source_target_pairs={{0,2},{1,3},{2,0},{3,1},{4,6},{5,7},{6,4},{7,5},{8,10},{9,11},{10,... | collective-permute-start | bytes 983048 | tf_op jit(solution)/shard_map/ppermute | solution.py:53
  161.5 25.5 %collective-permute-start.23 = (bf16[2,128,1024]{2,1,0:T(8,128)(2,1)}, bf16[2,128,1024]{2,1,0:T(8,128)(2,1)S(1)}, u32[]{:S(2)}, u32[]{:S(2)}) collective-permute-start(bf16[2,128,1024]{2,1,0:T(8,128)(2,1)} %get-tuple-element.203), channel_id=1, source_target_pairs={{0,4},{4,0},{8,12},{12,8},{16,20},{20,16},{24,28},{28,24},{1,5},{5... | collective-permute-start | bytes 1572872 | tf_op jit(solution)/shard_map/ppermute | solution.py:53
  164.8 1.7 collective-permute-start.21
  188.6 4.6 %collective-permute-start.24 = (f32[1,2048]{1,0:T(1,128)S(1)}, f32[1,2048]{1,0:T(1,128)S(1)}, u32[]{:S(2)}, u32[]{:S(2)}) collective-permute-start(f32[1,2048]{1,0:T(1,128)S(1)} %get-tuple-element.214), channel_id=1, source_target_pairs={{0,1},{1,0},{2,3},{3,2},{4,5},{5,4},{6,7},{7,6},{8,9},{9,8},{10,11... | collective-permute-start | bytes 24584 | tf_op jit(solution)/shard_map/ppermute | solution.py:53
  193.2 4.2 %collective-permute-start.25 = (bf16[2048,512]{1,0:T(8,128)(2,1)S(1)}, bf16[2048,512]{1,0:T(8,128)(2,1)S(1)}, u32[]{:S(2)}, u32[]{:S(2)}) collective-permute-start(bf16[2048,512]{1,0:T(8,128)(2,1)S(1)} %get-tuple-element.215), channel_id=1, source_target_pairs={{0,1},{1,0},{2,3},{3,2},{4,5},{5,4},{6,7},{7,6},{8,9},{9,8},{10,11... | collective-permute-start | bytes 6291464 | tf_op jit(solution)/shard_map/ppermute | solution.py:53
  193.4 3.7 %collective-permute-start.26 = (f32[1,2048]{1,0:T(1,128)S(1)}, f32[1,2048]{1,0:T(1,128)S(1)}, u32[]{:S(2)}, u32[]{:S(2)}) collective-permute-start(f32[1,2048]{1,0:T(1,128)S(1)} %add.96), channel_id=1, source_target_pairs={{0,2},{1,3},{2,0},{3,1},{4,6},{5,7},{6,4},{7,5},{8,10},{9,11},{10,... | collective-permute-start | bytes 24584 | tf_op jit(solution)/shard_map/ppermute | solution.py:53
  194.3 37.2 %collective-permute-start.27 = (bf16[4,144,1024]{2,1,0:T(8,128)(2,1)}, bf16[4,144,1024]{2,1,0:T(8,128)(2,1)S(1)}, u32[]{:S(2)}, u32[]{:S(2)}) collective-permute-start(bf16[4,144,1024]{2,1,0:T(8,128)(2,1)} %get-tuple-element.234), channel_id=1, source_target_pairs={{0,4},{4,0},{8,12},{12,8},{16,20},{20,16},{24,28},{28,24},{1,5},{5... | collective-permute-start | bytes 3538952 | tf_op jit(solution)/shard_map/ppermute | solution.py:53
  197.7 33.8 %collective-permute-start.31 = (bf16[2048,256]{1,0:T(8,128)(2,1)S(1)}, bf16[2048,256]{1,0:T(8,128)(2,1)S(1)}, u32[]{:S(2)}, u32[]{:S(2)}) collective-permute-start(bf16[2048,256]{1,0:T(8,128)(2,1)S(1)} %add_convert_fusion.2), channel_id=1, source_target_pairs={{0,2},{1,3},{2,0},{3,1},{4,6},{5,7},{6,4},{7,5},{8,10},{9,11},{10,... | collective-permute-start | bytes 3145736 | tf_op jit(solution)/shard_map/ppermute | solution.py:53
  198.6 32.9 %collective-permute-start.28 = (bf16[128,1024]{1,0:T(8,128)(2,1)S(1)}, bf16[128,1024]{1,0:T(8,128)(2,1)S(1)}, u32[]{:S(2)}, u32[]{:S(2)}) collective-permute-start(bf16[128,1024]{1,0:T(8,128)(2,1)S(1)} %get-tuple-element.236), channel_id=1, source_target_pairs={{0,8},{4,12},{8,0},{12,4},{16,24},{20,28},{24,16},{28,20},{1,9},{5... | collective-permute-start | bytes 786440 | tf_op jit(solution)/shard_map/ppermute | solution.py:53
  198.6 32.9 %collective-permute-start.29 = (bf16[128,1024]{1,0:T(8,128)(2,1)S(1)}, bf16[128,1024]{1,0:T(8,128)(2,1)S(1)}, u32[]{:S(2)}, u32[]{:S(2)}) collective-permute-start(bf16[128,1024]{1,0:T(8,128)(2,1)S(1)} %get-tuple-element.237), channel_id=1, source_target_pairs={{0,16},{4,20},{8,24},{12,28},{16,0},{20,4},{24,8},{28,12},{1,17},{... | collective-permute-start | bytes 786440 | tf_op jit(solution)/shard_map/ppermute | solution.py:53
  204.1 27.4 %collective-permute-start.30 = (bf16[128,1024]{1,0:T(8,128)(2,1)S(1)}, bf16[128,1024]{1,0:T(8,128)(2,1)S(1)}, u32[]{:S(2)}, u32[]{:S(2)}) collective-permute-start(bf16[128,1024]{1,0:T(8,128)(2,1)S(1)} %get-tuple-element.238), channel_id=1, source_target_pairs={{0,24},{4,28},{8,16},{12,20},{16,8},{20,12},{24,0},{28,4},{1,25},{... | collective-permute-start | bytes 786440 | tf_op jit(solution)/shard_map/ppermute | solution.py:53
  231.6 4.4 %collective-permute-start.32 = (bf16[2048,512]{1,0:T(8,128)(2,1)}, bf16[2048,512]{1,0:T(8,128)(2,1)S(1)}, u32[]{:S(2)}, u32[]{:S(2)}) collective-permute-start(bf16[2048,512]{1,0:T(8,128)(2,1)} %get-tuple-element.241), channel_id=1, source_target_pairs={{0,1},{1,0},{2,3},{3,2},{4,5},{5,4},{6,7},{7,6},{8,9},{9,8},{10,11... | collective-permute-start | bytes 6291464 | tf_op jit(solution)/shard_map/ppermute | solution.py:53
  238.2 33.3 %collective-permute-start.33 = (bf16[2048,256]{1,0:T(8,128)(2,1)}, bf16[2048,256]{1,0:T(8,128)(2,1)}, u32[]{:S(2)}, u32[]{:S(2)}) collective-permute-start(bf16[2048,256]{1,0:T(8,128)(2,1)} %get-tuple-element.266), channel_id=1, source_target_pairs={{0,2},{1,3},{2,0},{3,1},{4,6},{5,7},{6,4},{7,5},{8,10},{9,11},{10,... | collective-permute-start | bytes 3145736 | tf_op jit(solution)/shard_map/ppermute | solution.py:53
  239.6 27.9 %collective-permute-start.34 = (bf16[144,1024]{1,0:T(8,128)(2,1)}, bf16[144,1024]{1,0:T(8,128)(2,1)S(1)}, u32[]{:S(2)}, u32[]{:S(2)}) collective-permute-start(bf16[144,1024]{1,0:T(8,128)(2,1)} %get-tuple-element.268), channel_id=1, source_target_pairs={{0,8},{4,12},{8,0},{12,4},{16,24},{20,28},{24,16},{28,20},{1,9},{5... | collective-permute-start | bytes 884744 | tf_op jit(solution)/shard_map/ppermute | solution.py:53
  240.8 26.7 %collective-permute-start.35 = (bf16[144,1024]{1,0:T(8,128)(2,1)}, bf16[144,1024]{1,0:T(8,128)(2,1)S(1)}, u32[]{:S(2)}, u32[]{:S(2)}) collective-permute-start(bf16[144,1024]{1,0:T(8,128)(2,1)} %get-tuple-element.269), channel_id=1, source_target_pairs={{0,16},{4,20},{8,24},{12,28},{16,0},{20,4},{24,8},{28,12},{1,17},{... | collective-permute-start | bytes 884744 | tf_op jit(solution)/shard_map/ppermute | solution.py:53
  242.6 28.9 %collective-permute-start.36 = (bf16[144,1024]{1,0:T(8,128)(2,1)}, bf16[144,1024]{1,0:T(8,128)(2,1)S(1)}, u32[]{:S(2)}, u32[]{:S(2)}) collective-permute-start(bf16[144,1024]{1,0:T(8,128)(2,1)} %get-tuple-element.270), channel_id=1, source_target_pairs={{0,24},{4,28},{8,16},{12,20},{16,8},{20,12},{24,0},{28,4},{1,25},{... | collective-permute-start | bytes 884744 | tf_op jit(solution)/shard_map/ppermute | solution.py:53
  274.0 2.8 collective-permute-start.37
  276.9 3.5 %collective-permute-start.38 = (f32[1,128]{1,0:T(1,128)S(1)}, f32[1,128]{1,0:T(1,128)S(1)}, u32[]{:S(2)}, u32[]{:S(2)}) collective-permute-start(f32[1,128]{1,0:T(1,128)S(1)} %bitcast_add_fusion), channel_id=1, source_target_pairs={{0,2},{1,3},{2,0},{3,1},{4,6},{5,7},{6,4},{7,5},{8,10},{9,11},{10,... | collective-permute-start | bytes 1544 | tf_op jit(solution)/shard_map/ppermute | solution.py:53
  (82 other events, 470.5 us)
Sparse Core Ops, SparseCore 0:
  11.0 117.9 all-gather.2
  152.0 109.8 reduce-scatter.1

commit v4 on v3

--- a/solution.py
+++ b/solution.py
@@ -1131,6 +1131,10 @@
     f_back = swap(f_half, "mp", 2)
     if short:
         attn_terms = [attn_added[0]] + [swap(attn_added[k], "dp", 2 * k) for k in range(1, 4)]
+    if short:
+        gate_up_old = (gate_up_master, gate_up_first, gate_up_second, gate_up_average)
+        gate_up_out = adam_cols([wide_sum], gate_up_old, D ** (-0.5), "gate_up", mixed=True)
+        n_back = tie(n_back, gate_up_out[0])
     input_grad = input_call(
         tokens,
         scale_one,
@@ -1143,12 +1147,10 @@
         own_seed,
     )
     if short:
-        gate_up_old = (gate_up_master, gate_up_first, gate_up_second, gate_up_average)
-        gate_up_out = adam_cols([wide_sum], gate_up_old, D ** (-0.5), "gate_up", mixed=True)
-        f_back, attn_terms, input_grad, gate_up_out = at_once(
-            f_back, attn_terms, input_grad, gate_up_out
-        )
+        f_back, input_grad = at_once(f_back, input_grad)
     output = (f_part + f_back.astype(F32)).astype(BF)
+    if short:
+        attn_terms, output, input_grad = at_once(attn_terms, output, input_grad)
     qkv_old = (qkv_master, qkv_first, qkv_second, qkv_average)
     proj_old = (proj_master, proj_first, proj_second, proj_average)
     gate_up_old = (gate_up_master, gate_up_first, gate_up_second, gate_up_average)

time: 292 us -> 289 us (0.990); the launches traced: 288 us -> 288 us
  waiting for transfers between devices: 76.7 us -> 84.9 us
  other arithmetic: 27.5 us -> 23.6 us
  starting transfers between devices: 37.1 us -> 33.7 us
    all_gather x1, waiting for transfers between devices: 13.8 us -> 21.8 us  [local(): ffn_stack = lax.all_gather(ffn_block, 'dp', axis=0, tiled=False)]
    ppermute x39, starting transfers between devices: 37 us -> 33.6 us  [swap(): return lax.ppermute(x, axis, [(i, i ^ bit) for i in range(n)])]
    unnamed x184 -> x176, local copies, waits for them, and re-layouts: 17.4 us -> 18.6 us
  transfers between devices with their start and end apart: 41 -> 41, of which waited for: 17 -> 18; matrix products, arithmetic and copies ran while one was open for 12% -> 9% of each run, Pallas kernels for 36% -> 36%
where the time goes in v4:
time: 289 us; the launch traced here: 288 us
  Pallas kernels  106 us (37%)
  waiting for transfers between devices  84.9 us (29%)
  starting transfers between devices  33.7 us (12%)
  local copies, waits for them, and re-layouts  24.8 us (9%)
  other arithmetic  23.6 us (8%)
  between operations  15.3 us (5%)
    ppermute x39, waiting for transfers between devices, swap(): return lax.ppermute(x, axis, [(i, i ^ bit) for i in range(n)])  52 us
    ppermute x39, starting transfers between devices, swap(): return lax.ppermute(x, axis, [(i, i ^ bit) for i in range(n)])  33.6 us
    pallas_call x1, Pallas kernels, ffn_call(): pl.pallas_call(ffn_kernel, name='feed_forward', grid=(count // TALL,), in...  23.4 us
    all_gather x1, waiting for transfers between devices, local(): ffn_stack = lax.all_gather(ffn_block, 'dp', axis=0, tiled=False)  21.8 us
    unnamed x176, local copies, waits for them, and re-layouts  18.6 us
    pallas_call x1, Pallas kernels, attend_call(): pl.pallas_call(attend_kernel, name='attend', grid=(windows, tiles), in_sp...  16.2 us
    reduce_scatter x1, waiting for transfers between devices, local(): lax.psum_scatter(wide_blocks, 'dp', scatter_dimension=0, tiled=False)  11 us
    pallas_call x1, Pallas kernels, back_call(): pl.pallas_call(back_kernel, name='attend_back', grid=(windows,), in_specs...  9.8 us
  transfers between devices with their start and end apart: 41, of which 18 were waited for; matrix products, arithmetic and copies ran while one was open for 9% of the time, Pallas kernels for 36%

profile of v4, /device:TPU:0, one launch (start us, length us, event | category | flops | bytes accessed | tf_op | source)
XLA Modules:
  0.0 288.4 jit_solution(13928650354465304094)
XLA Ops:
  8.5 1.4 convert_element_type.127
  10.9 3.0 %collective-permute-start.1 = (bf16[2048,256]{1,0:T(8,128)(2,1)S(1)}, bf16[2048,256]{1,0:T(8,128)(2,1)S(1)}, u32[]{:S(2)}, u32[]{:S(2)}) collective-permute-start(bf16[2048,256]{1,0:T(8,128)(2,1)S(1)} %copy-done.8), channel_id=1, source_target_pairs={{0,2},{1,3},{2,0},{3,1},{4,6},{5,7},{6,4},{7,5},{8,10},{9,11},{10,... | collective-permute-start | bytes 3145736 | tf_op jit(solution)/shard_map/ppermute | solution.py:53
  14.2 1.6 collective-permute-start.9
  15.8 1.6 collective-permute-start.7
  17.3 2.6 collective-permute-start.5
  20.2 3.2 %fusion.4 = (f32[1024,32]{1,0:T(8,128)}, f32[1024,32]{1,0:T(8,128)}, f32[1024,32]{1,0:T(8,128)}) fusion(f32[32]{0:T(128)S(1)} %multiply_power_fusion, f32[1024]{0:T(1024)S(1)} %iota_convert_fusion), kind=kLoop, calls=%fused_computation.24 | loop fusion | flops 65536 | bytes 397440 | tf_op jit(solution)/shard_map/neg | solution.py:77
  23.3 4.5 %pad_maximum_fusion.1 = (f32[1024,128]{1,0:T(8,128)}, f32[1024,128]{1,0:T(8,128)}) fusion(f32[1024,32]{1,0:T(8,128)} %get-tuple-element.333, f32[1024,32]{1,0:T(8,128)} %get-tuple-element.332, f32[1024,32]{1,0:T(8,128)} %get-tuple-element.331), kind=kLoop, calls=%fused_computation.13 | loop fusion | flops 786432 | bytes 1441792 | tf_op jit(solution)/shard_map/concatenate | solution.py:76
  27.8 6.0 %collective-permute-done.7.refs_5_ = bf16[528,256]{1,0:T(8,128)(2,1)S(1)} collective-permute-done((bf16[528,256]{1,0:T(8,128)(2,1)S(1)}, bf16[528,256]{1,0:T(8,128)(2,1)S(1)}, u32[]{:S(2)}, u32[]{:S(2)}) %collective-permute-start.7) | collective-permute-done | bytes 270368 | tf_op jit(solution)/shard_map/ppermute | solution.py:53
  33.8 12.4 %collective-permute-done.5.refs_3_ = bf16[528,256]{1,0:T(8,128)(2,1)S(1)} collective-permute-done((bf16[528,256]{1,0:T(8,128)(2,1)S(1)}, bf16[528,256]{1,0:T(8,128)(2,1)S(1)}, u32[]{:S(2)}, u32[]{:S(2)}) %collective-permute-start.5) | collective-permute-done | bytes 270368 | tf_op jit(solution)/shard_map/ppermute | solution.py:53
  46.5 2.4 collective-permute-done.3.refs_1_
  50.7 2.1 collective-permute-done.6.refs_2_
  52.8 2.9 %collective-permute-done.4.refs_0_ = bf16[528,256]{1,0:T(8,128)(2,1)} collective-permute-done((bf16[528,256]{1,0:T(8,128)(2,1)}, bf16[528,256]{1,0:T(8,128)(2,1)}, u32[]{:S(2)}, u32[]{:S(2)}) %collective-permute-start.4) | collective-permute-done | bytes 270368 | tf_op jit(solution)/shard_map/ppermute | solution.py:53
  55.7 1.9 place_attention.1
  58.5 1.3 copy-done.6
  60.7 1.9 copy-done.22
  62.6 8.5 %qkv.1 = (bf16[3,2048,256]{2,1,0:T(8,128)(2,1)S(1)}, bf16[2048,1024]{1,0:T(8,128)(2,1)S(1)}, f32[2048,1]{1,0:T(8,128)S(1)}, bf16[320,1024]{1,0:T(8,128)(2,1)S(1)}, bf16[320,256]{1,0:T(8,128)(2,1)S(1)}) custom-call(bf16[2048,256]{1,0:T(8,128)(2,1)S(1)} %copy-done.9, bf16[2048,256]{1,0:T(8,128)(2,1)S(1)} %collective-permute-done.x1, ...), custom_call_target="tpu_custom_call" | custom-call | flops 1000 | bytes 1000 | tf_op jit(solution)/shard_map/qkv/pallas_call | solution.py:226
  71.2 16.2 %attend.1 = (bf16[2048,256]{1,0:T(8,128)(2,1)}, bf16[320,256]{1,0:T(8,128)(2,1)S(1)}) custom-call(bf16[3,2048,256]{2,1,0:T(8,128)(2,1)S(1)} %get-tuple-element.177.q_ref.k_ref.v_ref.a_ref, bf16[3,2048,256]{2,1,0:T(8,128)(2,1)S(1)} %get-tuple-element.177.q_ref.k_ref.v_ref.a_ref, bf16[3,2048,256]{2,1,0:T(8,128)(2,1)S(1)} %get-tuple-element.177.q_ref.k_ref.v_ref.a_ref, ...), custom_call_target="tpu_custom_call" | custom-call | flops 1000 | bytes 1000 | tf_op jit(solution)/shard_map/attend/pallas_call | solution.py:297
  88.2 1.7 collective-permute-start.12
  90.7 4.7 %collective-permute-done.12 = bf16[640,256]{1,0:T(8,128)(2,1)} collective-permute-done((bf16[640,256]{1,0:T(8,128)(2,1)S(1)}, bf16[640,256]{1,0:T(8,128)(2,1)}, u32[]{:S(2)}, u32[]{:S(2)}) %collective-permute-start.12) | collective-permute-done | bytes 327712 | tf_op jit(solution)/shard_map/ppermute | solution.py:53
  97.4 1.7 collective-permute-start.18
  105.7 1.5 convert_multiply_fusion
  107.2 21.8 %all-gather.3.cloned.1.call-done = bf16[24,128,1024]{2,1,0:T(8,128)(2,1)} async-done(((bf16[3,128,1024]{2,1,0:T(8,128)(2,1)}), bf16[24,128,1024]{2,1,0:T(8,128)(2,1)}) %all-gather.3.cloned.1.call-update) | async-done | bytes 6291472 | tf_op jit(solution)/shard_map/all_gather | solution.py:1010
  129.0 2.8 copy-done.12
  131.8 2.8 place_feed_forward.1
  134.6 9.6 %masked_rows.1 = (bf16[8,128,2048]{2,1,0:T(8,128)(2,1)S(1)}, bf16[4,128,1024]{2,1,0:T(8,128)(2,1)S(1)}, bf16[4,128,1024]{2,1,0:T(8,128)(2,1)S(1)}, bf16[320,512]...) custom-call(s32[16]{0:T(128)S(1)} %pad_add_fusion.1.pos_ref, ...), custom_call_target="tpu_custom_call" | custom-call | flops 1000 | bytes 1000 | tf_op jit(solution)/shard_map/masked_rows/pallas_call | solution.py:535
  145.8 1.5 fusion.16
  150.4 1.5 collective-permute-start.17
  152.1 13.1 %collective-permute-done.22.refs_0_ = bf16[2,128,1024]{2,1,0:T(8,128)(2,1)} collective-permute-done((bf16[2,128,1024]{2,1,0:T(8,128)(2,1)}, bf16[2,128,1024]{2,1,0:T(8,128)(2,1)}, u32[]{:S(2)}, u32[]{:S(2)}) %collective-permute-start.22) | collective-permute-done | bytes 524320 | tf_op jit(solution)/shard_map/ppermute | solution.py:53
  169.8 1.3 copy-done.40
  172.6 9.8 %attend_back.1 = (bf16[2048,768]{1,0:T(8,128)(2,1)S(1)}, f32[1,2048]{1,0:T(1,128)S(1)}) custom-call(bf16[320,256]{1,0:T(8,128)(2,1)S(1)} %copy-done.65, bf16[320,256]{1,0:T(8,128)(2,1)S(1)} %get-tuple-element.193.do_ref, bf16[3,2048,256]{2,1,0:T(8,128)(2,1)S(1)} %get-tuple-element.177.q_ref.k_ref.v_ref.a_ref, ...), custom_call_target="tpu_custom_call" | custom-call | flops 1000 | bytes 1000 | tf_op jit(solution)/shard_map/attend_back/pallas_call | solution.py:754
  182.4 6.8 %pack_attention.1 = (bf16[4,144,1024]{2,1,0:T(8,128)(2,1)S(1)}, bf16[4,144,1024]{2,1,0:T(8,128)(2,1)S(1)}) custom-call(s32[8]{0:T(128)S(1)} %pad_add_fusion.pos_ref, bf16[2048,1024]{1,0:T(8,128)(2,1)S(1)} %copy-done.27, bf16[2048,768]{1,0:T(8,128)(2,1)S(1)} %get-tuple-element.208.d_ref, bf16[320,1024]{1,0:T(8,128)(2,1)S(1)} %get-tuple-element.195.seed_ref, ...), custom_call_target="tpu_custom_call" | custom-call | flops 1000 | bytes 1000 | tf_op jit(solution)/shard_map/pack_attention/pallas_call | solution.py:654
  189.3 1.5 add_down.1
  191.1 3.9 %first_grad.1 = (bf16[2048,512]{1,0:T(8,128)(2,1)S(1)}, bf16[2048,256]{1,0:T(8,128)(2,1)S(1)}, bf16[2048,256]{1,0:T(8,128)(2,1)S(1)}) custom-call(bf16[2048,768]{1,0:T(8,128)(2,1)S(1)} %get-tuple-element.208.d_ref, bf16[4,256,1024]{2,1,0:T(8,128)(2,1)S(1)} %copy-done.7), custom_call_target="tpu_custom_call" | custom-call | flops 1000 | bytes 1000 | tf_op jit(solution)/shard_map/first_grad/pallas_call | solution.py:795
  196.7 1.5 collective-permute-start.27
  201.5 3.8 %collective-permute-start.30 = (bf16[128,1024]{1,0:T(8,128)(2,1)S(1)}, bf16[128,1024]{1,0:T(8,128)(2,1)S(1)}, u32[]{:S(2)}, u32[]{:S(2)}) collective-permute-start(bf16[128,1024]{1,0:T(8,128)(2,1)S(1)} %get-tuple-element.235), channel_id=1, source_target_pairs={{0,24},{4,28},{8,16},{12,20},{16,8},{20,12},{24,0},{28,4},{1,25},{... | collective-permute-start | bytes 786440 | tf_op jit(solution)/shard_map/ppermute | solution.py:53
  205.3 23.4 %feed_forward.1 = (bf16[2048,512]{1,0:T(8,128)(2,1)}, bf16[2048,256]{1,0:T(8,128)(2,1)S(1)}, bf16[2048,256]{1,0:T(8,128)(2,1)S(1)}, f32[2048,256]{1,0:T(8,128)}) custom-call(bf16[2048,256]{1,0:T(8,128)(2,1)S(1)} %copy-done.10, bf16[2048,256]{1,0:T(8,128)(2,1)} %copy-done.23, bf16[2048,256]{1,0:T(8,128)(2,1)} %copy-done.21, bf16[2048,256]{1,0:T(8,128)(2,1)} %copy-done.24, ...), custom_call_target="tpu_custom_call" | custom-call | flops 1000 | bytes 1000 | tf_op jit(solution)/shard_map/feed_forward/pallas_call | solution.py:404
  228.8 3.4 %collective-permute-done.27.refs_0_ = bf16[4,144,1024]{2,1,0:T(8,128)(2,1)S(1)} collective-permute-done((bf16[4,144,1024]{2,1,0:T(8,128)(2,1)S(1)}, bf16[4,144,1024]{2,1,0:T(8,128)(2,1)S(1)}, u32[]{:S(2)}, u32[]{:S(2)}) %collective-permute-start.27) | collective-permute-done | bytes 1179680 | tf_op jit(solution)/shard_map/ppermute | solution.py:53
  232.3 1.3 add_attention.1
  233.6 2.4 adam_down.1
  236.6 2.2 convert_add_fusion
  240.2 3.8 %collective-permute-start.35 = (bf16[144,1024]{1,0:T(8,128)(2,1)}, bf16[144,1024]{1,0:T(8,128)(2,1)}, u32[]{:S(2)}, u32[]{:S(2)}) collective-permute-start(bf16[144,1024]{1,0:T(8,128)(2,1)} %get-tuple-element.265), channel_id=1, source_target_pairs={{0,24},{4,28},{8,16},{12,20},{16,8},{20,12},{24,0},{28,4},{1,25},{... | collective-permute-start | bytes 884744 | tf_op jit(solution)/shard_map/ppermute | solution.py:53
  244.0 11.0 %reduce-scatter.2.cloned.1.call-done = bf16[1,128,2048]{2,1,0:T(8,128)(2,1)} async-done(((bf16[8,128,2048]{2,1,0:T(8,128)(2,1)}), bf16[1,128,2048]{2,1,0:T(8,128)(2,1)}) %reduce-scatter.2.cloned.1.call-update) | async-done | bytes 524304 | tf_op jit(solution)/shard_map/reduce_scatter | solution.py:1071
  255.0 5.6 %adam_gate_up.1 = (f32[2,128,1024]{2,1,0:T(8,128)}, f32[2,128,1024]{2,1,0:T(8,128)}, f32[2,128,1024]{2,1,0:T(8,128)}, f32[2,128,1024]{2,1,0:T(8,128)}, f32[2,128...) custom-call(bf16[128,2048]{1,0:T(8,128)(2,1)} %bitcast.32, f32[2,128,1024]{2,1,0:T(8,128)} %refs_1_.1, ...), custom_call_target="tpu_custom_call" | custom-call | tf_op jit(solution)/shard_map/adam_gate_up/pallas_call | solution.py:893
  264.3 4.3 %input_grad.1 = bf16[2048,256]{1,0:T(8,128)(2,1)} custom-call(bf16[2048,256]{1,0:T(8,128)(2,1)S(1)} %copy-done.10, f32[2048,1]{1,0:T(8,128)S(1)} %copy-done.44, f32[1,2048]{1,0:T(1,128)S(1)} %add.101.dot_ref, bf16[2048,256]{1,0:T(8,128)(2,1)S(1)} %copy-done.46, bf16[2048,256]{1,0:T(8,128)(2,1)S(1)} %slice.128.near_ref, bf16[2048,256]{1,0:T(8,128)(2,1)S(1)} %copy-done.48, ...), custom_call_target="tpu_custom_call" | custom-call | flops 1000 | bytes 1000 | tf_op jit(solution)/shard_map/input_grad/pallas_call | solution.py:833
  268.7 2.6 add_convert_fusion
  271.4 3.5 %adam_qkv.1 = (f32[3,128,256]{2,1,0:T(8,128)}, f32[3,128,256]{2,1,0:T(8,128)}, f32[3,128,256]{2,1,0:T(8,128)}, f32[3,128,256]{2,1,0:T(8,128)}, f32[3,128,256]{2,...) custom-call(f32[144,1024]{1,0:T(8,128)S(1)} %get-tuple-element.280.refs_0_, ...), custom_call_target="tpu_custom_call" | custom-call | tf_op jit(solution)/shard_map/adam_qkv/pallas_call | solution.py:893
  276.2 1.6 collective-permute-start.38
  278.4 1.9 adam_proj.1
  (287 shorter events, 41.4 us)
Async XLA Ops:
  7.2 121.8 %all-gather.3.cloned.1.call-start = ((), (), s32[]{:S(2)}) async-start(), calls=%async_computation.2 | async-start | bytes 7077888 | tf_op jit(solution)/shard_map/all_gather | solution.py:1010
  10.9 244.2 %reduce-scatter.2.cloned.1.call-start = ((), (), s32[]{:S(2)}) async-start(), calls=%async_computation.1 | async-start | bytes 4718592 | tf_op jit(solution)/shard_map/reduce_scatter | solution.py:1071
  10.9 39.3 %collective-permute-start.1 = (bf16[2048,256]{1,0:T(8,128)(2,1)S(1)}, bf16[2048,256]{1,0:T(8,128)(2,1)S(1)}, u32[]{:S(2)}, u32[]{:S(2)}) collective-permute-start(bf16[2048,256]{1,0:T(8,128)(2,1)S(1)} %copy-done.8), channel_id=1, source_target_pairs={{0,2},{1,3},{2,0},{3,1},{4,6},{5,7},{6,4},{7,5},{8,10},{9,11},{10,... | collective-permute-start | bytes 3145736 | tf_op jit(solution)/shard_map/ppermute | solution.py:53
  14.2 35.9 %collective-permute-start.9 = (bf16[528,256]{1,0:T(8,128)(2,1)S(1)}, bf16[528,256]{1,0:T(8,128)(2,1)S(1)}, u32[]{:S(2)}, u32[]{:S(2)}) collective-permute-start(bf16[528,256]{1,0:T(8,128)(2,1)S(1)} %constant_dynamic-update-slice_fusion.refs_7_), channel_id=1, source_target_pairs={{0,4},{4,0},{8,12},{12,8},{16,20},{20,16},{24,28},{28,24},{1,5},{5... | collective-permute-start | bytes 811016 | tf_op jit(solution)/shard_map/ppermute | solution.py:53
  15.8 18.0 %collective-permute-start.7 = (bf16[528,256]{1,0:T(8,128)(2,1)S(1)}, bf16[528,256]{1,0:T(8,128)(2,1)S(1)}, u32[]{:S(2)}, u32[]{:S(2)}) collective-permute-start(bf16[528,256]{1,0:T(8,128)(2,1)S(1)} %constant_dynamic-update-slice_fusion.refs_7_), channel_id=1, source_target_pairs={{0,8},{4,12},{8,0},{12,4},{16,24},{20,28},{24,16},{28,20},{1,9},{5... | collective-permute-start | bytes 811016 | tf_op jit(solution)/shard_map/ppermute | solution.py:53
  17.3 28.9 %collective-permute-start.5 = (bf16[528,256]{1,0:T(8,128)(2,1)S(1)}, bf16[528,256]{1,0:T(8,128)(2,1)S(1)}, u32[]{:S(2)}, u32[]{:S(2)}) collective-permute-start(bf16[528,256]{1,0:T(8,128)(2,1)S(1)} %constant_dynamic-update-slice_fusion.refs_7_), channel_id=1, source_target_pairs={{0,16},{4,20},{8,24},{12,28},{16,0},{20,4},{24,8},{28,12},{1,17},{... | collective-permute-start | bytes 811016 | tf_op jit(solution)/shard_map/ppermute | solution.py:53
  19.9 29.0 %collective-permute-start.3 = (bf16[528,256]{1,0:T(8,128)(2,1)S(1)}, bf16[528,256]{1,0:T(8,128)(2,1)}, u32[]{:S(2)}, u32[]{:S(2)}) collective-permute-start(bf16[528,256]{1,0:T(8,128)(2,1)S(1)} %constant_dynamic-update-slice_fusion.refs_7_), channel_id=1, source_target_pairs={{0,24},{4,28},{8,16},{12,20},{16,8},{20,12},{24,0},{28,4},{1,25},{... | collective-permute-start | bytes 811016 | tf_op jit(solution)/shard_map/ppermute | solution.py:53
  20.2 28.8 %copy-start.84 = (s32[8]{0:T(128)S(1)}, s32[8]{0:T(128)}, u32[]{:S(2)}) copy-start(s32[8]{0:T(128)} %param.31) | copy-start | bytes 100
  33.8 16.9 %collective-permute-start.8 = (bf16[528,256]{1,0:T(8,128)(2,1)S(1)}, bf16[528,256]{1,0:T(8,128)(2,1)}, u32[]{:S(2)}, u32[]{:S(2)}) collective-permute-start(bf16[528,256]{1,0:T(8,128)(2,1)S(1)} %collective-permute-done.7.refs_5_), channel_id=1, source_target_pairs={{0,4},{4,0},{8,12},{12,8},{16,20},{20,16},{24,28},{28,24},{1,5},{5... | collective-permute-start | bytes 811016 | tf_op jit(solution)/shard_map/ppermute | solution.py:53
  46.2 6.6 %collective-permute-start.6 = (bf16[528,256]{1,0:T(8,128)(2,1)S(1)}, bf16[528,256]{1,0:T(8,128)(2,1)}, u32[]{:S(2)}, u32[]{:S(2)}) collective-permute-start(bf16[528,256]{1,0:T(8,128)(2,1)S(1)} %collective-permute-done.5.refs_3_), channel_id=1, source_target_pairs={{0,4},{4,0},{8,12},{12,8},{16,20},{20,16},{24,28},{28,24},{1,5},{5... | collective-permute-start | bytes 811016 | tf_op jit(solution)/shard_map/ppermute | solution.py:53
  48.9 6.8 %collective-permute-start.4 = (bf16[528,256]{1,0:T(8,128)(2,1)}, bf16[528,256]{1,0:T(8,128)(2,1)}, u32[]{:S(2)}, u32[]{:S(2)}) collective-permute-start(bf16[528,256]{1,0:T(8,128)(2,1)} %collective-permute-done.3.refs_1_), channel_id=1, source_target_pairs={{0,4},{4,0},{8,12},{12,8},{16,20},{20,16},{24,28},{28,24},{1,5},{5... | collective-permute-start | bytes 811016 | tf_op jit(solution)/shard_map/ppermute | solution.py:53
  50.1 37.4 %copy-start.71 = (bf16[2,160,256]{2,1,0:T(8,128)(2,1)}, bf16[2,160,256]{2,1,0:T(8,128)(2,1)S(1)}, u32[]{:S(2)}) copy-start(bf16[2,160,256]{2,1,0:T(8,128)(2,1)S(1)} %pad.15) | copy-start | bytes 491524
  50.1 10.2 %collective-permute-start = (bf16[2048,256]{1,0:T(8,128)(2,1)S(1)}, bf16[2048,256]{1,0:T(8,128)(2,1)S(1)}, u32[]{:S(2)}, u32[]{:S(2)}) collective-permute-start(bf16[2048,256]{1,0:T(8,128)(2,1)S(1)} %copy-done.8), channel_id=1, source_target_pairs={{0,1},{1,0},{2,3},{3,2},{4,5},{5,4},{6,7},{7,6},{8,9},{9,8},{10,11... | collective-permute-start | bytes 3145736 | tf_op jit(solution)/shard_map/ppermute | solution.py:53
  50.2 10.2 %collective-permute-start.2 = (bf16[2048,256]{1,0:T(8,128)(2,1)S(1)}, bf16[2048,256]{1,0:T(8,128)(2,1)S(1)}, u32[]{:S(2)}, u32[]{:S(2)}) collective-permute-start(bf16[2048,256]{1,0:T(8,128)(2,1)S(1)} %collective-permute-done.1.x2), channel_id=1, source_target_pairs={{0,1},{1,0},{2,3},{3,2},{4,5},{5,4},{6,7},{7,6},{8,9},{9,8},{10,11... | collective-permute-start | bytes 3145736 | tf_op jit(solution)/shard_map/ppermute | solution.py:53
  59.9 11.2 %collective-permute-start.10 = (bf16[256,1024]{1,0:T(8,128)(2,1)S(1)}, bf16[256,1024]{1,0:T(8,128)(2,1)S(1)}, u32[]{:S(2)}, u32[]{:S(2)}) collective-permute-start(bf16[256,1024]{1,0:T(8,128)(2,1)S(1)} %slice_bitcast_fusion.o0), channel_id=1, source_target_pairs={{0,2},{1,3},{2,0},{3,1},{4,6},{5,7},{6,4},{7,5},{8,10},{9,11},{10,... | collective-permute-start | bytes 1572872 | tf_op jit(solution)/shard_map/ppermute | solution.py:53
  71.1 18.7 %copy-start.82 = (s32[16]{0:T(128)S(1)}, s32[16]{0:T(128)}, u32[]{:S(2)}) copy-start(s32[16]{0:T(128)} %param.30) | copy-start | bytes 196
  71.2 19.3 %copy-start.83 = (s32[2]{0:T(128)S(1)}, s32[2]{0:T(128)}, u32[]{:S(2)}) copy-start(s32[2]{0:T(128)} %param.29) | copy-start | bytes 28
  88.2 7.2 %collective-permute-start.12 = (bf16[640,256]{1,0:T(8,128)(2,1)S(1)}, bf16[640,256]{1,0:T(8,128)(2,1)}, u32[]{:S(2)}, u32[]{:S(2)}) collective-permute-start(bf16[640,256]{1,0:T(8,128)(2,1)S(1)} %pad_maximum_fusion.3), channel_id=1, source_target_pairs={{0,2},{1,3},{2,0},{3,1},{4,6},{5,7},{6,4},{7,5},{8,10},{9,11},{10,... | collective-permute-start | bytes 983048 | tf_op jit(solution)/shard_map/ppermute | solution.py:53
  95.4 2.0 collective-permute-start.13
  96.4 4.2 %collective-permute-start.11 = (bf16[640,256]{1,0:T(8,128)(2,1)}, bf16[640,256]{1,0:T(8,128)(2,1)S(1)}, u32[]{:S(2)}, u32[]{:S(2)}) collective-permute-start(bf16[640,256]{1,0:T(8,128)(2,1)} %copy-done.75), channel_id=1, source_target_pairs={{0,1},{1,0},{2,3},{3,2},{4,5},{5,4},{6,7},{7,6},{8,9},{9,8},{10,11... | collective-permute-start | bytes 983048 | tf_op jit(solution)/shard_map/ppermute | solution.py:53
  97.4 47.8 %collective-permute-start.18 = (bf16[2048,256]{1,0:T(8,128)(2,1)}, bf16[2048,256]{1,0:T(8,128)(2,1)}, u32[]{:S(2)}, u32[]{:S(2)}) collective-permute-start(bf16[2048,256]{1,0:T(8,128)(2,1)} %get-tuple-element.223.c0), channel_id=1, source_target_pairs={{0,2},{1,3},{2,0},{3,1},{4,6},{5,7},{6,4},{7,5},{8,10},{9,11},{10,... | collective-permute-start | bytes 3145736 | tf_op jit(solution)/shard_map/ppermute | solution.py:53
  99.1 2.7 collective-permute-start.14
  99.1 2.9 collective-permute-start.15
  145.2 20.8 %collective-permute-start.19 = (bf16[2048,256]{1,0:T(8,128)(2,1)}, bf16[2048,256]{1,0:T(8,128)(2,1)}, u32[]{:S(2)}, u32[]{:S(2)}) collective-permute-start(bf16[2048,256]{1,0:T(8,128)(2,1)} %get-tuple-element.223.c0), channel_id=1, source_target_pairs={{0,1},{1,0},{2,3},{3,2},{4,5},{5,4},{6,7},{7,6},{8,9},{9,8},{10,11... | collective-permute-start | bytes 3145736 | tf_op jit(solution)/shard_map/ppermute | solution.py:53
  145.2 20.8 %collective-permute-start.20 = (bf16[2048,256]{1,0:T(8,128)(2,1)}, bf16[2048,256]{1,0:T(8,128)(2,1)}, u32[]{:S(2)}, u32[]{:S(2)}) collective-permute-start(bf16[2048,256]{1,0:T(8,128)(2,1)} %collective-permute-done.18.c2), channel_id=1, source_target_pairs={{0,1},{1,0},{2,3},{3,2},{4,5},{5,4},{6,7},{7,6},{8,9},{9,8},{10,11... | collective-permute-start | bytes 3145736 | tf_op jit(solution)/shard_map/ppermute | solution.py:53
  145.7 3.1 %collective-permute-start.16 = (bf16[320,512]{1,0:T(8,128)(2,1)S(1)}, bf16[320,512]{1,0:T(8,128)(2,1)S(1)}, u32[]{:S(2)}, u32[]{:S(2)}) collective-permute-start(bf16[320,512]{1,0:T(8,128)(2,1)S(1)} %get-tuple-element.184), channel_id=1, source_target_pairs={{0,1},{1,0},{2,3},{3,2},{4,5},{5,4},{6,7},{7,6},{8,9},{9,8},{10,11... | collective-permute-start | bytes 983048 | tf_op jit(solution)/shard_map/ppermute | solution.py:53
  147.3 17.8 %collective-permute-start.22 = (bf16[2,128,1024]{2,1,0:T(8,128)(2,1)}, bf16[2,128,1024]{2,1,0:T(8,128)(2,1)}, u32[]{:S(2)}, u32[]{:S(2)}) collective-permute-start(bf16[2,128,1024]{2,1,0:T(8,128)(2,1)} %get-tuple-element.316), channel_id=1, source_target_pairs={{0,4},{4,0},{8,12},{12,8},{16,20},{20,16},{24,28},{28,24},{1,5},{5... | collective-permute-start | bytes 1572872 | tf_op jit(solution)/shard_map/ppermute | solution.py:53
  150.4 15.6 %collective-permute-start.17 = (bf16[320,512]{1,0:T(8,128)(2,1)}, bf16[320,512]{1,0:T(8,128)(2,1)}, u32[]{:S(2)}, u32[]{:S(2)}) collective-permute-start(bf16[320,512]{1,0:T(8,128)(2,1)} %pad_maximum_fusion.4), channel_id=1, source_target_pairs={{0,2},{1,3},{2,0},{3,1},{4,6},{5,7},{6,4},{7,5},{8,10},{9,11},{10,... | collective-permute-start | bytes 983048 | tf_op jit(solution)/shard_map/ppermute | solution.py:53
  152.0 17.8 %copy-start.1 = (bf16[4,1024,256]{2,1,0:T(8,128)(2,1)S(1)}, bf16[4,1024,256]{2,1,0:T(8,128)(2,1)}, u32[]{:S(2)}) copy-start(bf16[4,1024,256]{2,1,0:T(8,128)(2,1)} %copy-done) | copy-start | bytes 6291460
  152.0 17.8 %copy-start.13 = (f32[320,1024]{1,0:T(8,128)S(1)}, f32[320,1024]{1,0:T(8,128)}, u32[]{:S(2)}) copy-start(f32[320,1024]{1,0:T(8,128)} %get-tuple-element.317.seed_ref) | copy-start | bytes 3932164
  152.0 17.8 %copy-start.63 = (f32[320,128]{1,0:T(8,128)S(1)}, f32[320,128]{1,0:T(8,128)}, u32[]{:S(2)}) copy-start(f32[320,128]{1,0:T(8,128)} %copy-done.62) | copy-start | bytes 491524
  165.1 24.2 %collective-permute-start.23 = (bf16[2,128,1024]{2,1,0:T(8,128)(2,1)}, bf16[2,128,1024]{2,1,0:T(8,128)(2,1)S(1)}, u32[]{:S(2)}, u32[]{:S(2)}) collective-permute-start(bf16[2,128,1024]{2,1,0:T(8,128)(2,1)} %get-tuple-element.200), channel_id=1, source_target_pairs={{0,4},{4,0},{8,12},{12,8},{16,20},{20,16},{24,28},{28,24},{1,5},{5... | collective-permute-start | bytes 1572872 | tf_op jit(solution)/shard_map/ppermute | solution.py:53
  168.1 1.7 collective-permute-start.21
  190.8 4.3 %collective-permute-start.24 = (f32[1,2048]{1,0:T(1,128)S(1)}, f32[1,2048]{1,0:T(1,128)S(1)}, u32[]{:S(2)}, u32[]{:S(2)}) collective-permute-start(f32[1,2048]{1,0:T(1,128)S(1)} %get-tuple-element.211), channel_id=1, source_target_pairs={{0,1},{1,0},{2,3},{3,2},{4,5},{5,4},{6,7},{7,6},{8,9},{9,8},{10,11... | collective-permute-start | bytes 24584 | tf_op jit(solution)/shard_map/ppermute | solution.py:53
  195.1 4.2 %collective-permute-start.25 = (bf16[2048,512]{1,0:T(8,128)(2,1)S(1)}, bf16[2048,512]{1,0:T(8,128)(2,1)S(1)}, u32[]{:S(2)}, u32[]{:S(2)}) collective-permute-start(bf16[2048,512]{1,0:T(8,128)(2,1)S(1)} %get-tuple-element.212), channel_id=1, source_target_pairs={{0,1},{1,0},{2,3},{3,2},{4,5},{5,4},{6,7},{7,6},{8,9},{9,8},{10,11... | collective-permute-start | bytes 6291464 | tf_op jit(solution)/shard_map/ppermute | solution.py:53
  195.5 3.7 %collective-permute-start.26 = (f32[1,2048]{1,0:T(1,128)S(1)}, f32[1,2048]{1,0:T(1,128)S(1)}, u32[]{:S(2)}, u32[]{:S(2)}) collective-permute-start(f32[1,2048]{1,0:T(1,128)S(1)} %add.96), channel_id=1, source_target_pairs={{0,2},{1,3},{2,0},{3,1},{4,6},{5,7},{6,4},{7,5},{8,10},{9,11},{10,... | collective-permute-start | bytes 24584 | tf_op jit(solution)/shard_map/ppermute | solution.py:53
  196.7 35.5 %collective-permute-start.27 = (bf16[4,144,1024]{2,1,0:T(8,128)(2,1)S(1)}, bf16[4,144,1024]{2,1,0:T(8,128)(2,1)S(1)}, u32[]{:S(2)}, u32[]{:S(2)}) collective-permute-start(bf16[4,144,1024]{2,1,0:T(8,128)(2,1)S(1)} %get-tuple-element.231), channel_id=1, source_target_pairs={{0,4},{4,0},{8,12},{12,8},{16,20},{20,16},{24,28},{28,24},{1,5},{5... | collective-permute-start | bytes 3538952 | tf_op jit(solution)/shard_map/ppermute | solution.py:53
  199.6 32.5 %collective-permute-start.31 = (bf16[2048,256]{1,0:T(8,128)(2,1)S(1)}, bf16[2048,256]{1,0:T(8,128)(2,1)S(1)}, u32[]{:S(2)}, u32[]{:S(2)}) collective-permute-start(bf16[2048,256]{1,0:T(8,128)(2,1)S(1)} %add_convert_fusion.2), channel_id=1, source_target_pairs={{0,2},{1,3},{2,0},{3,1},{4,6},{5,7},{6,4},{7,5},{8,10},{9,11},{10,... | collective-permute-start | bytes 3145736 | tf_op jit(solution)/shard_map/ppermute | solution.py:53
  200.9 31.3 %collective-permute-start.28 = (bf16[128,1024]{1,0:T(8,128)(2,1)S(1)}, bf16[128,1024]{1,0:T(8,128)(2,1)S(1)}, u32[]{:S(2)}, u32[]{:S(2)}) collective-permute-start(bf16[128,1024]{1,0:T(8,128)(2,1)S(1)} %get-tuple-element.233), channel_id=1, source_target_pairs={{0,8},{4,12},{8,0},{12,4},{16,24},{20,28},{24,16},{28,20},{1,9},{5... | collective-permute-start | bytes 786440 | tf_op jit(solution)/shard_map/ppermute | solution.py:53
  200.9 31.3 %collective-permute-start.29 = (bf16[128,1024]{1,0:T(8,128)(2,1)S(1)}, bf16[128,1024]{1,0:T(8,128)(2,1)S(1)}, u32[]{:S(2)}, u32[]{:S(2)}) collective-permute-start(bf16[128,1024]{1,0:T(8,128)(2,1)S(1)} %get-tuple-element.234), channel_id=1, source_target_pairs={{0,16},{4,20},{8,24},{12,28},{16,0},{20,4},{24,8},{28,12},{1,17},{... | collective-permute-start | bytes 786440 | tf_op jit(solution)/shard_map/ppermute | solution.py:53
  201.5 30.7 %collective-permute-start.30 = (bf16[128,1024]{1,0:T(8,128)(2,1)S(1)}, bf16[128,1024]{1,0:T(8,128)(2,1)S(1)}, u32[]{:S(2)}, u32[]{:S(2)}) collective-permute-start(bf16[128,1024]{1,0:T(8,128)(2,1)S(1)} %get-tuple-element.235), channel_id=1, source_target_pairs={{0,24},{4,28},{8,16},{12,20},{16,8},{20,12},{24,0},{28,4},{1,25},{... | collective-permute-start | bytes 786440 | tf_op jit(solution)/shard_map/ppermute | solution.py:53
  232.2 4.4 %collective-permute-start.32 = (bf16[2048,512]{1,0:T(8,128)(2,1)}, bf16[2048,512]{1,0:T(8,128)(2,1)S(1)}, u32[]{:S(2)}, u32[]{:S(2)}) collective-permute-start(bf16[2048,512]{1,0:T(8,128)(2,1)} %get-tuple-element.238), channel_id=1, source_target_pairs={{0,1},{1,0},{2,3},{3,2},{4,5},{5,4},{6,7},{7,6},{8,9},{9,8},{10,11... | collective-permute-start | bytes 6291464 | tf_op jit(solution)/shard_map/ppermute | solution.py:53
  238.9 29.8 %collective-permute-start.36 = (bf16[2048,256]{1,0:T(8,128)(2,1)}, bf16[2048,256]{1,0:T(8,128)(2,1)}, u32[]{:S(2)}, u32[]{:S(2)}) collective-permute-start(bf16[2048,256]{1,0:T(8,128)(2,1)} %get-tuple-element.267), channel_id=1, source_target_pairs={{0,2},{1,3},{2,0},{3,1},{4,6},{5,7},{6,4},{7,5},{8,10},{9,11},{10,... | collective-permute-start | bytes 3145736 | tf_op jit(solution)/shard_map/ppermute | solution.py:53
  239.6 31.7 %collective-permute-start.33 = (bf16[144,1024]{1,0:T(8,128)(2,1)}, bf16[144,1024]{1,0:T(8,128)(2,1)}, u32[]{:S(2)}, u32[]{:S(2)}) collective-permute-start(bf16[144,1024]{1,0:T(8,128)(2,1)} %get-tuple-element.263), channel_id=1, source_target_pairs={{0,8},{4,12},{8,0},{12,4},{16,24},{20,28},{24,16},{28,20},{1,9},{5... | collective-permute-start | bytes 884744 | tf_op jit(solution)/shard_map/ppermute | solution.py:53
  239.6 31.7 %collective-permute-start.34 = (bf16[144,1024]{1,0:T(8,128)(2,1)}, bf16[144,1024]{1,0:T(8,128)(2,1)}, u32[]{:S(2)}, u32[]{:S(2)}) collective-permute-start(bf16[144,1024]{1,0:T(8,128)(2,1)} %get-tuple-element.264), channel_id=1, source_target_pairs={{0,16},{4,20},{8,24},{12,28},{16,0},{20,4},{24,8},{28,12},{1,17},{... | collective-permute-start | bytes 884744 | tf_op jit(solution)/shard_map/ppermute | solution.py:53
  240.2 31.1 %collective-permute-start.35 = (bf16[144,1024]{1,0:T(8,128)(2,1)}, bf16[144,1024]{1,0:T(8,128)(2,1)}, u32[]{:S(2)}, u32[]{:S(2)}) collective-permute-start(bf16[144,1024]{1,0:T(8,128)(2,1)} %get-tuple-element.265), channel_id=1, source_target_pairs={{0,24},{4,28},{8,16},{12,20},{16,8},{20,12},{24,0},{28,4},{1,25},{... | collective-permute-start | bytes 884744 | tf_op jit(solution)/shard_map/ppermute | solution.py:53
  275.0 1.2 collective-permute-start.37
  276.2 4.2 %collective-permute-start.38 = (f32[1,128]{1,0:T(1,128)S(1)}, f32[1,128]{1,0:T(1,128)S(1)}, u32[]{:S(2)}, u32[]{:S(2)}) collective-permute-start(f32[1,128]{1,0:T(1,128)S(1)} %bitcast_add_fusion), channel_id=1, source_target_pairs={{0,2},{1,3},{2,0},{3,1},{4,6},{5,7},{6,4},{7,5},{8,10},{9,11},{10,... | collective-permute-start | bytes 1544 | tf_op jit(solution)/shard_map/ppermute | solution.py:53
  (78 other events, 432.5 us)
Sparse Core Ops, SparseCore 0:
  11.0 117.9 all-gather.2
  152.0 102.9 reduce-scatter.1

commit v5 on v4

--- a/solution.py
+++ b/solution.py
@@ -1123,16 +1123,16 @@
     down_rate = FF ** (-0.5)
     if short:
         down_out = adam_rows(down_terms, 0, down_old, down_rate, "down")
-        f_near, attn_added, down_out = at_once(f_near, attn_added, down_out)
+        f_near, attn_added = at_once(f_near, attn_added)
     f_half = (f_far.astype(F32) + f_near[:, share:].astype(F32)).astype(BF)
-    f_part = residual + f_keep.astype(F32) + f_near[:, :share].astype(F32)
-    if short:
-        f_half, attn_added, f_part = at_once(f_half, attn_added, f_part)
+    if short:
+        f_half, attn_added = at_once(f_half, attn_added)
     f_back = swap(f_half, "mp", 2)
     if short:
         attn_terms = [attn_added[0]] + [swap(attn_added[k], "dp", 2 * k) for k in range(1, 4)]
     if short:
         gate_up_old = (gate_up_master, gate_up_first, gate_up_second, gate_up_average)
+        wide_sum = tie(wide_sum, down_out[0])
         gate_up_out = adam_cols([wide_sum], gate_up_old, D ** (-0.5), "gate_up", mixed=True)
         n_back = tie(n_back, gate_up_out[0])
     input_grad = input_call(
@@ -1148,7 +1148,9 @@
     )
     if short:
         f_back, input_grad = at_once(f_back, input_grad)
-    output = (f_part + f_back.astype(F32)).astype(BF)
+    output = (
+        residual + f_keep.astype(F32) + f_near[:, :share].astype(F32) + f_back.astype(F32)
+    ).astype(BF)
     if short:
         attn_terms, output, input_grad = at_once(attn_terms, output, input_grad)
     qkv_old = (qkv_master, qkv_first, qkv_second, qkv_average)

time: 289 us -> 289 us (level)
  waiting for transfers between devices: 84.9 us -> 81.3 us
  starting transfers between devices: 33.7 us -> 36.6 us
    reduce_scatter x1, waiting for transfers between devices: 11 us -> 5.09 us  [local(): lax.psum_scatter(wide_blocks, 'dp', scatter_dimension=0, tiled=False)]
    ppermute x39, starting transfers between devices: 33.6 us -> 36.5 us  [swap(): return lax.ppermute(x, axis, [(i, i ^ bit) for i in range(n)])]
    unnamed x176 -> x182, local copies, waits for them, and re-layouts: 18.6 us -> 19 us
where the time goes in v5:
time: 289 us; the launch traced here: 288 us
  Pallas kernels  106 us (37%)
  waiting for transfers between devices  81.3 us (28%)
  starting transfers between devices  36.6 us (13%)
  local copies, waits for them, and re-layouts  25.3 us (9%)
  other arithmetic  22.9 us (8%)
  between operations  15.3 us (5%)
    ppermute x39, waiting for transfers between devices, swap(): return lax.ppermute(x, axis, [(i, i ^ bit) for i in range(n)])  54.4 us
    ppermute x39, starting transfers between devices, swap(): return lax.ppermute(x, axis, [(i, i ^ bit) for i in range(n)])  36.5 us
    pallas_call x1, Pallas kernels, ffn_call(): pl.pallas_call(ffn_kernel, name='feed_forward', grid=(count // TALL,), in...  23.4 us
    all_gather x1, waiting for transfers between devices, local(): ffn_stack = lax.all_gather(ffn_block, 'dp', axis=0, tiled=False)  21.8 us
    unnamed x182, local copies, waits for them, and re-layouts  19 us
    pallas_call x1, Pallas kernels, attend_call(): pl.pallas_call(attend_kernel, name='attend', grid=(windows, tiles), in_sp...  16.2 us
    pallas_call x1, Pallas kernels, back_call(): pl.pallas_call(back_kernel, name='attend_back', grid=(windows,), in_specs...  9.81 us
    pallas_call x1, Pallas kernels, rows_pack_call(): pl.pallas_call(rows_pack_kernel, name='masked_rows', grid_spec=pltpu.Pref...  9.57 us
  transfers between devices with their start and end apart: 41, of which 18 were waited for; matrix products, arithmetic and copies ran while one was open for 9% of the time, Pallas kernels for 36%

profile of v5, /device:TPU:0, one launch (start us, length us, event | category | flops | bytes accessed | tf_op | source)
XLA Modules:
  0.0 287.6 jit_solution(6262553408369937714)
XLA Ops:
  8.5 1.4 convert_element_type.127
  10.9 3.0 %collective-permute-start.1 = (bf16[2048,256]{1,0:T(8,128)(2,1)S(1)}, bf16[2048,256]{1,0:T(8,128)(2,1)S(1)}, u32[]{:S(2)}, u32[]{:S(2)}) collective-permute-start(bf16[2048,256]{1,0:T(8,128)(2,1)S(1)} %copy-done.8), channel_id=1, source_target_pairs={{0,2},{1,3},{2,0},{3,1},{4,6},{5,7},{6,4},{7,5},{8,10},{9,11},{10,... | collective-permute-start | bytes 3145736 | tf_op jit(solution)/shard_map/ppermute | solution.py:53
  14.2 1.6 collective-permute-start.9
  15.8 1.6 collective-permute-start.7
  17.3 2.6 collective-permute-start.5
  20.2 3.2 %fusion.4 = (f32[1024,32]{1,0:T(8,128)}, f32[1024,32]{1,0:T(8,128)}, f32[1024,32]{1,0:T(8,128)}) fusion(f32[32]{0:T(128)S(1)} %multiply_power_fusion, f32[1024]{0:T(1024)S(1)} %iota_convert_fusion), kind=kLoop, calls=%fused_computation.23 | loop fusion | flops 65536 | bytes 397440 | tf_op jit(solution)/shard_map/neg | solution.py:77
  23.3 4.5 %pad_maximum_fusion.1 = (f32[1024,128]{1,0:T(8,128)}, f32[1024,128]{1,0:T(8,128)}) fusion(f32[1024,32]{1,0:T(8,128)} %get-tuple-element.319, f32[1024,32]{1,0:T(8,128)} %get-tuple-element.318, f32[1024,32]{1,0:T(8,128)} %get-tuple-element.317), kind=kLoop, calls=%fused_computation.12 | loop fusion | flops 786432 | bytes 1441792 | tf_op jit(solution)/shard_map/concatenate | solution.py:76
  27.8 6.0 %collective-permute-done.7.refs_5_ = bf16[528,256]{1,0:T(8,128)(2,1)S(1)} collective-permute-done((bf16[528,256]{1,0:T(8,128)(2,1)S(1)}, bf16[528,256]{1,0:T(8,128)(2,1)S(1)}, u32[]{:S(2)}, u32[]{:S(2)}) %collective-permute-start.7) | collective-permute-done | bytes 270368 | tf_op jit(solution)/shard_map/ppermute | solution.py:53
  33.8 12.4 %collective-permute-done.5.refs_3_ = bf16[528,256]{1,0:T(8,128)(2,1)S(1)} collective-permute-done((bf16[528,256]{1,0:T(8,128)(2,1)S(1)}, bf16[528,256]{1,0:T(8,128)(2,1)S(1)}, u32[]{:S(2)}, u32[]{:S(2)}) %collective-permute-start.5) | collective-permute-done | bytes 270368 | tf_op jit(solution)/shard_map/ppermute | solution.py:53
  46.5 2.4 collective-permute-done.3.refs_1_
  50.7 2.1 collective-permute-done.6.refs_2_
  52.8 2.9 %collective-permute-done.4.refs_0_ = bf16[528,256]{1,0:T(8,128)(2,1)} collective-permute-done((bf16[528,256]{1,0:T(8,128)(2,1)}, bf16[528,256]{1,0:T(8,128)(2,1)}, u32[]{:S(2)}, u32[]{:S(2)}) %collective-permute-start.4) | collective-permute-done | bytes 270368 | tf_op jit(solution)/shard_map/ppermute | solution.py:53
  55.7 1.9 place_attention.1
  60.7 1.9 copy-done.22
  62.5 8.5 %qkv.1 = (bf16[3,2048,256]{2,1,0:T(8,128)(2,1)S(1)}, bf16[2048,1024]{1,0:T(8,128)(2,1)S(1)}, f32[2048,1]{1,0:T(8,128)S(1)}, bf16[320,1024]{1,0:T(8,128)(2,1)S(1)}, bf16[320,256]{1,0:T(8,128)(2,1)S(1)}) custom-call(bf16[2048,256]{1,0:T(8,128)(2,1)S(1)} %copy-done.9, bf16[2048,256]{1,0:T(8,128)(2,1)S(1)} %collective-permute-done.x1, ...), custom_call_target="tpu_custom_call" | custom-call | flops 1000 | bytes 1000 | tf_op jit(solution)/shard_map/qkv/pallas_call | solution.py:226
  71.2 16.2 %attend.1 = (bf16[2048,256]{1,0:T(8,128)(2,1)}, bf16[320,256]{1,0:T(8,128)(2,1)S(1)}) custom-call(bf16[3,2048,256]{2,1,0:T(8,128)(2,1)S(1)} %get-tuple-element.171.q_ref.k_ref.v_ref.a_ref, bf16[3,2048,256]{2,1,0:T(8,128)(2,1)S(1)} %get-tuple-element.171.q_ref.k_ref.v_ref.a_ref, bf16[3,2048,256]{2,1,0:T(8,128)(2,1)S(1)} %get-tuple-element.171.q_ref.k_ref.v_ref.a_ref, ...), custom_call_target="tpu_custom_call" | custom-call | flops 1000 | bytes 1000 | tf_op jit(solution)/shard_map/attend/pallas_call | solution.py:297
  88.2 1.7 collective-permute-start.12
  90.7 4.7 %collective-permute-done.12 = bf16[640,256]{1,0:T(8,128)(2,1)} collective-permute-done((bf16[640,256]{1,0:T(8,128)(2,1)S(1)}, bf16[640,256]{1,0:T(8,128)(2,1)}, u32[]{:S(2)}, u32[]{:S(2)}) %collective-permute-start.12) | collective-permute-done | bytes 327712 | tf_op jit(solution)/shard_map/ppermute | solution.py:53
  97.4 1.7 collective-permute-start.18
  105.6 1.5 convert_multiply_fusion
  107.2 21.8 %all-gather.3.cloned.1.call-done = bf16[24,128,1024]{2,1,0:T(8,128)(2,1)} async-done(((bf16[3,128,1024]{2,1,0:T(8,128)(2,1)}), bf16[24,128,1024]{2,1,0:T(8,128)(2,1)}) %all-gather.3.cloned.1.call-update) | async-done | bytes 6291472 | tf_op jit(solution)/shard_map/all_gather | solution.py:1010
  129.0 2.8 copy-done.12
  131.8 2.8 place_feed_forward.1
  134.6 9.6 %masked_rows.1 = (bf16[8,128,2048]{2,1,0:T(8,128)(2,1)S(1)}, bf16[4,128,1024]{2,1,0:T(8,128)(2,1)S(1)}, bf16[4,128,1024]{2,1,0:T(8,128)(2,1)S(1)}, bf16[320,512]...) custom-call(s32[16]{0:T(128)S(1)} %pad_add_fusion.1.pos_ref, ...), custom_call_target="tpu_custom_call" | custom-call | flops 1000 | bytes 1000 | tf_op jit(solution)/shard_map/masked_rows/pallas_call | solution.py:535
  145.8 1.5 fusion.16
  150.4 1.5 collective-permute-start.17
  152.0 13.1 %collective-permute-done.22.refs_0_ = bf16[2,128,1024]{2,1,0:T(8,128)(2,1)} collective-permute-done((bf16[2,128,1024]{2,1,0:T(8,128)(2,1)}, bf16[2,128,1024]{2,1,0:T(8,128)(2,1)}, u32[]{:S(2)}, u32[]{:S(2)}) %collective-permute-start.22) | collective-permute-done | bytes 524320 | tf_op jit(solution)/shard_map/ppermute | solution.py:53
  169.8 1.3 copy-done.40
  172.6 9.8 %attend_back.1 = (bf16[2048,768]{1,0:T(8,128)(2,1)S(1)}, f32[1,2048]{1,0:T(1,128)S(1)}) custom-call(bf16[320,256]{1,0:T(8,128)(2,1)S(1)} %copy-done.67, bf16[320,256]{1,0:T(8,128)(2,1)S(1)} %get-tuple-element.187.do_ref, bf16[3,2048,256]{2,1,0:T(8,128)(2,1)S(1)} %get-tuple-element.171.q_ref.k_ref.v_ref.a_ref, ...), custom_call_target="tpu_custom_call" | custom-call | flops 1000 | bytes 1000 | tf_op jit(solution)/shard_map/attend_back/pallas_call | solution.py:754
  182.4 6.8 %pack_attention.1 = (bf16[4,144,1024]{2,1,0:T(8,128)(2,1)S(1)}, bf16[4,144,1024]{2,1,0:T(8,128)(2,1)S(1)}) custom-call(s32[8]{0:T(128)S(1)} %pad_add_fusion.pos_ref, bf16[2048,1024]{1,0:T(8,128)(2,1)S(1)} %copy-done.27, bf16[2048,768]{1,0:T(8,128)(2,1)S(1)} %get-tuple-element.202.d_ref, bf16[320,1024]{1,0:T(8,128)(2,1)S(1)} %get-tuple-element.189.seed_ref, ...), custom_call_target="tpu_custom_call" | custom-call | flops 1000 | bytes 1000 | tf_op jit(solution)/shard_map/pack_attention/pallas_call | solution.py:654
  189.3 1.5 add_down.1
  191.0 3.9 %first_grad.1 = (bf16[2048,512]{1,0:T(8,128)(2,1)S(1)}, bf16[2048,256]{1,0:T(8,128)(2,1)S(1)}, bf16[2048,256]{1,0:T(8,128)(2,1)S(1)}) custom-call(bf16[2048,768]{1,0:T(8,128)(2,1)S(1)} %get-tuple-element.202.d_ref, bf16[4,256,1024]{2,1,0:T(8,128)(2,1)S(1)} %copy-done.7), custom_call_target="tpu_custom_call" | custom-call | flops 1000 | bytes 1000 | tf_op jit(solution)/shard_map/first_grad/pallas_call | solution.py:795
  196.7 1.4 collective-permute-start.27
  201.6 3.8 %collective-permute-start.30 = (bf16[128,1024]{1,0:T(8,128)(2,1)S(1)}, bf16[128,1024]{1,0:T(8,128)(2,1)S(1)}, u32[]{:S(2)}, u32[]{:S(2)}) collective-permute-start(bf16[128,1024]{1,0:T(8,128)(2,1)S(1)} %get-tuple-element.229), channel_id=1, source_target_pairs={{0,24},{4,28},{8,16},{12,20},{16,8},{20,12},{24,0},{28,4},{1,25},{... | collective-permute-start | bytes 786440 | tf_op jit(solution)/shard_map/ppermute | solution.py:53
  205.4 23.4 %feed_forward.1 = (bf16[2048,512]{1,0:T(8,128)(2,1)}, bf16[2048,256]{1,0:T(8,128)(2,1)S(1)}, bf16[2048,256]{1,0:T(8,128)(2,1)S(1)}, f32[2048,256]{1,0:T(8,128)}) custom-call(bf16[2048,256]{1,0:T(8,128)(2,1)S(1)} %copy-done.10, bf16[2048,256]{1,0:T(8,128)(2,1)} %copy-done.23, bf16[2048,256]{1,0:T(8,128)(2,1)} %copy-done.21, bf16[2048,256]{1,0:T(8,128)(2,1)} %copy-done.24, ...), custom_call_target="tpu_custom_call" | custom-call | flops 1000 | bytes 1000 | tf_op jit(solution)/shard_map/feed_forward/pallas_call | solution.py:404
  228.9 3.3 %collective-permute-done.27.refs_0_ = bf16[4,144,1024]{2,1,0:T(8,128)(2,1)S(1)} collective-permute-done((bf16[4,144,1024]{2,1,0:T(8,128)(2,1)S(1)}, bf16[4,144,1024]{2,1,0:T(8,128)(2,1)S(1)}, u32[]{:S(2)}, u32[]{:S(2)}) %collective-permute-start.27) | collective-permute-done | bytes 1179680 | tf_op jit(solution)/shard_map/ppermute | solution.py:53
  232.2 1.3 add_attention.1
  233.6 3.0 %collective-permute-done.32 = bf16[2048,512]{1,0:T(8,128)(2,1)S(1)} collective-permute-done((bf16[2048,512]{1,0:T(8,128)(2,1)}, bf16[2048,512]{1,0:T(8,128)(2,1)S(1)}, u32[]{:S(2)}, u32[]{:S(2)}) %collective-permute-start.32) | collective-permute-done | bytes 2097184 | tf_op jit(solution)/shard_map/ppermute | solution.py:53
  236.6 1.3 add_convert_fusion.1
  239.3 2.4 adam_down.1
  241.7 4.3 %collective-permute-start.35 = (bf16[144,1024]{1,0:T(8,128)(2,1)}, bf16[144,1024]{1,0:T(8,128)(2,1)}, u32[]{:S(2)}, u32[]{:S(2)}) collective-permute-start(bf16[144,1024]{1,0:T(8,128)(2,1)} %get-tuple-element.247), channel_id=1, source_target_pairs={{0,24},{4,28},{8,16},{12,20},{16,8},{20,12},{24,0},{28,4},{1,25},{... | collective-permute-start | bytes 884744 | tf_op jit(solution)/shard_map/ppermute | solution.py:53
  246.0 5.1 %reduce-scatter.2.cloned.1.call-done = bf16[1,128,2048]{2,1,0:T(8,128)(2,1)} async-done(((bf16[8,128,2048]{2,1,0:T(8,128)(2,1)}), bf16[1,128,2048]{2,1,0:T(8,128)(2,1)}) %reduce-scatter.2.cloned.1.call-update) | async-done | bytes 524304 | tf_op jit(solution)/shard_map/reduce_scatter | solution.py:1071
  251.1 5.6 %adam_gate_up.1 = (f32[2,128,1024]{2,1,0:T(8,128)}, f32[2,128,1024]{2,1,0:T(8,128)}, f32[2,128,1024]{2,1,0:T(8,128)}, f32[2,128,1024]{2,1,0:T(8,128)}, f32[2,128...) custom-call(bf16[128,2048]{1,0:T(8,128)(2,1)} %bitcast.32, f32[2,128,1024]{2,1,0:T(8,128)} %refs_1_.1, ...), custom_call_target="tpu_custom_call" | custom-call | tf_op jit(solution)/shard_map/adam_gate_up/pallas_call | solution.py:893
  260.4 4.3 %input_grad.1 = bf16[2048,256]{1,0:T(8,128)(2,1)} custom-call(bf16[2048,256]{1,0:T(8,128)(2,1)S(1)} %copy-done.10, f32[2048,1]{1,0:T(8,128)S(1)} %copy-done.44, f32[1,2048]{1,0:T(1,128)S(1)} %add.101.dot_ref, bf16[2048,256]{1,0:T(8,128)(2,1)S(1)} %copy-done.46, bf16[2048,256]{1,0:T(8,128)(2,1)S(1)} %slice.128.near_ref, bf16[2048,256]{1,0:T(8,128)(2,1)S(1)} %copy-done.48, ...), custom_call_target="tpu_custom_call" | custom-call | flops 1000 | bytes 1000 | tf_op jit(solution)/shard_map/input_grad/pallas_call | solution.py:833
  264.8 2.8 add_convert_fusion
  267.7 3.5 %adam_qkv.1 = (f32[3,128,256]{2,1,0:T(8,128)}, f32[3,128,256]{2,1,0:T(8,128)}, f32[3,128,256]{2,1,0:T(8,128)}, f32[3,128,256]{2,1,0:T(8,128)}, f32[3,128,256]{2,...) custom-call(f32[144,1024]{1,0:T(8,128)S(1)} %get-tuple-element.269.refs_0_, ...), custom_call_target="tpu_custom_call" | custom-call | tf_op jit(solution)/shard_map/adam_qkv/pallas_call | solution.py:893
  272.5 4.5 %collective-permute-start.38 = (f32[1,128]{1,0:T(1,128)S(1)}, f32[1,128]{1,0:T(1,128)S(1)}, u32[]{:S(2)}, u32[]{:S(2)}) collective-permute-start(f32[1,128]{1,0:T(1,128)S(1)} %bitcast_add_fusion), channel_id=1, source_target_pairs={{0,2},{1,3},{2,0},{3,1},{4,6},{5,7},{6,4},{7,5},{8,10},{9,11},{10,... | collective-permute-start | bytes 1544 | tf_op jit(solution)/shard_map/ppermute | solution.py:53
  277.7 1.9 adam_proj.1
  (293 shorter events, 42.3 us)
Async XLA Ops:
  7.2 121.8 %all-gather.3.cloned.1.call-start = ((), (), s32[]{:S(2)}) async-start(), calls=%async_computation.2 | async-start | bytes 7077888 | tf_op jit(solution)/shard_map/all_gather | solution.py:1010
  10.9 240.3 %reduce-scatter.2.cloned.1.call-start = ((), (), s32[]{:S(2)}) async-start(), calls=%async_computation.1 | async-start | bytes 4718592 | tf_op jit(solution)/shard_map/reduce_scatter | solution.py:1071
  10.9 39.3 %collective-permute-start.1 = (bf16[2048,256]{1,0:T(8,128)(2,1)S(1)}, bf16[2048,256]{1,0:T(8,128)(2,1)S(1)}, u32[]{:S(2)}, u32[]{:S(2)}) collective-permute-start(bf16[2048,256]{1,0:T(8,128)(2,1)S(1)} %copy-done.8), channel_id=1, source_target_pairs={{0,2},{1,3},{2,0},{3,1},{4,6},{5,7},{6,4},{7,5},{8,10},{9,11},{10,... | collective-permute-start | bytes 3145736 | tf_op jit(solution)/shard_map/ppermute | solution.py:53
  14.2 35.9 %collective-permute-start.9 = (bf16[528,256]{1,0:T(8,128)(2,1)S(1)}, bf16[528,256]{1,0:T(8,128)(2,1)S(1)}, u32[]{:S(2)}, u32[]{:S(2)}) collective-permute-start(bf16[528,256]{1,0:T(8,128)(2,1)S(1)} %constant_dynamic-update-slice_fusion.refs_7_), channel_id=1, source_target_pairs={{0,4},{4,0},{8,12},{12,8},{16,20},{20,16},{24,28},{28,24},{1,5},{5... | collective-permute-start | bytes 811016 | tf_op jit(solution)/shard_map/ppermute | solution.py:53
  15.8 18.0 %collective-permute-start.7 = (bf16[528,256]{1,0:T(8,128)(2,1)S(1)}, bf16[528,256]{1,0:T(8,128)(2,1)S(1)}, u32[]{:S(2)}, u32[]{:S(2)}) collective-permute-start(bf16[528,256]{1,0:T(8,128)(2,1)S(1)} %constant_dynamic-update-slice_fusion.refs_7_), channel_id=1, source_target_pairs={{0,8},{4,12},{8,0},{12,4},{16,24},{20,28},{24,16},{28,20},{1,9},{5... | collective-permute-start | bytes 811016 | tf_op jit(solution)/shard_map/ppermute | solution.py:53
  17.3 28.9 %collective-permute-start.5 = (bf16[528,256]{1,0:T(8,128)(2,1)S(1)}, bf16[528,256]{1,0:T(8,128)(2,1)S(1)}, u32[]{:S(2)}, u32[]{:S(2)}) collective-permute-start(bf16[528,256]{1,0:T(8,128)(2,1)S(1)} %constant_dynamic-update-slice_fusion.refs_7_), channel_id=1, source_target_pairs={{0,16},{4,20},{8,24},{12,28},{16,0},{20,4},{24,8},{28,12},{1,17},{... | collective-permute-start | bytes 811016 | tf_op jit(solution)/shard_map/ppermute | solution.py:53
  19.9 29.0 %collective-permute-start.3 = (bf16[528,256]{1,0:T(8,128)(2,1)S(1)}, bf16[528,256]{1,0:T(8,128)(2,1)}, u32[]{:S(2)}, u32[]{:S(2)}) collective-permute-start(bf16[528,256]{1,0:T(8,128)(2,1)S(1)} %constant_dynamic-update-slice_fusion.refs_7_), channel_id=1, source_target_pairs={{0,24},{4,28},{8,16},{12,20},{16,8},{20,12},{24,0},{28,4},{1,25},{... | collective-permute-start | bytes 811016 | tf_op jit(solution)/shard_map/ppermute | solution.py:53
  20.2 28.8 %copy-start.87 = (s32[8]{0:T(128)S(1)}, s32[8]{0:T(128)}, u32[]{:S(2)}) copy-start(s32[8]{0:T(128)} %param.31) | copy-start | bytes 100
  33.8 16.9 %collective-permute-start.8 = (bf16[528,256]{1,0:T(8,128)(2,1)S(1)}, bf16[528,256]{1,0:T(8,128)(2,1)}, u32[]{:S(2)}, u32[]{:S(2)}) collective-permute-start(bf16[528,256]{1,0:T(8,128)(2,1)S(1)} %collective-permute-done.7.refs_5_), channel_id=1, source_target_pairs={{0,4},{4,0},{8,12},{12,8},{16,20},{20,16},{24,28},{28,24},{1,5},{5... | collective-permute-start | bytes 811016 | tf_op jit(solution)/shard_map/ppermute | solution.py:53
  46.2 6.6 %collective-permute-start.6 = (bf16[528,256]{1,0:T(8,128)(2,1)S(1)}, bf16[528,256]{1,0:T(8,128)(2,1)}, u32[]{:S(2)}, u32[]{:S(2)}) collective-permute-start(bf16[528,256]{1,0:T(8,128)(2,1)S(1)} %collective-permute-done.5.refs_3_), channel_id=1, source_target_pairs={{0,4},{4,0},{8,12},{12,8},{16,20},{20,16},{24,28},{28,24},{1,5},{5... | collective-permute-start | bytes 811016 | tf_op jit(solution)/shard_map/ppermute | solution.py:53
  48.9 6.8 %collective-permute-start.4 = (bf16[528,256]{1,0:T(8,128)(2,1)}, bf16[528,256]{1,0:T(8,128)(2,1)}, u32[]{:S(2)}, u32[]{:S(2)}) collective-permute-start(bf16[528,256]{1,0:T(8,128)(2,1)} %collective-permute-done.3.refs_1_), channel_id=1, source_target_pairs={{0,4},{4,0},{8,12},{12,8},{16,20},{20,16},{24,28},{28,24},{1,5},{5... | collective-permute-start | bytes 811016 | tf_op jit(solution)/shard_map/ppermute | solution.py:53
  50.1 37.3 %copy-start.74 = (bf16[2,160,256]{2,1,0:T(8,128)(2,1)}, bf16[2,160,256]{2,1,0:T(8,128)(2,1)S(1)}, u32[]{:S(2)}) copy-start(bf16[2,160,256]{2,1,0:T(8,128)(2,1)S(1)} %pad.15) | copy-start | bytes 491524
  50.1 10.2 %collective-permute-start = (bf16[2048,256]{1,0:T(8,128)(2,1)S(1)}, bf16[2048,256]{1,0:T(8,128)(2,1)S(1)}, u32[]{:S(2)}, u32[]{:S(2)}) collective-permute-start(bf16[2048,256]{1,0:T(8,128)(2,1)S(1)} %copy-done.8), channel_id=1, source_target_pairs={{0,1},{1,0},{2,3},{3,2},{4,5},{5,4},{6,7},{7,6},{8,9},{9,8},{10,11... | collective-permute-start | bytes 3145736 | tf_op jit(solution)/shard_map/ppermute | solution.py:53
  50.2 10.2 %collective-permute-start.2 = (bf16[2048,256]{1,0:T(8,128)(2,1)S(1)}, bf16[2048,256]{1,0:T(8,128)(2,1)S(1)}, u32[]{:S(2)}, u32[]{:S(2)}) collective-permute-start(bf16[2048,256]{1,0:T(8,128)(2,1)S(1)} %collective-permute-done.1.x2), channel_id=1, source_target_pairs={{0,1},{1,0},{2,3},{3,2},{4,5},{5,4},{6,7},{7,6},{8,9},{9,8},{10,11... | collective-permute-start | bytes 3145736 | tf_op jit(solution)/shard_map/ppermute | solution.py:53
  59.9 11.2 %collective-permute-start.10 = (bf16[256,1024]{1,0:T(8,128)(2,1)S(1)}, bf16[256,1024]{1,0:T(8,128)(2,1)S(1)}, u32[]{:S(2)}, u32[]{:S(2)}) collective-permute-start(bf16[256,1024]{1,0:T(8,128)(2,1)S(1)} %slice_bitcast_fusion.o0), channel_id=1, source_target_pairs={{0,2},{1,3},{2,0},{3,1},{4,6},{5,7},{6,4},{7,5},{8,10},{9,11},{10,... | collective-permute-start | bytes 1572872 | tf_op jit(solution)/shard_map/ppermute | solution.py:53
  71.1 18.7 %copy-start.85 = (s32[16]{0:T(128)S(1)}, s32[16]{0:T(128)}, u32[]{:S(2)}) copy-start(s32[16]{0:T(128)} %param.30) | copy-start | bytes 196
  71.1 19.3 %copy-start.86 = (s32[2]{0:T(128)S(1)}, s32[2]{0:T(128)}, u32[]{:S(2)}) copy-start(s32[2]{0:T(128)} %param.29) | copy-start | bytes 28
  88.2 7.2 %collective-permute-start.12 = (bf16[640,256]{1,0:T(8,128)(2,1)S(1)}, bf16[640,256]{1,0:T(8,128)(2,1)}, u32[]{:S(2)}, u32[]{:S(2)}) collective-permute-start(bf16[640,256]{1,0:T(8,128)(2,1)S(1)} %pad_maximum_fusion.3), channel_id=1, source_target_pairs={{0,2},{1,3},{2,0},{3,1},{4,6},{5,7},{6,4},{7,5},{8,10},{9,11},{10,... | collective-permute-start | bytes 983048 | tf_op jit(solution)/shard_map/ppermute | solution.py:53
  95.4 2.0 collective-permute-start.13
  96.4 4.2 %collective-permute-start.11 = (bf16[640,256]{1,0:T(8,128)(2,1)}, bf16[640,256]{1,0:T(8,128)(2,1)S(1)}, u32[]{:S(2)}, u32[]{:S(2)}) collective-permute-start(bf16[640,256]{1,0:T(8,128)(2,1)} %copy-done.78), channel_id=1, source_target_pairs={{0,1},{1,0},{2,3},{3,2},{4,5},{5,4},{6,7},{7,6},{8,9},{9,8},{10,11... | collective-permute-start | bytes 983048 | tf_op jit(solution)/shard_map/ppermute | solution.py:53
  97.4 47.8 %collective-permute-start.18 = (bf16[2048,256]{1,0:T(8,128)(2,1)}, bf16[2048,256]{1,0:T(8,128)(2,1)}, u32[]{:S(2)}, u32[]{:S(2)}) collective-permute-start(bf16[2048,256]{1,0:T(8,128)(2,1)} %get-tuple-element.217.c0), channel_id=1, source_target_pairs={{0,2},{1,3},{2,0},{3,1},{4,6},{5,7},{6,4},{7,5},{8,10},{9,11},{10,... | collective-permute-start | bytes 3145736 | tf_op jit(solution)/shard_map/ppermute | solution.py:53
  99.1 2.7 collective-permute-start.14
  99.1 2.9 collective-permute-start.15
  145.2 20.7 %collective-permute-start.19 = (bf16[2048,256]{1,0:T(8,128)(2,1)}, bf16[2048,256]{1,0:T(8,128)(2,1)}, u32[]{:S(2)}, u32[]{:S(2)}) collective-permute-start(bf16[2048,256]{1,0:T(8,128)(2,1)} %get-tuple-element.217.c0), channel_id=1, source_target_pairs={{0,1},{1,0},{2,3},{3,2},{4,5},{5,4},{6,7},{7,6},{8,9},{9,8},{10,11... | collective-permute-start | bytes 3145736 | tf_op jit(solution)/shard_map/ppermute | solution.py:53
  145.2 20.7 %collective-permute-start.20 = (bf16[2048,256]{1,0:T(8,128)(2,1)}, bf16[2048,256]{1,0:T(8,128)(2,1)}, u32[]{:S(2)}, u32[]{:S(2)}) collective-permute-start(bf16[2048,256]{1,0:T(8,128)(2,1)} %collective-permute-done.18.c2), channel_id=1, source_target_pairs={{0,1},{1,0},{2,3},{3,2},{4,5},{5,4},{6,7},{7,6},{8,9},{9,8},{10,11... | collective-permute-start | bytes 3145736 | tf_op jit(solution)/shard_map/ppermute | solution.py:53
  145.7 3.1 %collective-permute-start.16 = (bf16[320,512]{1,0:T(8,128)(2,1)S(1)}, bf16[320,512]{1,0:T(8,128)(2,1)S(1)}, u32[]{:S(2)}, u32[]{:S(2)}) collective-permute-start(bf16[320,512]{1,0:T(8,128)(2,1)S(1)} %get-tuple-element.178), channel_id=1, source_target_pairs={{0,1},{1,0},{2,3},{3,2},{4,5},{5,4},{6,7},{7,6},{8,9},{9,8},{10,11... | collective-permute-start | bytes 983048 | tf_op jit(solution)/shard_map/ppermute | solution.py:53
  147.3 17.8 %collective-permute-start.22 = (bf16[2,128,1024]{2,1,0:T(8,128)(2,1)}, bf16[2,128,1024]{2,1,0:T(8,128)(2,1)}, u32[]{:S(2)}, u32[]{:S(2)}) collective-permute-start(bf16[2,128,1024]{2,1,0:T(8,128)(2,1)} %get-tuple-element.302), channel_id=1, source_target_pairs={{0,4},{4,0},{8,12},{12,8},{16,20},{20,16},{24,28},{28,24},{1,5},{5... | collective-permute-start | bytes 1572872 | tf_op jit(solution)/shard_map/ppermute | solution.py:53
  150.4 15.5 %collective-permute-start.17 = (bf16[320,512]{1,0:T(8,128)(2,1)}, bf16[320,512]{1,0:T(8,128)(2,1)}, u32[]{:S(2)}, u32[]{:S(2)}) collective-permute-start(bf16[320,512]{1,0:T(8,128)(2,1)} %pad_maximum_fusion.4), channel_id=1, source_target_pairs={{0,2},{1,3},{2,0},{3,1},{4,6},{5,7},{6,4},{7,5},{8,10},{9,11},{10,... | collective-permute-start | bytes 983048 | tf_op jit(solution)/shard_map/ppermute | solution.py:53
  152.0 17.8 %copy-start.1 = (bf16[4,1024,256]{2,1,0:T(8,128)(2,1)S(1)}, bf16[4,1024,256]{2,1,0:T(8,128)(2,1)}, u32[]{:S(2)}) copy-start(bf16[4,1024,256]{2,1,0:T(8,128)(2,1)} %copy-done) | copy-start | bytes 6291460
  152.0 17.8 %copy-start.13 = (f32[320,1024]{1,0:T(8,128)S(1)}, f32[320,1024]{1,0:T(8,128)}, u32[]{:S(2)}) copy-start(f32[320,1024]{1,0:T(8,128)} %get-tuple-element.303.seed_ref) | copy-start | bytes 3932164
  152.0 17.8 %copy-start.65 = (f32[320,128]{1,0:T(8,128)S(1)}, f32[320,128]{1,0:T(8,128)}, u32[]{:S(2)}) copy-start(f32[320,128]{1,0:T(8,128)} %copy-done.64) | copy-start | bytes 491524
  165.1 24.2 %collective-permute-start.23 = (bf16[2,128,1024]{2,1,0:T(8,128)(2,1)}, bf16[2,128,1024]{2,1,0:T(8,128)(2,1)S(1)}, u32[]{:S(2)}, u32[]{:S(2)}) collective-permute-start(bf16[2,128,1024]{2,1,0:T(8,128)(2,1)} %get-tuple-element.194), channel_id=1, source_target_pairs={{0,4},{4,0},{8,12},{12,8},{16,20},{20,16},{24,28},{28,24},{1,5},{5... | collective-permute-start | bytes 1572872 | tf_op jit(solution)/shard_map/ppermute | solution.py:53
  168.1 1.7 collective-permute-start.21
  190.8 4.3 %collective-permute-start.24 = (f32[1,2048]{1,0:T(1,128)S(1)}, f32[1,2048]{1,0:T(1,128)S(1)}, u32[]{:S(2)}, u32[]{:S(2)}) collective-permute-start(f32[1,2048]{1,0:T(1,128)S(1)} %get-tuple-element.205), channel_id=1, source_target_pairs={{0,1},{1,0},{2,3},{3,2},{4,5},{5,4},{6,7},{7,6},{8,9},{9,8},{10,11... | collective-permute-start | bytes 24584 | tf_op jit(solution)/shard_map/ppermute | solution.py:53
  195.1 4.2 %collective-permute-start.25 = (bf16[2048,512]{1,0:T(8,128)(2,1)S(1)}, bf16[2048,512]{1,0:T(8,128)(2,1)S(1)}, u32[]{:S(2)}, u32[]{:S(2)}) collective-permute-start(bf16[2048,512]{1,0:T(8,128)(2,1)S(1)} %get-tuple-element.206), channel_id=1, source_target_pairs={{0,1},{1,0},{2,3},{3,2},{4,5},{5,4},{6,7},{7,6},{8,9},{9,8},{10,11... | collective-permute-start | bytes 6291464 | tf_op jit(solution)/shard_map/ppermute | solution.py:53
  195.5 3.7 %collective-permute-start.26 = (f32[1,2048]{1,0:T(1,128)S(1)}, f32[1,2048]{1,0:T(1,128)S(1)}, u32[]{:S(2)}, u32[]{:S(2)}) collective-permute-start(f32[1,2048]{1,0:T(1,128)S(1)} %add.96), channel_id=1, source_target_pairs={{0,2},{1,3},{2,0},{3,1},{4,6},{5,7},{6,4},{7,5},{8,10},{9,11},{10,... | collective-permute-start | bytes 24584 | tf_op jit(solution)/shard_map/ppermute | solution.py:53
  196.7 35.4 %collective-permute-start.27 = (bf16[4,144,1024]{2,1,0:T(8,128)(2,1)S(1)}, bf16[4,144,1024]{2,1,0:T(8,128)(2,1)S(1)}, u32[]{:S(2)}, u32[]{:S(2)}) collective-permute-start(bf16[4,144,1024]{2,1,0:T(8,128)(2,1)S(1)} %get-tuple-element.225), channel_id=1, source_target_pairs={{0,4},{4,0},{8,12},{12,8},{16,20},{20,16},{24,28},{28,24},{1,5},{5... | collective-permute-start | bytes 3538952 | tf_op jit(solution)/shard_map/ppermute | solution.py:53
  199.7 32.5 %collective-permute-start.31 = (bf16[2048,256]{1,0:T(8,128)(2,1)S(1)}, bf16[2048,256]{1,0:T(8,128)(2,1)S(1)}, u32[]{:S(2)}, u32[]{:S(2)}) collective-permute-start(bf16[2048,256]{1,0:T(8,128)(2,1)S(1)} %add_convert_fusion.2), channel_id=1, source_target_pairs={{0,2},{1,3},{2,0},{3,1},{4,6},{5,7},{6,4},{7,5},{8,10},{9,11},{10,... | collective-permute-start | bytes 3145736 | tf_op jit(solution)/shard_map/ppermute | solution.py:53
  201.0 31.1 %collective-permute-start.28 = (bf16[128,1024]{1,0:T(8,128)(2,1)S(1)}, bf16[128,1024]{1,0:T(8,128)(2,1)S(1)}, u32[]{:S(2)}, u32[]{:S(2)}) collective-permute-start(bf16[128,1024]{1,0:T(8,128)(2,1)S(1)} %get-tuple-element.227), channel_id=1, source_target_pairs={{0,8},{4,12},{8,0},{12,4},{16,24},{20,28},{24,16},{28,20},{1,9},{5... | collective-permute-start | bytes 786440 | tf_op jit(solution)/shard_map/ppermute | solution.py:53
  201.0 31.1 %collective-permute-start.29 = (bf16[128,1024]{1,0:T(8,128)(2,1)S(1)}, bf16[128,1024]{1,0:T(8,128)(2,1)S(1)}, u32[]{:S(2)}, u32[]{:S(2)}) collective-permute-start(bf16[128,1024]{1,0:T(8,128)(2,1)S(1)} %get-tuple-element.228), channel_id=1, source_target_pairs={{0,16},{4,20},{8,24},{12,28},{16,0},{20,4},{24,8},{28,12},{1,17},{... | collective-permute-start | bytes 786440 | tf_op jit(solution)/shard_map/ppermute | solution.py:53
  201.6 30.6 %collective-permute-start.30 = (bf16[128,1024]{1,0:T(8,128)(2,1)S(1)}, bf16[128,1024]{1,0:T(8,128)(2,1)S(1)}, u32[]{:S(2)}, u32[]{:S(2)}) collective-permute-start(bf16[128,1024]{1,0:T(8,128)(2,1)S(1)} %get-tuple-element.229), channel_id=1, source_target_pairs={{0,24},{4,28},{8,16},{12,20},{16,8},{20,12},{24,0},{28,4},{1,25},{... | collective-permute-start | bytes 786440 | tf_op jit(solution)/shard_map/ppermute | solution.py:53
  232.1 4.4 %collective-permute-start.32 = (bf16[2048,512]{1,0:T(8,128)(2,1)}, bf16[2048,512]{1,0:T(8,128)(2,1)S(1)}, u32[]{:S(2)}, u32[]{:S(2)}) collective-permute-start(bf16[2048,512]{1,0:T(8,128)(2,1)} %get-tuple-element.232), channel_id=1, source_target_pairs={{0,1},{1,0},{2,3},{3,2},{4,5},{5,4},{6,7},{7,6},{8,9},{9,8},{10,11... | collective-permute-start | bytes 6291464 | tf_op jit(solution)/shard_map/ppermute | solution.py:53
  237.9 26.8 %collective-permute-start.36 = (bf16[2048,256]{1,0:T(8,128)(2,1)}, bf16[2048,256]{1,0:T(8,128)(2,1)}, u32[]{:S(2)}, u32[]{:S(2)}) collective-permute-start(bf16[2048,256]{1,0:T(8,128)(2,1)} %add_convert_fusion.1), channel_id=1, source_target_pairs={{0,2},{1,3},{2,0},{3,1},{4,6},{5,7},{6,4},{7,5},{8,10},{9,11},{10,... | collective-permute-start | bytes 3145736 | tf_op jit(solution)/shard_map/ppermute | solution.py:53
  241.6 26.0 %collective-permute-start.33 = (bf16[144,1024]{1,0:T(8,128)(2,1)}, bf16[144,1024]{1,0:T(8,128)(2,1)}, u32[]{:S(2)}, u32[]{:S(2)}) collective-permute-start(bf16[144,1024]{1,0:T(8,128)(2,1)} %get-tuple-element.245), channel_id=1, source_target_pairs={{0,8},{4,12},{8,0},{12,4},{16,24},{20,28},{24,16},{28,20},{1,9},{5... | collective-permute-start | bytes 884744 | tf_op jit(solution)/shard_map/ppermute | solution.py:53
  241.6 26.0 %collective-permute-start.34 = (bf16[144,1024]{1,0:T(8,128)(2,1)}, bf16[144,1024]{1,0:T(8,128)(2,1)}, u32[]{:S(2)}, u32[]{:S(2)}) collective-permute-start(bf16[144,1024]{1,0:T(8,128)(2,1)} %get-tuple-element.246), channel_id=1, source_target_pairs={{0,16},{4,20},{8,24},{12,28},{16,0},{20,4},{24,8},{28,12},{1,17},{... | collective-permute-start | bytes 884744 | tf_op jit(solution)/shard_map/ppermute | solution.py:53
  241.7 25.9 %collective-permute-start.35 = (bf16[144,1024]{1,0:T(8,128)(2,1)}, bf16[144,1024]{1,0:T(8,128)(2,1)}, u32[]{:S(2)}, u32[]{:S(2)}) collective-permute-start(bf16[144,1024]{1,0:T(8,128)(2,1)} %get-tuple-element.247), channel_id=1, source_target_pairs={{0,24},{4,28},{8,16},{12,20},{16,8},{20,12},{24,0},{28,4},{1,25},{... | collective-permute-start | bytes 884744 | tf_op jit(solution)/shard_map/ppermute | solution.py:53
  271.3 1.2 collective-permute-start.37
  272.5 7.1 %collective-permute-start.38 = (f32[1,128]{1,0:T(1,128)S(1)}, f32[1,128]{1,0:T(1,128)S(1)}, u32[]{:S(2)}, u32[]{:S(2)}) collective-permute-start(f32[1,128]{1,0:T(1,128)S(1)} %bitcast_add_fusion), channel_id=1, source_target_pairs={{0,2},{1,3},{2,0},{3,1},{4,6},{5,7},{6,4},{7,5},{8,10},{9,11},{10,... | collective-permute-start | bytes 1544 | tf_op jit(solution)/shard_map/ppermute | solution.py:53
  (81 other events, 460.1 us)
Sparse Core Ops, SparseCore 0:
  11.0 117.9 all-gather.2
  152.0 99.0 reduce-scatter.1
